TPU v7x, 32 devices: a whole 2x2x4 slice. The times are simulated.
32 devices in a mesh: items: 8 (over y, x, core), frames: 4 (over z).
Axes of the slice: x: 2, y: 2, z: 4, core: 2. Of those that a mesh axis runs over, the one named last changes fastest.
Arguments:
- tokens: bfloat16 [8, 16, 196, 768], P('items', 'frames'), may hold values from -6 to 6
- cotangent: bfloat16 [8, 16, 196, 768], P('items', 'frames'), may hold values from -6 to 6
- date_year: int32 [8, 16], P('items', 'frames'), may hold values from 2015 to 2024
- date_day: int32 [8, 16], P('items', 'frames'), may hold values from 1 to 366
- item_dates: int32 [8, 3], P('items'), may hold values from 1 to 6, 16 in all within a row
- slot_frame: int32 [8, 16], P('items'), may hold values from 0 to 15, as said below
- frame_mask: int32 [8, 16], P('items'), may hold values 0 or 1
- qkv_weight: float32 [768, 2304], P('frames'), may hold values from -0.21875 to 0.21875
- qkv_first: float32 [768, 2304], P('frames'), may hold values from -112 to 112
- qkv_second: float32 [768, 2304], P('frames'), may hold values from 25.088 to 100.352
- out_weight: float32 [768, 768], P('frames'), may hold values from -2.5 to 2.5
- out_first: float32 [768, 768], P('frames'), may hold values from -6 to 6
- out_second: float32 [768, 768], P('frames'), may hold values from 0.25088 to 1.00352
- up_weight: float32 [768, 3072], P('frames'), may hold values from -0.21875 to 0.21875
- up_first: float32 [768, 3072], P('frames'), may hold values from -32 to 32
- up_second: float32 [768, 3072], P('frames'), may hold values from 2.25792 to 9.03168
- down_weight: float32 [3072, 768], P('frames'), may hold values from -0.109375 to 0.109375
- down_first: float32 [3072, 768], P('frames'), may hold values from -64 to 64
- down_second: float32 [3072, 768], P('frames'), may hold values from 9.03168 to 36.12672
- vectors: float32 [9216], P('frames')
- vector_first: float32 [9216], P('frames'), may hold values from -160 to 160
- vector_second: float32 [9216], P('frames'), may hold values from 56.448 to 225.792
Outputs:
- block_out: bfloat16 [8, 16, 196, 768], P('items', 'frames')
- token_grad: float32 [8, 16, 196, 768], P('items', 'frames')
- qkv_moment: float32 [768, 2304], P('frames')
- qkv_square: float32 [768, 2304], P('frames')
- qkv_master: float32 [768, 2304], P('frames')
- out_moment: float32 [768, 768], P('frames')
- out_square: float32 [768, 768], P('frames')
- out_master: float32 [768, 768], P('frames')
- up_moment: float32 [768, 3072], P('frames')
- up_square: float32 [768, 3072], P('frames')
- up_master: float32 [768, 3072], P('frames')
- down_moment: float32 [3072, 768], P('frames')
- down_square: float32 [3072, 768], P('frames')
- down_master: float32 [3072, 768], P('frames')
- vector_moment: float32 [9216], P('frames')
- vector_square: float32 [9216], P('frames')
- vector_master: float32 [9216], P('frames')
Inputs may be any that keep to these rules, and one draw needn't show every extreme that they name: `item_dates`: in each group the 3 items' dates add up to 16; the longest item has exactly 6. `slot_frame`: in each group a permutation of the frame numbers 0 to 15; frame numbers that follow each other stand on devices of frames that follow each other, cyclically.
All inputs are finite; a program needn't handle non-finite values. No bound on the sum of `frame_mask` on one device may be relied on, other than what follows from the above.
Results may differ from a plain program's by a relative error of at most 0.012.
Values may be sent and summed in bfloat16 or wider, within the bound.
A program may use at most 576 MiB of HBM per device.

v0:
```python
import jax
import jax.numpy as jnp
from jax import lax
from jax.sharding import PartitionSpec as P

D = 768
HEADS = 12
HEAD = 64
GRID = 14
STEP = 10
FRAME_TOK = 196


beta_one = 0.9
beta_two = 0.999


def sincos(values, length_out):
    half_width = length_out // 2
    frequency = 1.0 / 10000.0 ** (jnp.arange(half_width, dtype=jnp.float32) / half_width)
    angles = values[..., None] * frequency
    return jnp.concatenate([jnp.sin(angles), jnp.cos(angles)], axis=-1)


def positions(year_values, day_values):
    cell_index = jnp.arange(FRAME_TOK, dtype=jnp.int32)
    spatial = jnp.concatenate(
        [
            sincos((cell_index // GRID).astype(jnp.float32), 3 * D // 8),
            sincos((cell_index % GRID).astype(jnp.float32), 3 * D // 8),
        ],
        axis=-1,
    )
    temporal = jnp.concatenate(
        [
            sincos((year_values - 2000).astype(jnp.float32), D // 8),
            sincos(day_values.astype(jnp.float32), D // 8),
        ],
        axis=-1,
    )
    slot_count = year_values.shape[0]
    return jnp.concatenate(
        [
            jnp.broadcast_to(spatial[None], (slot_count, FRAME_TOK, 3 * D // 4)),
            jnp.broadcast_to(temporal[:, None], (slot_count, FRAME_TOK, D // 4)),
        ],
        axis=-1,
    )


def slot_items(dates_group, frames_group, mask_group):
    item_ends = jnp.cumsum(dates_group)
    starts = item_ends - dates_group
    item_index = jnp.sum((frames_group[:, None] >= item_ends[None, :]).astype(jnp.int32), axis=1)
    is_first = jnp.any(frames_group[:, None] == starts[None, :], axis=1)
    is_valid = jnp.logical_or(mask_group > 0, is_first)
    return (item_index, is_valid)


def layer_norm(values, gain_vec, shift_vec):
    average = jnp.mean(values, axis=-1, keepdims=True)
    centred = values - average
    spread = jnp.mean(centred * centred, axis=-1, keepdims=True)
    return centred * lax.rsqrt(spread + 1e-06) * gain_vec + shift_vec


def unpack(vector_all):
    pieces = [vector_all[index * D : (index + 1) * D] for index in range(8)]
    return tuple(pieces) + (vector_all[8 * D :],)


def exact_gelu(values):
    return jax.nn.gelu(values, approximate=False)


def attention_scores(query_part, key_part, allowed):
    scores = (
        jnp.einsum("qhe,khe->hqk", query_part, key_part, preferred_element_type=jnp.float32) * 0.125
    )
    return jnp.where(allowed[None], scores, -1000000000.0)


def adamw(weight, first_moment, second, gradient, step_rate, decay):
    first_new = beta_one * first_moment + (1.0 - beta_one) * gradient
    second_new = beta_two * second + (1.0 - beta_two) * gradient * gradient
    first_hat = first_new / (1.0 - beta_one**STEP)
    second_hat = second_new / (1.0 - beta_two**STEP)
    weight_new = weight - step_rate * (first_hat / (jnp.sqrt(second_hat) + 1e-08) + decay * weight)
    return (first_new, second_new, weight_new)


def on_device(
    tokens,
    cotangent,
    date_year,
    date_day,
    item_dates,
    slot_frame,
    frame_mask,
    qkv_weight,
    qkv_first,
    qkv_second,
    out_weight,
    out_first,
    out_second,
    up_weight,
    up_first,
    up_second,
    down_weight,
    down_first,
    down_second,
    vectors,
    vector_first,
    vector_second,
):
    frame_rank = lax.axis_index("frames")
    qkv_full, out_full, up_full, down_full, vector_full = (
        lax.all_gather(qkv_weight.astype(jnp.bfloat16), "frames", axis=0, tiled=True),
        lax.all_gather(out_weight.astype(jnp.bfloat16), "frames", axis=0, tiled=True),
        lax.all_gather(up_weight.astype(jnp.bfloat16), "frames", axis=0, tiled=True),
        lax.all_gather(down_weight.astype(jnp.bfloat16), "frames", axis=0, tiled=True),
        lax.all_gather(vectors.astype(jnp.bfloat16), "frames", axis=0, tiled=True),
    )
    (
        gain_one,
        shift_one,
        bias_query,
        bias_value,
        bias_output,
        gain_two,
        shift_two,
        bias_down,
        bias_up,
    ) = unpack(vector_full.astype(jnp.float32))
    slot_local = tokens.shape[1]
    row_count = slot_local * FRAME_TOK
    key_count = slot_frame.shape[1] * FRAME_TOK
    group_heads = HEADS // 3
    group_cols = group_heads * HEAD
    residual_in = tokens.reshape(row_count, D).astype(jnp.float32) + positions(
        date_year[0], date_day[0]
    ).reshape(row_count, D)
    item_index, is_valid = slot_items(item_dates[0], slot_frame[0], frame_mask[0])
    key_items = jnp.repeat(item_index, FRAME_TOK)
    key_valid = jnp.repeat(is_valid, FRAME_TOK)
    own_items = lax.dynamic_slice_in_dim(key_items, frame_rank * row_count, row_count)
    allowed = (own_items[:, None] == key_items[None, :]) & key_valid[None, :]
    normed, norm_one_back = jax.vjp(layer_norm, residual_in, gain_one, shift_one)
    normed_low = normed.astype(jnp.bfloat16)
    projected = jnp.dot(normed_low, qkv_full, preferred_element_type=jnp.float32)
    query_low = (projected[:, :D] + bias_query).astype(jnp.bfloat16)
    key_low = projected[:, D : 2 * D].astype(jnp.bfloat16)
    value_low = (projected[:, 2 * D :] + bias_value).astype(jnp.bfloat16)
    key_all, value_all = (
        lax.all_gather(key_low, "frames", axis=0, tiled=True),
        lax.all_gather(value_low, "frames", axis=0, tiled=True),
    )

    def head_slice(matrix, group_index, count):
        return matrix[:, group_index * group_cols : (group_index + 1) * group_cols].reshape(
            count, group_heads, HEAD
        )

    outputs = []
    maxima = []
    row_sums = []
    for group_index in range(3):
        query_part = head_slice(query_low, group_index, row_count)
        key_part = head_slice(key_all, group_index, key_count)
        value_part = head_slice(value_all, group_index, key_count)
        scores = attention_scores(query_part, key_part, allowed)
        row_max = jnp.max(scores, axis=-1, keepdims=True)
        weights = jnp.exp(scores - row_max)
        row_total = jnp.sum(weights, axis=-1, keepdims=True)
        probs_low = (weights / row_total).astype(jnp.bfloat16)
        attended_part = jnp.einsum(
            "hqk,khe->qhe", probs_low, value_part, preferred_element_type=jnp.float32
        )
        outputs.append(attended_part.reshape(row_count, group_cols))
        maxima.append(row_max)
        row_sums.append(row_total)
    attended_low = jnp.concatenate(outputs, axis=1).astype(jnp.bfloat16)
    branch = jnp.dot(attended_low, out_full, preferred_element_type=jnp.float32) + bias_output
    hidden = residual_in + branch
    normed_two, norm_two_back = jax.vjp(layer_norm, hidden, gain_two, shift_two)
    normed_two_low = normed_two.astype(jnp.bfloat16)
    inner = jnp.dot(normed_two_low, up_full, preferred_element_type=jnp.float32) + bias_up
    active, gelu_back = jax.vjp(exact_gelu, inner)
    active_low = active.astype(jnp.bfloat16)
    mlp_out = jnp.dot(active_low, down_full, preferred_element_type=jnp.float32) + bias_down
    block_out = (hidden + mlp_out).astype(jnp.bfloat16)
    grad_out_low = cotangent.reshape(row_count, D)
    grad_out = grad_out_low.astype(jnp.float32)
    down_grad = jnp.einsum(
        "tf,td->fd", active_low, grad_out_low, preferred_element_type=jnp.float32
    )
    bias_down_grad = jnp.sum(grad_out, axis=0)
    active_grad = jnp.einsum(
        "td,fd->tf", grad_out_low, down_full, preferred_element_type=jnp.float32
    )
    (inner_grad,) = gelu_back(active_grad)
    inner_grad_low = inner_grad.astype(jnp.bfloat16)
    up_grad = jnp.einsum(
        "td,tf->df", normed_two_low, inner_grad_low, preferred_element_type=jnp.float32
    )
    bias_up_grad = jnp.sum(inner_grad_low.astype(jnp.float32), axis=0)
    normed_two_grad = jnp.einsum(
        "tf,df->td", inner_grad_low, up_full, preferred_element_type=jnp.float32
    )
    hidden_from_norm, gain_two_grad, shift_two_grad = norm_two_back(normed_two_grad)
    hidden_grad = grad_out + hidden_from_norm
    branch_grad_low = hidden_grad.astype(jnp.bfloat16)
    out_grad = jnp.einsum(
        "tc,td->cd", attended_low, branch_grad_low, preferred_element_type=jnp.float32
    )
    bias_output_grad = jnp.sum(branch_grad_low.astype(jnp.float32), axis=0)
    attended_grad_low = jnp.einsum(
        "td,cd->tc", branch_grad_low, out_full, preferred_element_type=jnp.float32
    ).astype(jnp.bfloat16)
    query_grads = []
    key_terms = []
    value_terms = []
    for group_index in range(3):
        query_part = head_slice(query_low, group_index, row_count)
        key_part = head_slice(key_all, group_index, key_count)
        value_part = head_slice(value_all, group_index, key_count)
        upstream = head_slice(attended_grad_low, group_index, row_count)
        scores = attention_scores(query_part, key_part, allowed)
        probs = jnp.exp(scores - maxima[group_index]) / row_sums[group_index]
        probs_low = probs.astype(jnp.bfloat16)
        prob_grad = jnp.einsum(
            "qhe,khe->hqk", upstream, value_part, preferred_element_type=jnp.float32
        )
        centre = jnp.sum(probs * prob_grad, axis=-1, keepdims=True)
        score_grad_low = (probs * (prob_grad - centre)).astype(jnp.bfloat16)
        query_term = (
            jnp.einsum("hqk,khe->qhe", score_grad_low, key_part, preferred_element_type=jnp.float32)
            * 0.125
        )
        key_term = (
            jnp.einsum(
                "hqk,qhe->khe", score_grad_low, query_part, preferred_element_type=jnp.float32
            )
            * 0.125
        )
        value_term = jnp.einsum(
            "hqk,qhe->khe", probs_low, upstream, preferred_element_type=jnp.float32
        )
        query_grads.append(query_term.reshape(row_count, group_cols))
        key_terms.append(key_term.reshape(key_count, group_cols))
        value_terms.append(value_term.reshape(key_count, group_cols))
    key_grad, value_grad = (
        lax.psum_scatter(
            jnp.concatenate(key_terms, axis=1).astype(jnp.bfloat16),
            "frames",
            scatter_dimension=0,
            tiled=True,
        ).astype(jnp.float32),
        lax.psum_scatter(
            jnp.concatenate(value_terms, axis=1).astype(jnp.bfloat16),
            "frames",
            scatter_dimension=0,
            tiled=True,
        ).astype(jnp.float32),
    )
    query_grad_low = jnp.concatenate(query_grads, axis=1).astype(jnp.bfloat16)
    value_grad_low = value_grad.astype(jnp.bfloat16)
    projected_grad_low = jnp.concatenate(
        [query_grad_low, key_grad.astype(jnp.bfloat16), value_grad_low], axis=1
    )
    qkv_grad = jnp.einsum(
        "td,tc->dc", normed_low, projected_grad_low, preferred_element_type=jnp.float32
    )
    bias_query_grad = jnp.sum(query_grad_low.astype(jnp.float32), axis=0)
    bias_value_grad = jnp.sum(value_grad_low.astype(jnp.float32), axis=0)
    normed_grad = jnp.einsum(
        "tc,dc->td", projected_grad_low, qkv_full, preferred_element_type=jnp.float32
    )
    input_from_norm, gain_one_grad, shift_one_grad = norm_one_back(normed_grad)
    token_grad = hidden_grad + input_from_norm
    vector_grad = jnp.concatenate(
        [
            gain_one_grad,
            shift_one_grad,
            bias_query_grad,
            bias_value_grad,
            bias_output_grad,
            gain_two_grad,
            shift_two_grad,
            bias_down_grad,
            bias_up_grad,
        ]
    )
    frame_sums = (
        lax.psum_scatter(qkv_grad, "frames", scatter_dimension=0, tiled=True),
        lax.psum_scatter(out_grad, "frames", scatter_dimension=0, tiled=True),
        lax.psum_scatter(up_grad, "frames", scatter_dimension=0, tiled=True),
        lax.psum_scatter(down_grad, "frames", scatter_dimension=0, tiled=True),
        lax.psum_scatter(vector_grad, "frames", scatter_dimension=0, tiled=True),
    )
    summed = lax.psum(
        (frame_sums[0], frame_sums[1], frame_sums[2], frame_sums[3], frame_sums[4]), "items"
    )
    qkv_new = adamw(qkv_weight, qkv_first, qkv_second, summed[0], 0.05, 0.05)
    out_new = adamw(out_weight, out_first, out_second, summed[1], 0.5, 0.05)
    up_new = adamw(up_weight, up_first, up_second, summed[2], 0.05, 0.05)
    down_new = adamw(down_weight, down_first, down_second, summed[3], 0.03, 0.05)
    vector_new = adamw(vectors, vector_first, vector_second, summed[4], 0.3, 0.0)
    return (
        block_out.reshape(1, slot_local, FRAME_TOK, D),
        token_grad.reshape(1, slot_local, FRAME_TOK, D),
        qkv_new[0],
        qkv_new[1],
        qkv_new[2],
        out_new[0],
        out_new[1],
        out_new[2],
        up_new[0],
        up_new[1],
        up_new[2],
        down_new[0],
        down_new[1],
        down_new[2],
        vector_new[0],
        vector_new[1],
        vector_new[2],
    )


def solution(mesh):
    placed = (
        P("items", "frames", None, None),
        P("items", "frames", None, None),
        P("items", "frames"),
        P("items", "frames"),
        P("items", None),
        P("items", None),
        P("items", None),
        P("frames", None),
        P("frames", None),
        P("frames", None),
        P("frames", None),
        P("frames", None),
        P("frames", None),
        P("frames", None),
        P("frames", None),
        P("frames", None),
        P("frames", None),
        P("frames", None),
        P("frames", None),
        P("frames"),
        P("frames"),
        P("frames"),
    )
    return jax.shard_map(
        on_device,
        mesh=mesh,
        in_specs=placed,
        out_specs=(
            P("items", "frames", None, None),
            P("items", "frames", None, None),
            P("frames", None),
            P("frames", None),
            P("frames", None),
            P("frames", None),
            P("frames", None),
            P("frames", None),
            P("frames", None),
            P("frames", None),
            P("frames", None),
            P("frames", None),
            P("frames", None),
            P("frames", None),
            P("frames"),
            P("frames"),
            P("frames"),
        ),
        check_vma=False,
    )
```

profile of v0, /device:TPU:13, one launch (start us, length us, event | category | flops | bytes accessed | tf_op | source)
XLA Modules:
  0.0 1538.9 jit_solution(17736534517583746563)
XLA Ops:
  9.9 10.5 all-gather
  43.1 35.9 %all-gather.8.cloned.1.call-done = bf16[768,2304]{1,0:T(8,128)(2,1)} async-done(((bf16[192,2304]{1,0:T(8,128)(2,1)}), bf16[768,2304]{1,0:T(8,128)(2,1)}) %all-gather.8.cloned.1.call-update) | async-done | bytes 3538960 | tf_op jit(solution)/shard_map/all_gather | solution.py:118
  79.0 5.2 fusion.88
  106.9 70.9 %all-gather.12.cloned.1.call-done = bf16[3136,768]{1,0:T(8,128)(2,1)} async-done(((bf16[784,768]{1,0:T(8,128)(2,1)}), bf16[3136,768]{1,0:T(8,128)(2,1)}) %all-gather.12.cloned.1.call-update) | async-done | bytes 4816912 | tf_op jit(solution)/shard_map/all_gather | solution.py:155
  191.4 78.1 %all-gather.10.cloned.1.call-done = bf16[3136,768]{1,0:T(8,128)(2,1)} async-done(((bf16[784,768]{1,0:T(8,128)(2,1)}), bf16[3136,768]{1,0:T(8,128)(2,1)}) %all-gather.10.cloned.1.call-update) | async-done | bytes 4816912 | tf_op jit(solution)/shard_map/all_gather | solution.py:156
  269.5 4.7 fusion.101
  281.5 20.1 %fusion.106 = (f32[4,784]{1,0:T(4,128)S(1)}, f32[4,784,3136]{2,1,0:T(8,128)}) fusion(pred[784,3136]{1,0:T(8,128)(4,1)} %compare_and_fusion, bf16[784,4,64]{0,2,1:T(8,128)(2,1)S(1)} %bitcast.126, bf16[3136,4,64]{0,2,1:T(8,128)(2,1)} %bitcast.134), kind=kOutput, calls=%fused_computation.205 | convolution fusion | flops 1298156544 | bytes 43816192 | tf_op jit(solution)/shard_map/sub | solution.py:173
  301.6 20.2 %fusion.105 = (f32[4,784]{1,0:T(4,128)S(1)}, f32[4,784,3136]{2,1,0:T(8,128)}) fusion(pred[784,3136]{1,0:T(8,128)(4,1)} %compare_and_fusion, bf16[784,4,64]{0,2,1:T(8,128)(2,1)S(1)} %bitcast.128, bf16[3136,4,64]{0,2,1:T(8,128)(2,1)S(1)} %bitcast.130), kind=kOutput, calls=%fused_computation.204 | convolution fusion | flops 1298156544 | bytes 43816192 | tf_op jit(solution)/shard_map/sub | solution.py:173
  321.9 15.9 %fusion.60 = bf16[4,64,784]{2,1,0:T(8,128)(2,1)S(1)} fusion(bf16[3136,4,64]{0,2,1:T(8,128)(2,1)} %bitcast.145, f32[4,784,3136]{2,1,0:T(8,128)} %get-tuple-element.175, f32[4,784]{1,0:T(4,128)S(1)} %get-tuple-element.174), kind=kOutput, calls=%fused_computation.116 | convolution fusion | flops 1278685184 | bytes 41357568 | tf_op jit(solution)/shard_map/hqk,khe->qhe/dot_general | solution.py:176
  337.8 15.6 %fusion.63 = bf16[4,64,784]{2,1,0:T(8,128)(2,1)S(1)} fusion(bf16[3136,4,64]{0,2,1:T(8,128)(2,1)S(1)} %bitcast.147, f32[4,784,3136]{2,1,0:T(8,128)} %get-tuple-element.173, f32[4,784]{1,0:T(4,128)S(1)} %get-tuple-element.172), kind=kOutput, calls=%fused_computation.117 | convolution fusion | flops 1278685184 | bytes 41357568 | tf_op jit(solution)/shard_map/hqk,khe->qhe/dot_general | solution.py:176
  353.4 20.2 %fusion.107 = (f32[4,784]{1,0:T(4,128)S(1)}, f32[4,784,3136]{2,1,0:T(8,128)}) fusion(pred[784,3136]{1,0:T(8,128)(4,1)} %compare_and_fusion, bf16[784,4,64]{0,2,1:T(8,128)(2,1)S(1)} %bitcast.125, bf16[3136,4,64]{0,2,1:T(8,128)(2,1)S(1)} %bitcast.133), kind=kOutput, calls=%fused_computation.206 | convolution fusion | flops 1298156544 | bytes 43816192 | tf_op jit(solution)/shard_map/sub | solution.py:173
  376.6 16.4 %fusion.57 = bf16[4,64,784]{2,1,0:T(8,128)(2,1)} fusion(bf16[3136,4,64]{0,2,1:T(8,128)(2,1)S(1)} %bitcast.149, f32[4,784,3136]{2,1,0:T(8,128)} %get-tuple-element.177, f32[4,784]{1,0:T(4,128)S(1)} %get-tuple-element.176), kind=kOutput, calls=%fused_computation.115 | convolution fusion | flops 1278685184 | bytes 41357568 | tf_op jit(solution)/shard_map/hqk,khe->qhe/dot_general | solution.py:176
  398.0 9.0 fusion.90
  407.0 73.3 %all-gather.18.cloned.1.call-done = bf16[3072,768]{1,0:T(8,128)(2,1)} async-done(((bf16[768,768]{1,0:T(8,128)(2,1)}), bf16[3072,768]{1,0:T(8,128)(2,1)}) %all-gather.18.cloned.1.call-update) | async-done | bytes 4718608 | tf_op jit(solution)/shard_map/all_gather | solution.py:121
  480.3 31.8 %convert_reduce_fusion = (f32[3072]{0:T(1024)}, bf16[784,3072]{1,0:T(8,128)(2,1)S(1)}, f32[784,3072]{1,0:T(8,128)}) fusion(f32[784,3072]{1,0:T(8,128)} %fusion.90, f32[3072]{0:T(1024)S(1)} %copy-done.59, bf16[784,768]{1,0:T(8,128)(2,1)} %reshape.375, bf16[3072,768]{1,0:T(8,128)(2,1)} %all-gather.18.cloned.1.call-done), kind=kOutput, calls=%fused_computation.45 | convolution fusion | flops 3880006656 | bytes 30031872 | tf_op jit(solution)/shard_map/td,fd->tf/dot_general | solution.py:198
  512.1 4.9 multiply_reduce_fusion.3
  522.4 15.6 %fusion.45 = bf16[4,64,3136]{2,1,0:T(8,128)(2,1)} fusion(bf16[784,4,64]{0,2,1:T(8,128)(2,1)S(1)} %bitcast.151, f32[4,784,3136]{2,1,0:T(8,128)} %get-tuple-element.173, f32[4,784]{1,0:T(4,128)S(1)} %copy-done.81), kind=kOutput, calls=%fused_computation.69 | convolution fusion | flops 1279287296 | bytes 41357568 | tf_op jit(solution)/shard_map/hqk,qhe->khe/dot_general | solution.py:246
  538.0 25.7 %multiply_reduce_fusion = (f32[4,784]{1,0:T(4,128)}, f32[4,784,3136]{2,1,0:T(8,128)}) fusion(f32[4,784,3136]{2,1,0:T(8,128)} %get-tuple-element.173, f32[4,784]{1,0:T(4,128)S(1)} %copy-done.81, bf16[784,4,64]{0,2,1:T(8,128)(2,1)S(1)} %bitcast.152, bf16[3136,4,64]{0,2,1:T(8,128)(2,1)S(1)} %bitcast.148), kind=kOutput, calls=%fused_computation.4 | convolution fusion | flops 1288315904 | bytes 80708096 | tf_op jit(solution)/shard_map/qhe,khe->hqk/dot_general | solution.py:231
  564.7 14.5 fusion.42
  579.2 30.2 %multiply_reduce_fusion.1 = (f32[4,784]{1,0:T(4,128)S(1)}, f32[4,784,3136]{2,1,0:T(8,128)}) fusion(f32[4,784,3136]{2,1,0:T(8,128)} %get-tuple-element.175, f32[4,784]{1,0:T(4,128)S(1)} %copy-done.77, bf16[784,4,64]{0,2,1:T(8,128)(2,1)} %bitcast.154, bf16[3136,4,64]{0,2,1:T(8,128)(2,1)S(1)} %bitcast.146), kind=kOutput, calls=%fused_computation.6 | convolution fusion | flops 1288315904 | bytes 80708096 | tf_op jit(solution)/shard_map/qhe,khe->hqk/dot_general | solution.py:231
  611.4 14.4 fusion.39
  625.9 26.4 %multiply_reduce_fusion.2 = (f32[4,784]{1,0:T(4,128)S(1)}, f32[4,784,3136]{2,1,0:T(8,128)}) fusion(f32[4,784,3136]{2,1,0:T(8,128)} %get-tuple-element.177, f32[4,784]{1,0:T(4,128)S(1)} %copy-done.79, bf16[784,4,64]{0,2,1:T(8,128)(2,1)} %bitcast.156, bf16[3136,4,64]{0,2,1:T(8,128)(2,1)} %bitcast.150), kind=kOutput, calls=%fused_computation.8 | convolution fusion | flops 1288315904 | bytes 80708096 | tf_op jit(solution)/shard_map/qhe,khe->hqk/dot_general | solution.py:231
  654.8 7.4 copy.146
  662.9 33.2 %multiply_convert_fusion = bf16[4,784,3136]{2,1,0:T(8,128)(2,1)} fusion(f32[4,784,3136]{2,1,0:T(8,128)} %get-tuple-element.186, f32[4,784]{1,0:T(4,128)S(1)} %copy-done.83, f32[4,784,3136]{2,1,0:T(8,128)} %get-tuple-element.173, f32[4,784]{1,0:T(4,128)S(1)} %copy-done.82), kind=kLoop, calls=%fused_computation.3 | loop fusion | flops 39337984 | bytes 98370048 | tf_op jit(solution)/shard_map/convert_element_type | solution.py:235
  696.2 9.9 fusion.50
  706.1 32.3 %multiply_convert_fusion.1 = bf16[4,784,3136]{2,1,0:T(8,128)(2,1)} fusion(f32[4,784,3136]{2,1,0:T(8,128)} %get-tuple-element.184, f32[4,784]{1,0:T(4,128)S(1)} %get-tuple-element.183, f32[4,784,3136]{2,1,0:T(8,128)} %get-tuple-element.175, f32[4,784]{1,0:T(4,128)S(1)} %copy-done.77), kind=kLoop, calls=%fused_computation.5 | loop fusion | flops 39337984 | bytes 98370048 | tf_op jit(solution)/shard_map/convert_element_type | solution.py:235
  738.4 10.2 fusion.49
  748.6 32.0 %multiply_convert_fusion.2 = bf16[4,784,3136]{2,1,0:T(8,128)(2,1)} fusion(f32[4,784,3136]{2,1,0:T(8,128)} %get-tuple-element.182, f32[4,784]{1,0:T(4,128)S(1)} %get-tuple-element.181, f32[4,784,3136]{2,1,0:T(8,128)} %get-tuple-element.177, f32[4,784]{1,0:T(4,128)S(1)} %copy-done.79), kind=kLoop, calls=%fused_computation.7 | loop fusion | flops 39337984 | bytes 98370048 | tf_op jit(solution)/shard_map/convert_element_type | solution.py:235
  780.6 10.1 fusion.48
  793.3 7.4 copy.144
  806.3 10.5 fusion.89
  817.5 11.2 multiply_convert_fusion.3
  828.7 9.5 fusion.109
  838.5 10.9 fusion.68
  850.3 10.6 fusion.67
  861.7 10.5 fusion.66
  876.3 12.4 reduce-scatter.19.cloned.1.call-done
  895.1 8.7 fusion.87
  907.6 8.7 add_convert_fusion.1
  919.5 18.2 %reduce-scatter.13.cloned.1.call-done = f32[192,768]{1,0:T(8,128)} async-done(((f32[768,768]{1,0:T(8,128)}), f32[192,768]{1,0:T(8,128)}) %reduce-scatter.13.cloned.1.call-update) | async-done | bytes 589840 | tf_op jit(solution)/shard_map/reduce_scatter | solution.py:296
  937.7 165.2 %reduce-scatter.15.cloned.1.call-done = f32[192,3072]{1,0:T(8,128)} async-done(((f32[768,3072]{1,0:T(8,128)}), f32[192,3072]{1,0:T(8,128)}) %reduce-scatter.15.cloned.1.call-update) | async-done | bytes 2359312 | tf_op jit(solution)/shard_map/reduce_scatter | solution.py:297
  1103.0 164.5 %reduce-scatter.17.cloned.1.call-done = f32[768,768]{1,0:T(8,128)} async-done(((f32[3072,768]{1,0:T(8,128)}), f32[768,768]{1,0:T(8,128)}) %reduce-scatter.17.cloned.1.call-update) | async-done | bytes 2359312 | tf_op jit(solution)/shard_map/reduce_scatter | solution.py:298
  1267.5 126.7 %reduce-scatter.11.cloned.1.call-done = f32[192,2304]{1,0:T(8,128)} async-done(((f32[768,2304]{1,0:T(8,128)}), f32[192,2304]{1,0:T(8,128)}) %reduce-scatter.11.cloned.1.call-update) | async-done | bytes 1769488 | tf_op jit(solution)/shard_map/reduce_scatter | solution.py:295
  1395.9 7.4 multiply_reduce_fusion.4
  1412.7 13.4 all-reduce
  1426.2 22.4 %psum.39 = f32[2304]{0:T(1024)S(1)} all-reduce(f32[2304]{0:T(1024)S(1)} %dynamic-slice.1), channel_id=1, replica_groups=mesh['items'=8,'frames'=4] {'items'}, use_global_device_ids=true, to_apply=%region_40.41 | all-reduce | flops 2304 | bytes 18432 | tf_op jit(solution)/shard_map/psum | solution.py:301
  1449.3 62.4 %all-reduce.4.cloned.1.call-done = (f32[192,2304]{1,0:T(8,128)}, f32[192,768]{1,0:T(8,128)}, f32[192,3072]{1,0:T(8,128)}, f32[768,768]{1,0:T(8,128)}) async-done(((f32[192,2304]{1,0:T(8,128)}, f32[192,768]{1,0:T(8,128)}, f32[192,3072]{1,0:T(8,128)}, f32[768,768]{1,0:T(8,128)}), (f32[192,2304]{1,0:T(8,128)}, f32[192,768]{1,0:T(8,128)}, f32[192,3072]{1,0:T(8,128)}, ...) | async-done | bytes 7077904 | tf_op jit(solution)/shard_map/psum | solution.py:301
  1514.8 5.4 multiply_subtract_fusion.2
  (348 shorter events, 141.7 us)
Async XLA Ops:
  7.2 71.8 %all-gather.8.cloned.1.call-start = ((), (), s32[]{:S(2)}) async-start(), calls=%async_computation.6 | async-start | bytes 4423680 | tf_op jit(solution)/shard_map/all_gather | solution.py:118
  9.9 168.0 %all-gather.12.cloned.1.call-start = ((), (), s32[]{:S(2)}) async-start(), calls=%async_computation.8 | async-start | bytes 6021120 | tf_op jit(solution)/shard_map/all_gather | solution.py:155
  26.2 52.8 %copy-start.71 = (f32[784]{0:T(1024)}, f32[784]{0:T(1024)S(1)}, u32[]{:S(2)}) copy-start(f32[784]{0:T(1024)S(1)} %div.185) | copy-start | bytes 9412
  30.9 48.1 %copy-start.73 = (f32[784]{0:T(1024)}, f32[784]{0:T(1024)S(1)}, u32[]{:S(2)}) copy-start(f32[784]{0:T(1024)S(1)} %rsqrt.20) | copy-start | bytes 9412
  42.4 41.8 %copy-start.15 = (f32[784,768]{1,0:T(8,128)}, f32[784,768]{1,0:T(8,128)S(1)}, u32[]{:S(2)}) copy-start(f32[784,768]{1,0:T(8,128)S(1)} %add.224) | copy-start | bytes 7225348
  43.1 41.1 %copy-start.69 = (f32[768]{0:T(1024)}, f32[768]{0:T(1024)S(1)}, u32[]{:S(2)}) copy-start(f32[768]{0:T(1024)S(1)} %get-tuple-element.159) | copy-start | bytes 9220
  43.1 41.1 %copy-start.88 = (f32[768]{0:T(1024)}, f32[768]{0:T(1024)S(1)}, u32[]{:S(2)}) copy-start(f32[768]{0:T(1024)S(1)} %get-tuple-element.158) | copy-start | bytes 9220
  88.2 181.2 %all-gather.10.cloned.1.call-start = ((), (), s32[]{:S(2)}) async-start(), calls=%async_computation.7 | async-start | bytes 6021120 | tf_op jit(solution)/shard_map/all_gather | solution.py:156
  92.6 300.5 %all-gather.14.cloned.1.call-start = ((), (), s32[]{:S(2)}) async-start(), calls=%async_computation.9 | async-start | bytes 1474560 | tf_op jit(solution)/shard_map/all_gather | solution.py:119
  93.4 304.5 %all-gather.16.cloned.1.call-start = ((), (), s32[]{:S(2)}) async-start(), calls=%async_computation.10 | async-start | bytes 5898240 | tf_op jit(solution)/shard_map/all_gather | solution.py:120
  95.6 384.7 %all-gather.18.cloned.1.call-start = ((), (), s32[]{:S(2)}) async-start(), calls=%async_computation.11 | async-start | bytes 5898240 | tf_op jit(solution)/shard_map/all_gather | solution.py:121
  98.8 775.0 %reduce-scatter.21.cloned.1.call-start = ((), (), s32[]{:S(2)}) async-start(), calls=%async_computation.17 | async-start | bytes 6021120
  106.7 194.9 %copy-start.9 = (bf16[784,256]{0,1:T(8,128)(2,1)}, bf16[784,256]{0,1:T(8,128)(2,1)S(1)}, u32[]{:S(2)}) copy-start(bf16[784,256]{0,1:T(8,128)(2,1)S(1)} %copy.136) | copy-start | bytes 1204228
  106.9 174.6 %copy-start.8 = (bf16[784,256]{0,1:T(8,128)(2,1)}, bf16[784,256]{0,1:T(8,128)(2,1)S(1)}, u32[]{:S(2)}) copy-start(bf16[784,256]{0,1:T(8,128)(2,1)S(1)} %copy.133) | copy-start | bytes 1204228
  187.3 114.3 %copy-start.23 = (bf16[3136,256]{0,1:T(8,128)(2,1)}, bf16[3136,256]{0,1:T(8,128)(2,1)S(1)}, u32[]{:S(2)}) copy-start(bf16[3136,256]{0,1:T(8,128)(2,1)S(1)} %copy.137) | copy-start | bytes 4816900
  301.6 20.3 %copy-start.76 = (f32[4,784]{1,0:T(4,128)}, f32[4,784]{1,0:T(4,128)S(1)}, u32[]{:S(2)}) copy-start(f32[4,784]{1,0:T(4,128)S(1)} %get-tuple-element.174) | copy-start | bytes 37636
  321.9 15.9 %copy-start.80 = (f32[4,784]{1,0:T(4,128)}, f32[4,784]{1,0:T(4,128)S(1)}, u32[]{:S(2)}) copy-start(f32[4,784]{1,0:T(4,128)S(1)} %get-tuple-element.172) | copy-start | bytes 37636
  321.9 15.9 %copy-start.44 = (bf16[3136,256]{0,1:T(8,128)(2,1)S(1)}, bf16[3136,256]{0,1:T(8,128)(2,1)}, u32[]{:S(2)}) copy-start(bf16[3136,256]{0,1:T(8,128)(2,1)} %copy.135) | copy-start | bytes 4816900
  337.8 55.3 %copy-start.100 = (bf16[4,64,784]{2,1,0:T(8,128)(2,1)}, bf16[4,64,784]{2,1,0:T(8,128)(2,1)S(1)}, u32[]{:S(2)}) copy-start(bf16[4,64,784]{2,1,0:T(8,128)(2,1)S(1)} %fusion.60) | copy-start | bytes 1204228
  337.8 15.6 %copy-start.7 = (bf16[784,256]{0,1:T(8,128)(2,1)S(1)}, bf16[784,256]{0,1:T(8,128)(2,1)}, u32[]{:S(2)}) copy-start(bf16[784,256]{0,1:T(8,128)(2,1)} %copy.130) | copy-start | bytes 1204228
  337.8 15.6 %copy-start.25 = (bf16[3136,256]{0,1:T(8,128)(2,1)S(1)}, bf16[3136,256]{0,1:T(8,128)(2,1)}, u32[]{:S(2)}) copy-start(bf16[3136,256]{0,1:T(8,128)(2,1)} %copy.131) | copy-start | bytes 4816900
  353.4 39.7 %copy-start.102 = (bf16[4,64,784]{2,1,0:T(8,128)(2,1)}, bf16[4,64,784]{2,1,0:T(8,128)(2,1)S(1)}, u32[]{:S(2)}) copy-start(bf16[4,64,784]{2,1,0:T(8,128)(2,1)S(1)} %fusion.63) | copy-start | bytes 1204228
  373.7 19.4 %copy-start.78 = (f32[4,784]{1,0:T(4,128)}, f32[4,784]{1,0:T(4,128)S(1)}, u32[]{:S(2)}) copy-start(f32[4,784]{1,0:T(4,128)S(1)} %get-tuple-element.176) | copy-start | bytes 37636
  376.6 16.5 %copy-start.46 = (bf16[3136,256]{0,1:T(8,128)(2,1)}, bf16[3136,256]{0,1:T(8,128)(2,1)S(1)}, u32[]{:S(2)}) copy-start(bf16[3136,256]{0,1:T(8,128)(2,1)S(1)} %copy.129) | copy-start | bytes 4816900
  376.6 16.5 %copy-start.90 = (f32[768]{0:T(1024)S(1)}, f32[768]{0:T(1024)}, u32[]{:S(2)}) copy-start(f32[768]{0:T(1024)} %get-tuple-element.155) | copy-start | bytes 9220
  398.0 82.3 %copy-start.59 = (f32[3072]{0:T(1024)S(1)}, f32[3072]{0:T(1024)}, u32[]{:S(2)}) copy-start(f32[3072]{0:T(1024)} %slice.125) | copy-start | bytes 36868
  480.3 31.8 %copy-start.3 = (f32[784,768]{1,0:T(8,128)S(1)}, f32[784,768]{1,0:T(8,128)}, u32[]{:S(2)}) copy-start(f32[784,768]{1,0:T(8,128)} %copy-done.2) | copy-start | bytes 7225348
  480.3 31.8 %copy-start.49 = (f32[784]{0:T(1024)S(1)}, f32[784]{0:T(1024)}, u32[]{:S(2)}) copy-start(f32[784]{0:T(1024)} %copy-done.48) | copy-start | bytes 9412
  480.3 31.8 %copy-start.52 = (f32[768]{0:T(1024)S(1)}, f32[768]{0:T(1024)}, u32[]{:S(2)}) copy-start(f32[768]{0:T(1024)} %get-tuple-element.154) | copy-start | bytes 9220
  480.3 31.8 %copy-start.55 = (f32[784]{0:T(1024)S(1)}, f32[784]{0:T(1024)}, u32[]{:S(2)}) copy-start(f32[784]{0:T(1024)} %copy-done.54) | copy-start | bytes 9412
  480.3 31.8 %copy-start.95 = (bf16[768,3072]{1,0:T(8,128)(2,1)S(1)}, bf16[768,3072]{1,0:T(8,128)(2,1)}, u32[]{:S(2)}) copy-start(bf16[768,3072]{1,0:T(8,128)(2,1)} %all-gather.16.cloned.1.call-done) | copy-start | bytes 14155780
  522.4 15.6 %copy-start.45 = (bf16[3136,256]{0,1:T(8,128)(2,1)S(1)}, bf16[3136,256]{0,1:T(8,128)(2,1)}, u32[]{:S(2)}) copy-start(bf16[3136,256]{0,1:T(8,128)(2,1)} %copy.135) | copy-start | bytes 4816900
  538.0 26.7 %copy-start.77 = (f32[4,784]{1,0:T(4,128)S(1)}, f32[4,784]{1,0:T(4,128)}, u32[]{:S(2)}) copy-start(f32[4,784]{1,0:T(4,128)} %copy-done.76) | copy-start | bytes 37636
  564.7 14.5 copy-start.43
  579.2 32.2 %copy-start.79 = (f32[4,784]{1,0:T(4,128)S(1)}, f32[4,784]{1,0:T(4,128)}, u32[]{:S(2)}) copy-start(f32[4,784]{1,0:T(4,128)} %copy-done.78) | copy-start | bytes 37636
  625.9 26.4 %copy-start.42 = (bf16[4,64,3136]{2,1,0:T(8,128)(2,1)S(1)}, bf16[4,64,3136]{2,1,0:T(8,128)(2,1)}, u32[]{:S(2)}) copy-start(bf16[4,64,3136]{2,1,0:T(8,128)(2,1)} %fusion.45) | copy-start | bytes 4816900
  662.2 226.4 %reduce-scatter.19.cloned.1.call-start = ((), (), s32[]{:S(2)}) async-start(), calls=%async_computation.16 | async-start | bytes 6021120
  662.9 33.2 %copy-start.10 = (bf16[784,256]{0,1:T(8,128)(2,1)S(1)}, bf16[784,256]{0,1:T(8,128)(2,1)}, u32[]{:S(2)}) copy-start(bf16[784,256]{0,1:T(8,128)(2,1)} %copy-done.9) | copy-start | bytes 1204228
  800.7 137.0 %reduce-scatter.13.cloned.1.call-start = ((), (), s32[]{:S(2)}) async-start(), calls=%async_computation.13 | async-start | bytes 2949120 | tf_op jit(solution)/shard_map/reduce_scatter | solution.py:296
  806.2 296.8 %reduce-scatter.15.cloned.1.call-start = ((), (), s32[]{:S(2)}) async-start(), calls=%async_computation.14 | async-start | bytes 11796480 | tf_op jit(solution)/shard_map/reduce_scatter | solution.py:297
  816.8 450.7 %reduce-scatter.17.cloned.1.call-start = ((), (), s32[]{:S(2)}) async-start(), calls=%async_computation.15 | async-start | bytes 11796480 | tf_op jit(solution)/shard_map/reduce_scatter | solution.py:298
  838.3 555.9 %reduce-scatter.11.cloned.1.call-start = ((), (), s32[]{:S(2)}) async-start(), calls=%async_computation.12 | async-start | bytes 8847360 | tf_op jit(solution)/shard_map/reduce_scatter | solution.py:295
  903.9 607.9 %all-reduce.4.cloned.1.call-start = ((), (), s32[]{:S(2)}) async-start(), calls=%async_computation.18 | async-start | bytes 14155776 | tf_op jit(solution)/shard_map/psum | solution.py:301
  1409.9 38.8 %copy-start.62 = (f32[2304]{0:T(1024)S(1)}, f32[2304]{0:T(1024)}, u32[]{:S(2)}) copy-start(f32[2304]{0:T(1024)} %param.41) | copy-start | bytes 27652
  1409.9 38.8 %copy-start.85 = (f32[2304]{0:T(1024)S(1)}, f32[2304]{0:T(1024)}, u32[]{:S(2)}) copy-start(f32[2304]{0:T(1024)} %param.43) | copy-start | bytes 27652
  1409.9 38.7 %copy-start.86 = (f32[2304]{0:T(1024)S(1)}, f32[2304]{0:T(1024)}, u32[]{:S(2)}) copy-start(f32[2304]{0:T(1024)} %param.42) | copy-start | bytes 27652
  1409.9 101.8 %copy-start.34 = (f32[192,768]{1,0:T(8,128)S(1)}, f32[192,768]{1,0:T(8,128)}, u32[]{:S(2)}) copy-start(f32[192,768]{1,0:T(8,128)} %param.32) | copy-start | bytes 1769476
  1412.6 102.2 %copy-start.22 = (f32[192,2304]{1,0:T(8,128)S(1)}, f32[192,2304]{1,0:T(8,128)}, u32[]{:S(2)}) copy-start(f32[192,2304]{1,0:T(8,128)} %param.29) | copy-start | bytes 5308420
  (70 other events, 292.8 us)
Sparse Core Ops, SparseCore 0:
  10.2 68.7 all-gather.7
  88.4 89.4 all-gather.11
  180.0 89.4 all-gather.9
  271.5 30.6 all-gather.13
  304.2 86.7 all-gather.15
  392.4 87.8 all-gather.17
  662.4 87.8 reduce-scatter.20
  800.8 87.8 reduce-scatter.18
  891.6 46.1 reduce-scatter.12
  939.9 162.9 reduce-scatter.14
  1105.3 162.1 reduce-scatter.16
  1269.6 124.5 reduce-scatter.10
  1397.9 113.7 all-reduce.3
where the time goes:
time: 1550 us; the launch traced here: 1540 us
  waiting for transfers between devices  808 us (52%)
  matrix products  402 us (26%)
  other arithmetic  166 us (11%)
  local copies, waits for them, and re-layouts  98.9 us (6%)
  blocking collectives  46.3 us (3%)
  between operations  16.3 us (1%)
    reduce_scatter x1, waiting for transfers between devices, on_device(): lax.psum_scatter(up_grad, 'frames', scatter_dimension=0, tiled=True)  165 us
    reduce_scatter x1, waiting for transfers between devices, on_device(): lax.psum_scatter(down_grad, 'frames', scatter_dimension=0, tiled=True)  165 us
    reduce_scatter x1, waiting for transfers between devices, on_device(): lax.psum_scatter(qkv_grad, 'frames', scatter_dimension=0, tiled=True)  127 us
    convert_element_type x3, other arithmetic, on_device(): score_grad_low = (probs * (prob_grad - centre)).astype(jnp.bfloat16)  97.6 us
    dot_general x3, matrix products, on_device(): jnp.einsum('qhe,khe->hqk', upstream, value_part, preferred_element_type=j...  82.3 us
    all_gather x1, waiting for transfers between devices, on_device(): lax.all_gather(value_low, 'frames', axis=0, tiled=True)  78.1 us
    all_gather x1, waiting for transfers between devices, on_device(): lax.all_gather(down_weight.astype(jnp.bfloat16), 'frames', axis=0, tiled=...  73.3 us
    all_gather x1, waiting for transfers between devices, on_device(): lax.all_gather(key_low, 'frames', axis=0, tiled=True)  70.9 us
  transfers between devices with their start and end apart: 13, of which 10 were waited for; matrix products, arithmetic and copies ran while one was open for 29% of the time, Pallas kernels for 0%

commit v1 on v0

v1 whole, which is shorter than its diff:
```python
import jax
import jax.numpy as jnp
from jax import lax
from jax.experimental import pallas as pl
from jax.experimental.pallas import tpu as pltpu
from jax.sharding import PartitionSpec as P

D = 768
HEADS = 12
HEAD = 64
GRID = 14
STEP = 10
FRAME_TOK = 196


beta_one = 0.9
beta_two = 0.999


def sincos(values, length_out):
    half_width = length_out // 2
    frequency = 1.0 / 10000.0 ** (jnp.arange(half_width, dtype=jnp.float32) / half_width)
    angles = values[..., None] * frequency
    return jnp.concatenate([jnp.sin(angles), jnp.cos(angles)], axis=-1)


def positions(year_values, day_values):
    cell_index = jnp.arange(FRAME_TOK, dtype=jnp.int32)
    spatial = jnp.concatenate(
        [
            sincos((cell_index // GRID).astype(jnp.float32), 3 * D // 8),
            sincos((cell_index % GRID).astype(jnp.float32), 3 * D // 8),
        ],
        axis=-1,
    )
    temporal = jnp.concatenate(
        [
            sincos((year_values - 2000).astype(jnp.float32), D // 8),
            sincos(day_values.astype(jnp.float32), D // 8),
        ],
        axis=-1,
    )
    slot_count = year_values.shape[0]
    return jnp.concatenate(
        [
            jnp.broadcast_to(spatial[None], (slot_count, FRAME_TOK, 3 * D // 4)),
            jnp.broadcast_to(temporal[:, None], (slot_count, FRAME_TOK, D // 4)),
        ],
        axis=-1,
    )


def slot_items(dates_group, frames_group, mask_group):
    item_ends = jnp.cumsum(dates_group)
    starts = item_ends - dates_group
    item_index = jnp.sum((frames_group[:, None] >= item_ends[None, :]).astype(jnp.int32), axis=1)
    is_first = jnp.any(frames_group[:, None] == starts[None, :], axis=1)
    is_valid = jnp.logical_or(mask_group > 0, is_first)
    return (item_index, is_valid)


def layer_norm(values, gain_vec, shift_vec):
    average = jnp.mean(values, axis=-1, keepdims=True)
    centred = values - average
    spread = jnp.mean(centred * centred, axis=-1, keepdims=True)
    return centred * lax.rsqrt(spread + 1e-06) * gain_vec + shift_vec


def unpack(vector_all):
    pieces = [vector_all[index * D : (index + 1) * D] for index in range(8)]
    return tuple(pieces) + (vector_all[8 * D :],)


def exact_gelu(values):
    return jax.nn.gelu(values, approximate=False)


SP = 208
NK = 6
NEG = -1e30
NT = (((1,), (1,)), ((), ()))
NN = (((1,), (0,)), ((), ()))


def mm(a, b, dims=NN):
    return lax.dot_general(a, b, dims, preferred_element_type=jnp.float32)


def augmented_keys(parts, valid, bias_lane, mine):
    row = lax.broadcasted_iota(jnp.int32, (SP, 128), 0)
    lane = lax.broadcasted_iota(jnp.int32, (SP, 128), 1)
    blocks = []
    for part, live in zip(parts, valid):
        bias = jnp.where(row >= FRAME_TOK, NEG, live).astype(jnp.bfloat16)
        blocks.append(jnp.where(mine, part, jnp.where(lane == bias_lane, bias, jnp.zeros_like(part))))
    return jnp.concatenate(blocks, axis=0)


def attn_fwd_kernel(idx_ref, val_ref, q_ref, k_ref, v_ref, o_ref, lse_ref):
    lane = lax.broadcasted_iota(jnp.int32, (SP, 128), 1)

    def one(step, _):
        j, b = step // 6, step % 6
        cols = pl.ds(pl.multiple_of(b * 128, 128), 128)
        parts = [k_ref[idx_ref[j * NK + t], :, cols] for t in range(NK)]
        valid = [jnp.where(val_ref[j * NK + t] > 0, 0.0, NEG) for t in range(NK)]
        vg = jnp.concatenate([v_ref[idx_ref[j * NK + t], :, cols] for t in range(NK)], axis=0)
        q = q_ref[j, :, cols]
        scores = []
        for h in range(2):
            mine = (lane < 64) if h == 0 else (lane >= 64)
            spare = 64 if h == 0 else 0
            ka = augmented_keys(parts, valid, spare, mine)
            qa = jnp.where(mine, q, jnp.where(lane == spare, jnp.ones_like(q), jnp.zeros_like(q)))
            scores.append(mm(qa, ka, NT))
        peaks = [jnp.max(s, axis=1, keepdims=True) for s in scores]
        probs = [jnp.exp(s - m) for s, m in zip(scores, peaks)]
        sums = [jnp.sum(p, axis=1, keepdims=True) for p in probs]
        outs = [mm(p.astype(jnp.bfloat16), vg) / total for p, total in zip(probs, sums)]
        o_ref[j, :, cols] = jnp.where(lane < 64, outs[0], outs[1]).astype(jnp.bfloat16)
        logs = [m + jnp.log(total) for m, total in zip(peaks, sums)]
        lse_ref[j, b] = jnp.transpose(jnp.where(lane == 0, logs[0], logs[1]))[:8]
        return 0

    lax.fori_loop(0, 24, one, 0)


def attn_bwd_kernel(
    idx_ref, val_ref, q_ref, k_ref, v_ref, o_ref, do_ref, lse_ref, dq_ref, dk_ref, dv_ref
):
    lane = lax.broadcasted_iota(jnp.int32, (SP, 128), 1)
    row = lax.broadcasted_iota(jnp.int32, (SP, 128), 0)
    dk_ref[...] = jnp.zeros_like(dk_ref)
    dv_ref[...] = jnp.zeros_like(dv_ref)

    def one(step, _):
        j, b = step // 6, step % 6
        cols = pl.ds(pl.multiple_of(b * 128, 128), 128)
        parts = [k_ref[idx_ref[j * NK + t], :, cols] for t in range(NK)]
        valid = [jnp.where(val_ref[j * NK + t] > 0, 0.0, NEG) for t in range(NK)]
        kg = jnp.concatenate(parts, axis=0)
        vg = jnp.concatenate([v_ref[idx_ref[j * NK + t], :, cols] for t in range(NK)], axis=0)
        kg_t = jnp.transpose(kg)
        q, do, o = q_ref[j, :, cols], do_ref[j, :, cols], o_ref[j, :, cols]
        prod_t = jnp.transpose(do.astype(jnp.float32) * o.astype(jnp.float32))
        logs = lse_ref[j, b]
        dk = jnp.zeros((NK * SP, 128), jnp.float32)
        dv = jnp.zeros((NK * SP, 128), jnp.float32)
        dq_t = []
        for h in range(2):
            mine = (lane < 64) if h == 0 else (lane >= 64)
            spare = 64 if h == 0 else 0
            ka = augmented_keys(parts, valid, spare, mine)
            qm = jnp.where(mine, q, jnp.zeros_like(q))
            qa = jnp.where(lane == spare, jnp.ones_like(q), qm)
            dom = jnp.where(mine, do, jnp.zeros_like(do))
            centre = jnp.sum(prod_t[h * 64 : (h + 1) * 64], axis=0, keepdims=True)
            s_t = mm(ka, qa, NT)
            da_t = mm(vg, dom, NT)
            p = jnp.exp(s_t - logs[h : h + 1])
            ds = (p * (da_t - centre)).astype(jnp.bfloat16)
            dv = dv + mm(p.astype(jnp.bfloat16), dom)
            dk = dk + mm(ds, qm)
            dq_t.append(mm(kg_t, ds))
        dq = jnp.transpose(jnp.concatenate([dq_t[0][:64], dq_t[1][64:]], axis=0))
        dq_ref[j, :, cols] = (dq * 0.125).astype(jnp.bfloat16)
        for t in range(NK):
            slot = idx_ref[j * NK + t]
            keep = jnp.logical_and(row < FRAME_TOK, val_ref[j * NK + t] > 0)
            dk_ref[slot, :, cols] += jnp.where(keep, dk[t * SP : (t + 1) * SP], 0.0)
            dv_ref[slot, :, cols] += jnp.where(keep, dv[t * SP : (t + 1) * SP], 0.0)
        return 0

    lax.fori_loop(0, 24, one, 0)


VM = pl.BlockSpec(memory_space=pltpu.VMEM)
SM = pl.BlockSpec(memory_space=pltpu.SMEM)


def attn_fwd(idx, val, q, k, v):
    return pl.pallas_call(
        attn_fwd_kernel,
        out_shape=(
            jax.ShapeDtypeStruct((4, SP, D), jnp.bfloat16),
            jax.ShapeDtypeStruct((4, 6, 8, SP), jnp.float32),
        ),
        in_specs=[SM, SM, VM, VM, VM],
        out_specs=(VM, VM),
        compiler_params=pltpu.CompilerParams(vmem_limit_bytes=60 * 2**20),
        cost_estimate=pl.CostEstimate(
            flops=2 * 2 * 24 * 12 * SP * SP * 256,
            bytes_accessed=14 * 2**20,
            transcendentals=24 * 12 * SP * SP,
        ),
        name="attn_fwd",
    )(idx, val, q, k, v)


def attn_bwd(idx, val, q, k, v, o, do, lse):
    return pl.pallas_call(
        attn_bwd_kernel,
        out_shape=(
            jax.ShapeDtypeStruct((4, SP, D), jnp.bfloat16),
            jax.ShapeDtypeStruct((16, SP, D), jnp.float32),
            jax.ShapeDtypeStruct((16, SP, D), jnp.float32),
        ),
        in_specs=[SM, SM] + [VM] * 6,
        out_specs=(VM, VM, VM),
        compiler_params=pltpu.CompilerParams(vmem_limit_bytes=62 * 2**20),
        cost_estimate=pl.CostEstimate(
            flops=2 * 5 * 24 * 12 * SP * SP * 256,
            bytes_accessed=40 * 2**20,
            transcendentals=24 * 12 * SP * SP,
        ),
        name="attn_bwd",
    )(idx, val, q, k, v, o, do, lse)


def key_tables(item_index, is_valid, q_items):
    match = (q_items[:, None] == item_index[None, :]) & is_valid[None, :]
    rank = jnp.cumsum(match.astype(jnp.int32), axis=1) - 1
    count = jnp.sum(match.astype(jnp.int32), axis=1)
    place = jnp.arange(NK, dtype=jnp.int32)
    hit = match[:, None, :] & (rank[:, None, :] == place[None, :, None])
    slots = jnp.arange(item_index.shape[0], dtype=jnp.int32)
    idx = jnp.sum(jnp.where(hit, slots[None, None, :], 0), axis=2)
    val = (place[None, :] < count[:, None]).astype(jnp.int32)
    return idx.reshape(-1), val.reshape(-1)


def adamw(weight, first_moment, second, gradient, step_rate, decay):
    first_new = beta_one * first_moment + (1.0 - beta_one) * gradient
    second_new = beta_two * second + (1.0 - beta_two) * gradient * gradient
    first_hat = first_new / (1.0 - beta_one**STEP)
    second_hat = second_new / (1.0 - beta_two**STEP)
    weight_new = weight - step_rate * (first_hat / (jnp.sqrt(second_hat) + 1e-08) + decay * weight)
    return (first_new, second_new, weight_new)


def on_device(
    tokens,
    cotangent,
    date_year,
    date_day,
    item_dates,
    slot_frame,
    frame_mask,
    qkv_weight,
    qkv_first,
    qkv_second,
    out_weight,
    out_first,
    out_second,
    up_weight,
    up_first,
    up_second,
    down_weight,
    down_first,
    down_second,
    vectors,
    vector_first,
    vector_second,
):
    frame_rank = lax.axis_index("frames")
    bf, f32 = jnp.bfloat16, jnp.float32
    gather = lambda w: lax.all_gather(w.astype(bf), "frames", axis=0, tiled=True)
    qkv_full, vector_full, out_full, up_full, down_full = (
        gather(qkv_weight), gather(vectors), gather(out_weight), gather(up_weight), gather(down_weight))
    (gain_one, shift_one, bias_query, bias_value, bias_output, gain_two, shift_two, bias_down, bias_up,
    ) = unpack(vector_full.astype(f32))
    pad = lambda a: jnp.pad(a[0], ((0, 0), (0, SP - FRAME_TOK), (0, 0))).reshape(4 * SP, D)
    pos = jnp.pad(positions(date_year[0], date_day[0]), ((0, 0), (0, SP - FRAME_TOK), (0, 0))).reshape(4 * SP, D)
    residual_in = pad(tokens).astype(f32) + pos
    item_index, is_valid = slot_items(item_dates[0], slot_frame[0], frame_mask[0])
    own_items = lax.dynamic_slice_in_dim(item_index, frame_rank * 4, 4)
    idx, val = key_tables(item_index, is_valid, own_items)
    normed, norm_one_back = jax.vjp(layer_norm, residual_in, gain_one, shift_one)
    normed_low = normed.astype(bf)
    normed_all = lax.all_gather(normed_low, "frames", axis=0, tiled=True)
    query_low = (mm(normed_low, qkv_full[:, :D]) + bias_query).astype(bf)
    key_value = mm(normed_all, qkv_full[:, D:]) + jnp.concatenate([jnp.zeros_like(bias_value), bias_value])
    key_all = key_value[:, :D].astype(bf)
    value_all = key_value[:, D:].astype(bf)
    q3 = (query_low * jnp.asarray(0.125, bf)).reshape(4, SP, D)
    k3 = key_all.reshape(16, SP, D)
    v3 = value_all.reshape(16, SP, D)
    o3, lse = attn_fwd(idx, val, q3, k3, v3)
    attended_low = o3.reshape(4 * SP, D)
    branch = mm(attended_low, out_full) + bias_output
    hidden = residual_in + branch
    normed_two, norm_two_back = jax.vjp(layer_norm, hidden, gain_two, shift_two)
    normed_two_low = normed_two.astype(bf)
    inner = mm(normed_two_low, up_full) + bias_up
    active, gelu_back = jax.vjp(exact_gelu, inner)
    active_low = active.astype(bf)
    mlp_out = mm(active_low, down_full) + bias_down
    block_out = (hidden + mlp_out).astype(bf)
    grad_out_low = pad(cotangent)
    grad_out = grad_out_low.astype(f32)
    TN = (((0,), (0,)), ((), ()))
    down_grad = mm(active_low, grad_out_low, TN)
    bias_down_grad = jnp.sum(grad_out, axis=0)
    (inner_grad,) = gelu_back(mm(grad_out_low, down_full, NT))
    inner_grad_low = inner_grad.astype(bf)
    up_grad = mm(normed_two_low, inner_grad_low, TN)
    bias_up_grad = jnp.sum(inner_grad_low.astype(f32), axis=0)
    hidden_from_norm, gain_two_grad, shift_two_grad = norm_two_back(mm(inner_grad_low, up_full, NT))
    hidden_grad = grad_out + hidden_from_norm
    branch_grad_low = hidden_grad.astype(bf)
    out_grad = mm(attended_low, branch_grad_low, TN)
    bias_output_grad = jnp.sum(branch_grad_low.astype(f32), axis=0)
    attended_grad_low = mm(branch_grad_low, out_full, NT).astype(bf)
    dq3, dk3, dv3 = attn_bwd(idx, val, q3, k3, v3, o3, attended_grad_low.reshape(4, SP, D), lse)
    dq = dq3.reshape(4 * SP, D)
    dk = dk3.reshape(16 * SP, D).astype(bf)
    dv = dv3.reshape(16 * SP, D).astype(bf)
    bias_query_grad = jnp.sum(dq.astype(f32), axis=0)
    bias_value_grad = jnp.sum(dv3, axis=(0, 1))
    qkv_grad = jnp.concatenate([mm(normed_low, dq, TN), mm(normed_all, dk, TN), mm(normed_all, dv, TN)], axis=1)
    part = (mm(dk, qkv_full[:, D : 2 * D], NT) + mm(dv, qkv_full[:, 2 * D :], NT)).astype(bf)
    normed_grad = lax.psum_scatter(part, "frames", scatter_dimension=0, tiled=True).astype(f32)
    normed_grad = normed_grad + mm(dq, qkv_full[:, :D], NT)
    input_from_norm, gain_one_grad, shift_one_grad = norm_one_back(normed_grad)
    token_grad = hidden_grad + input_from_norm
    vector_grad = jnp.concatenate([gain_one_grad, shift_one_grad, bias_query_grad, bias_value_grad,
        bias_output_grad, gain_two_grad, shift_two_grad, bias_down_grad, bias_up_grad])
    scatter = lambda g: lax.psum_scatter(g.astype(bf), "frames", scatter_dimension=0, tiled=True)
    vec_sum = lax.psum(lax.psum_scatter(vector_grad, "frames", scatter_dimension=0, tiled=True), "items")
    sums = [lax.psum(scatter(g), "items").astype(f32) for g in (down_grad, up_grad, out_grad, qkv_grad)]
    qkv_new = adamw(qkv_weight, qkv_first, qkv_second, sums[3], 0.05, 0.05)
    out_new = adamw(out_weight, out_first, out_second, sums[2], 0.5, 0.05)
    up_new = adamw(up_weight, up_first, up_second, sums[1], 0.05, 0.05)
    down_new = adamw(down_weight, down_first, down_second, sums[0], 0.03, 0.05)
    vector_new = adamw(vectors, vector_first, vector_second, vec_sum, 0.3, 0.0)
    cut = lambda a: a.reshape(1, 4, SP, D)[:, :, :FRAME_TOK]
    return (cut(block_out), cut(token_grad)) + qkv_new + out_new + up_new + down_new + vector_new


def solution(mesh):
    placed = (
        P("items", "frames", None, None),
        P("items", "frames", None, None),
        P("items", "frames"),
        P("items", "frames"),
        P("items", None),
        P("items", None),
        P("items", None),
        P("frames", None),
        P("frames", None),
        P("frames", None),
        P("frames", None),
        P("frames", None),
        P("frames", None),
        P("frames", None),
        P("frames", None),
        P("frames", None),
        P("frames", None),
        P("frames", None),
        P("frames", None),
        P("frames"),
        P("frames"),
        P("frames"),
    )
    return jax.shard_map(
        on_device,
        mesh=mesh,
        in_specs=placed,
        out_specs=(
            P("items", "frames", None, None),
            P("items", "frames", None, None),
            P("frames", None),
            P("frames", None),
            P("frames", None),
            P("frames", None),
            P("frames", None),
            P("frames", None),
            P("frames", None),
            P("frames", None),
            P("frames", None),
            P("frames", None),
            P("frames", None),
            P("frames", None),
            P("frames"),
            P("frames"),
            P("frames"),
        ),
        check_vma=False,
    )
```

time: 1550 us -> 974 us (0.63)
  matrix products: 402 us -> 143 us
  waiting for transfers between devices: 808 us -> 553 us
  other arithmetic: 166 us -> 69.4 us
  Pallas kernels: 0 us -> 88.3 us
  local copies, waits for them, and re-layouts: 98.9 us -> 47.2 us
    reduce_scatter x4 -> x5, waiting for transfers between devices: 475 us -> 274 us  [the longest x4 180 us: on_device(): lax.psum_scatter(g.astype(bf), 'frames', scatter_dimension=0, tiled=True)]
    dot_general x27 -> x17, matrix products: 342 us -> 143 us  [mm(): return lax.dot_general(a, b, dims, preferred_element_type=jnp.float32)]
    convert_element_type x11 -> x12, other arithmetic: 121 us -> 30.9 us  [the longest x1 11.9 us: on_device(): active_low = active.astype(bf)]
    pallas_call x0 -> x2, Pallas kernels: none -> 88.3 us  [the longest x1 57.3 us: attn_bwd(): pl.pallas_call(attn_bwd_kernel, out_shape=(jax.ShapeDtypeStruct((4, SP, D...]
    sub x3 -> x0, matrix products: 60.6 us -> none  [on_device(): weights = jnp.exp(scores - row_max)]
    psum x1, waiting for transfers between devices: 62.4 us -> 13.1 us  [on_device(): lax.psum(scatter(g), 'items').astype(f32)]
    slice x17 -> x3, local copies, waits for them, and re-layouts: 35.2 us -> 8.82 us  [the longest x1 8.54 us: on_device(): value_all = key_value[:, D:].astype(bf)]
    unnamed x234 -> x158, local copies, waits for them, and re-layouts: 46 us -> 31.8 us
  transfers between devices with their start and end apart: 13 -> 11, of which waited for: 10 -> 9; matrix products, arithmetic and copies ran while one was open for 29% -> 20% of each run, Pallas kernels for 0% -> 9%
where the time goes in v1:
time: 974 us; the launch traced here: 965 us
  waiting for transfers between devices  553 us (57%)
  matrix products  143 us (15%)
  Pallas kernels  88.3 us (9%)
  other arithmetic  69.4 us (7%)
  blocking collectives  47.5 us (5%)
  local copies, waits for them, and re-layouts  47.2 us (5%)
  between operations  15.5 us (2%)
    reduce_scatter x4, waiting for transfers between devices, on_device(): lax.psum_scatter(g.astype(bf), 'frames', scatter_dimension=0, tiled=True)  180 us
    all_gather x4, waiting for transfers between devices, on_device(): lax.all_gather(w.astype(bf), 'frames', axis=0, tiled=True)  173 us
    dot_general x17, matrix products, mm(): return lax.dot_general(a, b, dims, preferred_element_type=jnp.float32)  143 us
    reduce_scatter x1, waiting for transfers between devices, on_device(): lax.psum_scatter(part, 'frames', scatter_dimension=0, tiled=True)  94.3 us
    all_gather x1, waiting for transfers between devices, on_device(): normed_all = lax.all_gather(normed_low, 'frames', axis=0, tiled=True)  92.5 us
    pallas_call x1, Pallas kernels, attn_bwd(): pl.pallas_call(attn_bwd_kernel, out_shape=(jax.ShapeDtypeStruct((4, SP, D...  57.3 us
    unnamed x158, local copies, waits for them, and re-layouts  31.8 us
    pallas_call x1, Pallas kernels, attn_fwd(): pl.pallas_call(attn_fwd_kernel, out_shape=(jax.ShapeDtypeStruct((4, SP, D...  31 us
  transfers between devices with their start and end apart: 11, of which 9 were waited for; matrix products, arithmetic and copies ran while one was open for 20% of the time, Pallas kernels for 9%

profile of v1, /device:TPU:13, one launch (start us, length us, event | category | flops | bytes accessed | tf_op | source)
XLA Modules:
  0.0 965.2 jit_solution(17728639425464041319)
XLA Ops:
  7.3 2.5 convert_element_type.185
  9.9 10.5 %all-gather = bf16[4,1,2304]{2,1,0:T(2,128)(2,1)S(1)} all-gather(bf16[1,1,2304]{2,1,0:T(2,128)(2,1)S(1)} %reshape.336), channel_id=1, replica_groups=mesh['items'=8,'frames'=4] {'frames'}, dimensions={0}, use_global_device_ids=true | all-gather | bytes 23040 | tf_op jit(solution)/shard_map/all_gather | solution.py:267
  22.9 3.0 fusion.48
  29.8 3.3 add_convert_fusion.7
  34.0 2.8 convert_element_type.189
  36.9 2.8 convert_element_type.191
  42.2 2.4 copy.112
  44.8 2.1 add_convert_fusion.3
  48.1 30.9 %all-gather.7.cloned.1.call-done = bf16[768,2304]{1,0:T(8,128)(2,1)} async-done(((bf16[192,2304]{1,0:T(8,128)(2,1)}), bf16[768,2304]{1,0:T(8,128)(2,1)}) %all-gather.7.cloned.1.call-update) | async-done | bytes 3538960 | tf_op jit(solution)/shard_map/all_gather | solution.py:267
  79.0 3.9 fusion.15
  82.9 92.5 %all-gather.9.cloned.1.call-done = bf16[3328,768]{1,0:T(8,128)(2,1)} async-done(((bf16[832,768]{1,0:T(8,128)(2,1)}), bf16[3328,768]{1,0:T(8,128)(2,1)}) %all-gather.9.cloned.1.call-update) | async-done | bytes 5111824 | tf_op jit(solution)/shard_map/all_gather | solution.py:280
  175.4 13.5 %add_convert_fusion = bf16[3328,1536]{1,0:T(8,128)(2,1)} fusion(bf16[3328,768]{1,0:T(8,128)(2,1)} %all-gather.9.cloned.1.call-done, f32[1536]{0:T(1024)S(1)} %concatenate.22, bf16[768,2304]{1,0:T(8,128)(2,1)} %all-gather.7.cloned.1.call-done), kind=kOutput, calls=%fused_computation | convolution fusion | flops 7861960704 | bytes 17700864 | tf_op jit(solution)/shard_map/dot_general | solution.py:86
  189.0 8.5 fusion.51
  197.5 31.0 %attn_fwd.1 = (bf16[4,208,768]{2,1,0:T(8,128)(2,1)}, f32[4,6,8,208]{3,2,1,0:T(8,128)}) custom-call(s32[24]{0:T(128)} %reshape.325.idx_ref, s32[24]{0:T(128)} %reshape.335.val_ref, bf16[4,208,768]{2,1,0:T(8,128)(2,1)} %bitcast.95, bf16[16,208,768]{2,1,0:T(8,128)(2,1)} %bitcast.79, bf16[16,208,768]{2,1,0:T(8,128)(2,1)} %bitcast.77), custom_call_target="tpu_custom_call" | custom-call | flops 12759072768 | bytes 14680064 | tf_op jit(solution)/shard_map/attn_fwd/pallas_call | solution.py:182
  228.5 2.9 fusion.53
  233.4 63.6 %all-gather.13.cloned.1.call-done = bf16[768,3072]{1,0:T(8,128)(2,1)} async-done(((bf16[192,3072]{1,0:T(8,128)(2,1)}), bf16[768,3072]{1,0:T(8,128)(2,1)}) %all-gather.13.cloned.1.call-update) | async-done | bytes 4718608 | tf_op jit(solution)/shard_map/all_gather | solution.py:267
  297.1 11.5 %fusion.35 = f32[832,3072]{1,0:T(8,128)} fusion(bf16[768,3072]{1,0:T(8,128)(2,1)} %all-gather.13.cloned.1.call-done, f32[832,768]{1,0:T(8,128)} %copy-done.6, f32[768]{0:T(1024)S(1)} %get-tuple-element.136, f32[768]{0:T(1024)S(1)} %get-tuple-element.137, f32[832]{0:T(1024)S(1)} %fusion.26, f32[832]{0:T(1024)S(1)} %broadcast_multiply_fusion.1), kind=kOutput, calls=%fused_computation.140 | convolution fusion | flops 3929063424 | bytes 17510912 | tf_op jit(solution)/shard_map/dot_general | solution.py:86
  308.6 78.4 %all-gather.15.cloned.1.call-done = bf16[3072,768]{1,0:T(8,128)(2,1)} async-done(((bf16[768,768]{1,0:T(8,128)(2,1)}), bf16[3072,768]{1,0:T(8,128)(2,1)}) %all-gather.15.cloned.1.call-update) | async-done | bytes 4718608 | tf_op jit(solution)/shard_map/all_gather | solution.py:267
  387.0 32.6 %convert_reduce_fusion = (f32[3072]{0:T(1024)}, bf16[832,3072]{1,0:T(8,128)(2,1)S(1)}, f32[832,3072]{1,0:T(8,128)}) fusion(f32[832,3072]{1,0:T(8,128)} %fusion.35, f32[3072]{0:T(1024)S(1)} %slice.82, bf16[832,768]{1,0:T(8,128)(2,1)S(1)} %bitcast.72, bf16[3072,768]{1,0:T(8,128)(2,1)} %all-gather.15.cloned.1.call-done), kind=kOutput, calls=%fused_computation.3 | convolution fusion | flops 4117558272 | bytes 31580160 | tf_op jit(solution)/shard_map/dot_general | solution.py:86
  419.5 5.2 multiply_reduce_fusion
  428.0 2.5 convolution_convert_fusion.3
  430.5 2.2 convolution_convert_fusion.2
  432.7 57.3 %attn_bwd.1 = (bf16[4,208,768]{2,1,0:T(8,128)(2,1)}, f32[16,208,768]{2,1,0:T(8,128)}, f32[16,208,768]{2,1,0:T(8,128)}) custom-call(s32[24]{0:T(128)} %reshape.325.idx_ref, s32[24]{0:T(128)} %reshape.335.val_ref, bf16[4,208,768]{2,1,0:T(8,128)(2,1)} %bitcast.96, bf16[16,208,768]{2,1,0:T(8,128)(2,1)} %bitcast.80, bf16[16,208,768]{2,1,0:T(8,128)(2,1)} %bitcast.78, ...), custom_call_target="tpu_custom_call" | custom-call | flops 31897681920 | bytes 41943040 | tf_op jit(solution)/shard_map/attn_bwd/pallas_call | solution.py:201
  490.1 4.6 convert_element_type.197
  494.7 10.5 %convolution_convert_fusion.5 = bf16[768,768]{0,1:T(8,128)(2,1)} fusion(bf16[3328,768]{1,0:T(8,128)(2,1)} %all-gather.9.cloned.1.call-done, bf16[3328,768]{1,0:T(8,128)(2,1)S(1)} %bitcast.83), kind=kOutput, calls=%fused_computation.67 | convolution fusion | flops 3926458368 | bytes 11403264 | tf_op jit(solution)/shard_map/dot_general | solution.py:86
  506.8 5.0 bitcast_convert_fusion
  511.8 6.9 convolution_convert_fusion.4
  519.1 4.2 copy.105
  525.0 9.6 convolution_convert_fusion.1
  534.7 11.9 %multiply_convert_fusion = bf16[832,3072]{1,0:T(8,128)(2,1)} fusion(f32[832,3072]{1,0:T(8,128)} %get-tuple-element.110, f32[832,3072]{1,0:T(8,128)} %fusion.35, f32[3072]{0:T(1024)S(1)} %slice.82), kind=kLoop, calls=%fused_computation.6 | loop fusion | flops 10223616 | bytes 25571328 | tf_op jit(solution)/shard_map/convert_element_type | solution.py:296
  546.6 9.5 convolution_convert_fusion
  558.2 6.3 fusion.18
  564.5 8.7 add_convert_fusion.1
  577.1 8.0 add_convert_fusion.4
  586.9 3.9 reduce-scatter.16.cloned.1.call-done
  590.8 88.1 %reduce-scatter.12.cloned.1.call-done = bf16[192,3072]{1,0:T(8,128)(2,1)} async-done(((bf16[768,3072]{1,0:T(8,128)(2,1)}), bf16[192,3072]{1,0:T(8,128)(2,1)}) %reduce-scatter.12.cloned.1.call-update) | async-done | bytes 1179664 | tf_op jit(solution)/shard_map/reduce_scatter | solution.py:328
  678.9 88.1 %reduce-scatter.14.cloned.1.call-done = bf16[768,768]{1,0:T(8,128)(2,1)} async-done(((bf16[3072,768]{1,0:T(8,128)(2,1)}), bf16[768,768]{1,0:T(8,128)(2,1)}) %reduce-scatter.14.cloned.1.call-update) | async-done | bytes 1179664 | tf_op jit(solution)/shard_map/reduce_scatter | solution.py:328
  767.1 94.3 %reduce-scatter.8.cloned.1.call-done = bf16[832,768]{1,0:T(8,128)(2,1)} async-done(((bf16[3328,768]{1,0:T(8,128)(2,1)}), bf16[832,768]{1,0:T(8,128)(2,1)}) %reduce-scatter.8.cloned.1.call-update) | async-done | bytes 1277968 | tf_op jit(solution)/shard_map/reduce_scatter | solution.py:322
  861.4 4.4 multiply_reduce_fusion.1
  870.4 3.2 add_add_fusion.2
  873.9 2.4 copy.108
  887.4 13.8 %all-reduce.4 = f32[9216]{0:T(1024)} all-reduce(f32[9216]{0:T(1024)} %constant_dynamic-update-slice_fusion), channel_id=7, replica_groups=mesh['items'=8,'frames'=4] {'frames'}, use_global_device_ids=true, to_apply=%region_32.33.clone | all-reduce | flops 9216 | bytes 73728
  902.0 23.3 %psum.39 = f32[2304]{0:T(1024)} all-reduce(f32[2304]{0:T(1024)S(1)} %dynamic-slice.1), channel_id=1, replica_groups=mesh['items'=8,'frames'=4] {'items'}, use_global_device_ids=true, to_apply=%region_33.34 | all-reduce | flops 2304 | bytes 18432 | tf_op jit(solution)/shard_map/psum | solution.py:329
  926.7 13.1 %all-reduce.8.cloned.1.call-done = (bf16[192,2304]{1,0:T(8,128)(2,1)}, bf16[192,768]{1,0:T(8,128)(2,1)}, bf16[192,3072]{1,0:T(8,128)(2,1)}, bf16[768,768]{1,0:T(8,128)(2,1)}) async-done(((bf16[192,2304]{1,0:T(8,128)(2,1)}, bf16[192,768]{1,0:T(8,128)(2,1)}, bf16[192,3072]{1,0:T(8,128)(2,1)}, bf16[768,768]{1,0:T(8,128)(2,1)}), (bf16[192,2304]{1,0:T(8,128)(2,1)}, bf16[192,768]{1,0:T(8,128)(2,1)}, ...) | async-done | bytes 3538960 | tf_op jit(solution)/shard_map/psum | solution.py:330
  939.8 2.6 multiply_subtract_fusion.3
  942.4 5.1 multiply_subtract_fusion.2
  948.4 4.4 multiply_subtract_fusion.1
  954.3 4.1 multiply_subtract_fusion
  (241 shorter events, 47.8 us)
Async XLA Ops:
  7.2 13.2 %copy-start.57 = (s32[1,4]{1,0:T(1,128)S(1)}, s32[1,4]{1,0:T(1,128)}, u32[]{:S(2)}) copy-start(s32[1,4]{1,0:T(1,128)} %param.25) | copy-start | bytes 52
  7.2 13.2 %copy-start.58 = (s32[1,4]{1,0:T(1,128)S(1)}, s32[1,4]{1,0:T(1,128)}, u32[]{:S(2)}) copy-start(s32[1,4]{1,0:T(1,128)} %param.24) | copy-start | bytes 52
  7.2 71.8 %all-gather.7.cloned.1.call-start = ((), (), s32[]{:S(2)}) async-start(), calls=%async_computation.5 | async-start | bytes 4423680 | tf_op jit(solution)/shard_map/all_gather | solution.py:267
  9.8 165.7 %all-gather.9.cloned.1.call-start = ((), (), s32[]{:S(2)}) async-start(), calls=%async_computation.6 | async-start | bytes 6389760 | tf_op jit(solution)/shard_map/all_gather | solution.py:280
  29.8 15.1 %copy-start.30 = (f32[768]{0:T(1024)}, f32[768]{0:T(1024)S(1)}, u32[]{:S(2)}) copy-start(f32[768]{0:T(1024)S(1)} %get-tuple-element.142) | copy-start | bytes 9220
  29.8 267.3 %copy-start.51 = (f32[768]{0:T(1024)}, f32[768]{0:T(1024)S(1)}, u32[]{:S(2)}) copy-start(f32[768]{0:T(1024)S(1)} %get-tuple-element.136) | copy-start | bytes 9220
  29.8 394.9 %copy-start.43 = (f32[768]{0:T(1024)}, f32[768]{0:T(1024)S(1)}, u32[]{:S(2)}) copy-start(f32[768]{0:T(1024)S(1)} %get-tuple-element.137) | copy-start | bytes 9220
  33.1 195.4 %all-gather.11.cloned.1.call-start = ((), (), s32[]{:S(2)}) async-start(), calls=%async_computation.7 | async-start | bytes 1474560 | tf_op jit(solution)/shard_map/all_gather | solution.py:267
  33.9 263.1 %all-gather.13.cloned.1.call-start = ((), (), s32[]{:S(2)}) async-start(), calls=%async_computation.8 | async-start | bytes 5898240 | tf_op jit(solution)/shard_map/all_gather | solution.py:267
  36.9 350.1 %all-gather.15.cloned.1.call-start = ((), (), s32[]{:S(2)}) async-start(), calls=%async_computation.9 | async-start | bytes 5898240 | tf_op jit(solution)/shard_map/all_gather | solution.py:267
  39.8 547.2 %reduce-scatter.10.cloned.1.call-start = ((), (), s32[]{:S(2)}) async-start(), calls=%async_computation.11 | async-start | bytes 1474560 | tf_op jit(solution)/shard_map/reduce_scatter | solution.py:328
  197.5 31.0 %copy-start.2 = (f32[4,208,768]{2,1,0:T(8,128)S(1)}, f32[4,208,768]{2,1,0:T(8,128)}, u32[]{:S(2)}) copy-start(f32[4,208,768]{2,1,0:T(8,128)} %copy.94) | copy-start | bytes 7667716
  231.4 193.3 %copy-start.33 = (f32[832]{0:T(1024)}, f32[832]{0:T(1024)S(1)}, u32[]{:S(2)}) copy-start(f32[832]{0:T(1024)S(1)} %broadcast_multiply_fusion.1) | copy-start | bytes 9988
  233.4 75.2 %copy-start.35 = (f32[832]{0:T(1024)}, f32[832]{0:T(1024)S(1)}, u32[]{:S(2)}) copy-start(f32[832]{0:T(1024)S(1)} %multiply_reduce_fusion.4) | copy-start | bytes 9988
  233.4 191.3 %copy-start.45 = (f32[832]{0:T(1024)}, f32[832]{0:T(1024)S(1)}, u32[]{:S(2)}) copy-start(f32[832]{0:T(1024)S(1)} %fusion.26) | copy-start | bytes 9988
  297.1 89.9 %copy-start.4 = (bf16[4,208,768]{2,1,0:T(8,128)(2,1)S(1)}, bf16[4,208,768]{2,1,0:T(8,128)(2,1)}, u32[]{:S(2)}) copy-start(bf16[4,208,768]{2,1,0:T(8,128)(2,1)} %pad.14.clone) | copy-start | bytes 3833860
  387.0 32.6 %copy-start.7 = (f32[832,768]{1,0:T(8,128)S(1)}, f32[832,768]{1,0:T(8,128)}, u32[]{:S(2)}) copy-start(f32[832,768]{1,0:T(8,128)} %copy-done.6) | copy-start | bytes 7667716
  387.0 32.6 %copy-start.59 = (bf16[768,3072]{1,0:T(8,128)(2,1)S(1)}, bf16[768,3072]{1,0:T(8,128)(2,1)}, u32[]{:S(2)}) copy-start(bf16[768,3072]{1,0:T(8,128)(2,1)} %all-gather.13.cloned.1.call-done) | copy-start | bytes 14155780
  419.5 5.2 copy-start.67
  419.5 5.2 copy-start.36
  430.5 160.4 %reduce-scatter.16.cloned.1.call-start = ((), (), s32[]{:S(2)}) async-start(), calls=%async_computation.14 | async-start | bytes 4423680 | tf_op jit(solution)/shard_map/reduce_scatter | solution.py:328
  490.1 15.0 %slice-start = ((s8[10223616]{0:T(1024)(128)(4,1)}), s8[4194304]{0:T(1024)(128)(4,1)S(1)}, s32[]{:S(2)}) async-start(s8[10223616]{0:T(1024)(128)(4,1)} %bitcast.74), calls=%async_computation.16 | async-start | bytes 8388608
  490.1 15.0 %slice-start.1 = ((s8[10223616]{0:T(1024)(128)(4,1)}), s8[4194304]{0:T(1024)(128)(4,1)S(1)}, s32[]{:S(2)}) async-start(s8[10223616]{0:T(1024)(128)(4,1)} %bitcast.74), calls=%async_computation.17 | async-start | bytes 8388608
  494.7 10.5 %copy-start.14 = (bf16[16,208,768]{2,1,0:T(8,128)(2,1)}, bf16[16,208,768]{2,1,0:T(8,128)(2,1)S(1)}, u32[]{:S(2)}) copy-start(bf16[16,208,768]{2,1,0:T(8,128)(2,1)S(1)} %convert_element_type.197) | copy-start | bytes 15335428
  494.7 10.5 %slice-start.2 = ((s8[10223616]{0:T(1024)(128)(4,1)}), s8[1835008]{0:T(1024)(128)(4,1)S(1)}, s32[]{:S(2)}) async-start(s8[10223616]{0:T(1024)(128)(4,1)} %bitcast.74), calls=%async_computation.18 | async-start | bytes 3670016
  511.8 6.9 copy-start.25
  523.3 155.6 %reduce-scatter.12.cloned.1.call-start = ((), (), s32[]{:S(2)}) async-start(), calls=%async_computation.12 | async-start | bytes 5898240 | tf_op jit(solution)/shard_map/reduce_scatter | solution.py:328
  534.6 232.4 %reduce-scatter.14.cloned.1.call-start = ((), (), s32[]{:S(2)}) async-start(), calls=%async_computation.13 | async-start | bytes 5898240 | tf_op jit(solution)/shard_map/reduce_scatter | solution.py:328
  534.7 11.9 %copy-start.5 = (bf16[4,208,768]{2,1,0:T(8,128)(2,1)S(1)}, bf16[4,208,768]{2,1,0:T(8,128)(2,1)}, u32[]{:S(2)}) copy-start(bf16[4,208,768]{2,1,0:T(8,128)(2,1)} %pad.14.clone) | copy-start | bytes 3833860
  556.2 305.2 %reduce-scatter.8.cloned.1.call-start = ((), (), s32[]{:S(2)}) async-start(), calls=%async_computation.10 | async-start | bytes 6389760 | tf_op jit(solution)/shard_map/reduce_scatter | solution.py:322
  573.2 366.6 %all-reduce.8.cloned.1.call-start = ((), (), s32[]{:S(2)}) async-start(), calls=%async_computation.15 | async-start | bytes 7077888 | tf_op jit(solution)/shard_map/psum | solution.py:330
  586.6 274.7 %copy-start.3 = (f32[4,208,768]{2,1,0:T(8,128)S(1)}, f32[4,208,768]{2,1,0:T(8,128)}, u32[]{:S(2)}) copy-start(f32[4,208,768]{2,1,0:T(8,128)} %copy.94) | copy-start | bytes 7667716
  586.6 274.7 %copy-start.31 = (f32[768]{0:T(1024)S(1)}, f32[768]{0:T(1024)}, u32[]{:S(2)}) copy-start(f32[768]{0:T(1024)} %copy-done.30) | copy-start | bytes 9220
  586.7 274.7 %copy-start.40 = (f32[832]{0:T(1024)S(1)}, f32[832]{0:T(1024)}, u32[]{:S(2)}) copy-start(f32[832]{0:T(1024)} %copy-done.39) | copy-start | bytes 9988
  586.7 274.7 %copy-start.42 = (f32[832]{0:T(1024)S(1)}, f32[832]{0:T(1024)}, u32[]{:S(2)}) copy-start(f32[832]{0:T(1024)} %copy-done.41) | copy-start | bytes 9988
  873.8 6.5 copy-start.48
  873.8 7.8 copy-start.47
  873.8 9.1 copy-start.54
  873.9 10.4 %copy-start.53 = (f32[768]{0:T(1024)S(1)}, f32[768]{0:T(1024)}, u32[]{:S(2)}) copy-start(f32[768]{0:T(1024)} %get-tuple-element.99) | copy-start | bytes 9220
  873.9 12.9 %copy-start.49 = (f32[3072]{0:T(1024)S(1)}, f32[3072]{0:T(1024)}, u32[]{:S(2)}) copy-start(f32[3072]{0:T(1024)} %get-tuple-element.108) | copy-start | bytes 36868
  873.9 65.9 %copy-start.17 = (f32[192,768]{1,0:T(8,128)S(1)}, f32[192,768]{1,0:T(8,128)}, u32[]{:S(2)}) copy-start(f32[192,768]{1,0:T(8,128)} %param.32) | copy-start | bytes 1769476
  873.9 65.9 %copy-start.28 = (f32[192,768]{1,0:T(8,128)S(1)}, f32[192,768]{1,0:T(8,128)}, u32[]{:S(2)}) copy-start(f32[192,768]{1,0:T(8,128)} %param.34) | copy-start | bytes 1769476
  873.9 65.9 %copy-start.29 = (f32[192,768]{1,0:T(8,128)S(1)}, f32[192,768]{1,0:T(8,128)}, u32[]{:S(2)}) copy-start(f32[192,768]{1,0:T(8,128)} %param.33) | copy-start | bytes 1769476
  876.3 66.1 %copy-start.12 = (f32[192,2304]{1,0:T(8,128)S(1)}, f32[192,2304]{1,0:T(8,128)}, u32[]{:S(2)}) copy-start(f32[192,2304]{1,0:T(8,128)} %param.29) | copy-start | bytes 5308420
  942.4 5.2 copy-start.10
  942.4 6.0 copy-start.27
  948.4 5.6 copy-start.21
  948.4 5.9 copy-start.26
  (34 other events, 93.3 us)
Sparse Core Ops, SparseCore 0:
  10.2 68.7 all-gather.6
  81.1 94.2 all-gather.8
  177.6 30.6 all-gather.10
  210.3 86.7 all-gather.12
  299.1 87.8 all-gather.14
  430.6 28.1 reduce-scatter.9
  523.4 67.3 reduce-scatter.15
  593.1 85.7 reduce-scatter.11
  681.2 85.7 reduce-scatter.13
  769.2 92.1 reduce-scatter.7
  865.1 74.7 all-reduce.7

commit v2 on v1

--- a/solution.py
+++ b/solution.py
@@ -1,5 +1,8 @@
+import functools
+
 import jax
 import jax.numpy as jnp
+import numpy as np
 from jax import lax
 from jax.experimental import pallas as pl
 from jax.experimental.pallas import tpu as pltpu
@@ -24,30 +27,28 @@
     return jnp.concatenate([jnp.sin(angles), jnp.cos(angles)], axis=-1)
 
 
-def positions(year_values, day_values):
-    cell_index = jnp.arange(FRAME_TOK, dtype=jnp.int32)
-    spatial = jnp.concatenate(
-        [
-            sincos((cell_index // GRID).astype(jnp.float32), 3 * D // 8),
-            sincos((cell_index % GRID).astype(jnp.float32), 3 * D // 8),
-        ],
-        axis=-1,
-    )
-    temporal = jnp.concatenate(
+def temporal_rows(year_values, day_values):
+    dates = jnp.concatenate(
         [
             sincos((year_values - 2000).astype(jnp.float32), D // 8),
             sincos(day_values.astype(jnp.float32), D // 8),
         ],
         axis=-1,
     )
-    slot_count = year_values.shape[0]
-    return jnp.concatenate(
-        [
-            jnp.broadcast_to(spatial[None], (slot_count, FRAME_TOK, 3 * D // 4)),
-            jnp.broadcast_to(temporal[:, None], (slot_count, FRAME_TOK, D // 4)),
-        ],
-        axis=-1,
-    )
+    return jnp.pad(dates, ((0, 0), (3 * D // 4, 0)))
+
+
+def spatial_rows():
+    half = 3 * D // 16
+    frequency = (1.0 / np.float32(10000.0) ** (np.arange(half, dtype=np.float32) / np.float32(half))).astype(np.float32)
+    cells = np.arange(FRAME_TOK)
+    parts = []
+    for values in (cells // GRID, cells % GRID):
+        angles = values.astype(np.float32)[:, None] * frequency
+        parts += [np.sin(angles), np.cos(angles)]
+    rows = np.zeros((SP, D), np.float32)
+    rows[:FRAME_TOK, : 3 * D // 4] = np.concatenate(parts, axis=-1)
+    return rows
 
 
 def slot_items(dates_group, frames_group, mask_group):
@@ -126,7 +127,7 @@
 
 
 def attn_bwd_kernel(
-    idx_ref, val_ref, q_ref, k_ref, v_ref, o_ref, do_ref, lse_ref, dq_ref, dk_ref, dv_ref
+    idx_ref, val_ref, q_ref, k_ref, v_ref, o_ref, do_ref, lse_ref, dq_ref, dk_out, dv_out, dk_ref, dv_ref
 ):
     lane = lax.broadcasted_iota(jnp.int32, (SP, 128), 1)
     row = lax.broadcasted_iota(jnp.int32, (SP, 128), 0)
@@ -173,6 +174,13 @@
 
     lax.fori_loop(0, 24, one, 0)
 
+    def narrow(slot, _):
+        dk_out[slot] = dk_ref[slot].astype(jnp.bfloat16)
+        dv_out[slot] = dv_ref[slot].astype(jnp.bfloat16)
+        return 0
+
+    lax.fori_loop(0, 16, narrow, 0)
+
 
 VM = pl.BlockSpec(memory_space=pltpu.VMEM)
 SM = pl.BlockSpec(memory_space=pltpu.SMEM)
@@ -202,11 +210,12 @@
         attn_bwd_kernel,
         out_shape=(
             jax.ShapeDtypeStruct((4, SP, D), jnp.bfloat16),
-            jax.ShapeDtypeStruct((16, SP, D), jnp.float32),
-            jax.ShapeDtypeStruct((16, SP, D), jnp.float32),
+            jax.ShapeDtypeStruct((16, SP, D), jnp.bfloat16),
+            jax.ShapeDtypeStruct((16, SP, D), jnp.bfloat16),
         ),
         in_specs=[SM, SM] + [VM] * 6,
         out_specs=(VM, VM, VM),
+        scratch_shapes=[pltpu.VMEM((16, SP, D), jnp.float32)] * 2,
         compiler_params=pltpu.CompilerParams(vmem_limit_bytes=62 * 2**20),
         cost_estimate=pl.CostEstimate(
             flops=2 * 5 * 24 * 12 * SP * SP * 256,
@@ -236,6 +245,752 @@
     second_hat = second_new / (1.0 - beta_two**STEP)
     weight_new = weight - step_rate * (first_hat / (jnp.sqrt(second_hat) + 1e-08) + decay * weight)
     return (first_new, second_new, weight_new)
+
+
+VEC_ROWS = 16
+MESH = pl.DeviceIdType.MESH
+Z, X, Y, DA, DB, C0, C1, C2, C3 = range(9)
+
+
+def norm_rows(x):
+    mean = jnp.mean(x, axis=-1, keepdims=True)
+    centred = x - mean
+    spread = jnp.mean(centred * centred, axis=-1, keepdims=True)
+    return centred * lax.rsqrt(spread + 1e-06)
+
+
+def place():
+    i, f = lax.axis_index("items"), lax.axis_index("frames")
+    core = i % 2
+    upper = f // 2
+    stay = core == upper
+    mine = jnp.where(stay, f, 3 - f)
+    other = f + 1 - 2 * (f % 2)
+    far = jnp.where(stay, other, 3 - other)
+    flip = lambda v, bit: v + bit - 2 * bit * ((v // bit) % 2)
+    return i, f, core, stay, mine, other, far, flip
+
+
+def halves(core, a, b):
+    return jnp.where(core == 0, a, b)
+
+
+def front_kernel(
+    tok, tmp, vec, spatial, wq, wo, wu, wd,
+    q_out, k_out, v_out, n_out, x_out, vec_out, tmp_out, wq_out, wo_out, wu_out, wd_out,
+    t_s, tmp_s, vec_s, n_s, q_s, k_s, v_s, x_s, wq_s,
+    rq32, ro32, ru32, rd32, rq, ro, ru, rd, sq32, so32, su32, sd32, sq, so, su, sd,
+    t_send, t_recv, m_send, m_recv, v_send, v_recv, w_send, w_recv, reg_sem, own_sem, put_sem, loc_sem, out_sem,
+):
+    bf, f32 = jnp.bfloat16, jnp.float32
+    i, f, core, stay, mine, other, far, flip = place()
+    c_dev = (flip(i, 1), f)
+    x_dev = (halves(core, flip(i, 2), flip(i, 4)), f)
+    y_dev = (halves(core, flip(i, 4), flip(i, 2)), f)
+    e_dev = (i, other)
+    m_dev = (flip(i, 1), 3 - f)
+    xy = (i // 2) % 4
+    xy_x, xy_y = halves(core, flip(xy, 1), flip(xy, 2)), halves(core, flip(xy, 2), flip(xy, 1))
+    diag = flip(flip(xy, 1), 2)
+    zs = [flip(f, 1), flip(f, 2), flip(flip(f, 1), 2)]
+
+    barrier = pltpu.get_barrier_semaphore()
+    partners = [c_dev, x_dev, y_dev, m_dev] + [(i, z) for z in zs]
+    for dev in partners:
+        pl.semaphore_signal(barrier, inc=1, device_id=dev, device_id_type=MESH)
+
+    weights = [(wq, wq_out, rq32, rq, sq32, sq), (wo, wo_out, ro32, ro, so32, so),
+               (wu, wu_out, ru32, ru, su32, su), (wd, wd_out, rd32, rd, sd32, sd)]
+
+    def region_load(w):
+        src, _, r32, _, _, _ = weights[w]
+        rows, cols = r32.shape
+        return pltpu.make_async_copy(
+            src.at[pl.ds(pl.multiple_of(xy * rows, rows), rows), pl.ds(pl.multiple_of(core * cols, 128), cols)],
+            r32, reg_sem.at[w])
+
+    def own_load(w):
+        return pltpu.make_async_copy(weights[w][0], weights[w][4], own_sem.at[w])
+
+    def own_put(w):
+        out, small = weights[w][1], weights[w][5]
+        rows = small.shape[0]
+        return pltpu.make_async_copy(small, out.at[pl.ds(pl.multiple_of(f * rows, rows), rows), :], put_sem.at[w])
+
+    for w in range(4):
+        region_load(w).start()
+    for w in range(4):
+        own_load(w).start()
+    tok_load = pltpu.make_async_copy(tok, t_s.at[mine], loc_sem.at[0])
+    tmp_load = pltpu.make_async_copy(tmp, tmp_s.at[mine], loc_sem.at[1])
+    vec_load = pltpu.make_async_copy(vec, vec_s.at[f], loc_sem.at[2])
+
+    @pl.when(stay)
+    def _():
+        tok_load.start()
+        tmp_load.start()
+
+    vec_load.start()
+    pl.semaphore_wait(barrier, len(partners))
+
+    def remote(src, dst, ssem, rsem, dev):
+        return pltpu.make_async_remote_copy(
+            src_ref=src, dst_ref=dst, send_sem=ssem, recv_sem=rsem, device_id=dev, device_id_type=MESH)
+
+    def tok_copy(kind, j):
+        if kind == 0:
+            return remote(tok.at[j], t_s.at[f, j], t_send.at[0, j], t_recv.at[0, j], m_dev)
+        if kind == 3:
+            return remote(t_s.at[far, j], t_s.at[far, j], t_send.at[3, j], t_recv.at[3, j], c_dev)
+        return remote(t_s.at[mine, j], t_s.at[mine, j], t_send.at[kind, j], t_recv.at[kind, j],
+                      c_dev if kind == 1 else e_dev)
+
+    def tok_arrival(kind, j):
+        shard = (mine, 3 - mine, far, 3 - far)[kind]
+        return remote(t_s.at[shard, j], t_s.at[shard, j], t_send.at[kind, j], t_recv.at[kind, j], c_dev)
+
+    def tmp_copy(kind):
+        if kind == 0:
+            return remote(tmp, tmp_s.at[f], m_send.at[0], m_recv.at[0], m_dev)
+        if kind == 3:
+            return remote(tmp_s.at[far], tmp_s.at[far], m_send.at[3], m_recv.at[3], c_dev)
+        return remote(tmp_s.at[mine], tmp_s.at[mine], m_send.at[kind], m_recv.at[kind], c_dev if kind == 1 else e_dev)
+
+    def tmp_arrival(kind):
+        shard = (mine, 3 - mine, far, 3 - far)[kind]
+        return remote(tmp_s.at[shard], tmp_s.at[shard], m_send.at[kind], m_recv.at[kind], c_dev)
+
+    def part(w, z, at, half, piece):
+        out, r = weights[w][1], weights[w][3]
+        rows, cols = r.shape
+        unit = rows // 3
+        start = z * 4 * rows + at * rows
+        if piece == 0:
+            return out.at[pl.ds(pl.multiple_of(start, 16), rows), pl.ds(pl.multiple_of(half * cols, 128), cols)]
+        if piece == 1:
+            return out.at[pl.ds(pl.multiple_of(start, 16), 2 * unit), pl.ds(pl.multiple_of(half * cols, 128), cols)]
+        return out.at[pl.ds(pl.multiple_of(start + 2 * unit, 16), unit), pl.ds(pl.multiple_of(half * cols, 128), cols)]
+
+    def w_copy(w, d, kind):
+        sems = (w_send.at[w, d, kind], w_recv.at[w, d, kind])
+        z = zs[d]
+        if kind == Z:
+            return remote(weights[w][3], part(w, f, xy, core, 0), *sems, (i, z))
+        at = {X: xy, Y: xy, DA: xy_x, DB: xy_y, C0: xy, C1: xy_x, C2: xy_y, C3: diag}[kind]
+        piece = {DA: 1, DB: 2}.get(kind, 0)
+        dev = {X: x_dev, Y: y_dev, DA: y_dev, DB: x_dev}.get(kind, c_dev)
+        ref = part(w, z, at, core, piece)
+        return remote(ref, ref, *sems, dev)
+
+    def w_arrival(w, d, kind):
+        sems = (w_send.at[w, d, kind], w_recv.at[w, d, kind])
+        z = zs[d]
+        at = {Z: xy, X: xy_x, Y: xy_y, DA: diag, DB: diag, C0: xy, C1: xy_y, C2: xy_x, C3: diag}[kind]
+        piece = {DA: 1, DB: 2}.get(kind, 0)
+        half = (1 - core) if kind >= C0 else core
+        ref = part(w, z, at, half, piece)
+        return remote(ref, ref, *sems, c_dev)
+
+    def w_send_region(w):
+        region_load(w).wait()
+        weights[w][3][...] = weights[w][2][...].astype(bf)
+        for d in range(3):
+            w_copy(w, d, Z).start()
+
+    def w_stage_one(w):
+        for d in range(3):
+            w_arrival(w, d, Z).wait_recv()
+            for kind in (X, Y, C0):
+                w_copy(w, d, kind).start()
+
+    def w_stage_two(w):
+        for d in range(3):
+            w_arrival(w, d, X).wait_recv()
+            w_copy(w, d, DA).start()
+            w_copy(w, d, C1).start()
+            w_arrival(w, d, Y).wait_recv()
+            w_copy(w, d, DB).start()
+            w_copy(w, d, C2).start()
+
+    def w_stage_three(w):
+        for d in range(3):
+            w_arrival(w, d, DA).wait_recv()
+            w_arrival(w, d, DB).wait_recv()
+            w_copy(w, d, C3).start()
+
+    def w_stage_four(w):
+        for d in range(3):
+            for kind in (C0, C1, C2, C3):
+                w_arrival(w, d, kind).wait_recv()
+
+    def w_own(w):
+        own_load(w).wait()
+        weights[w][5][...] = weights[w][4][...].astype(bf)
+        own_put(w).start()
+
+    w_send_region(0)
+
+    @pl.when(jnp.logical_not(stay))
+    def _():
+        tmp_copy(0).start()
+        for j in range(4):
+            tok_copy(0, j).start()
+
+    @pl.when(stay)
+    def _():
+        tok_load.wait()
+        tmp_load.wait()
+        for kind in (2, 1):
+            tmp_copy(kind).start()
+            for j in range(4):
+                tok_copy(kind, j).start()
+
+    vec_load.wait()
+    def v_copy(d):
+        return remote(vec_s.at[f], vec_s.at[f], v_send.at[d], v_recv.at[d], (i, zs[d]))
+    def v_arrival(d):
+        return remote(vec_s.at[zs[d]], vec_s.at[zs[d]], v_send.at[d], v_recv.at[d], (i, zs[d]))
+    for d in range(3):
+        v_copy(d).start()
+    for w in range(4):
+        w_own(w)
+    w_stage_one(0)
+    w_stage_two(0)
+    w_stage_three(0)
+
+    @pl.when(jnp.logical_not(stay))
+    def _():
+        tmp_arrival(0).wait_recv()
+        for kind in (2, 1):
+            tmp_copy(kind).start()
+        for j in range(4):
+            tok_arrival(0, j).wait_recv()
+            for kind in (2, 1):
+                tok_copy(kind, j).start()
+
+    for w in (1, 2, 3):
+        w_send_region(w)
+    w_stage_four(0)
+    own_put(0).wait()
+    wq_load = pltpu.make_async_copy(wq_out, wq_s, loc_sem.at[3])
+    wq_load.start()
+    for d in range(3):
+        v_arrival(d).wait_recv()
+    vec_put = pltpu.make_async_copy(vec_s, vec_out, loc_sem.at[4])
+    vec_put.start()
+    tmp_put = pltpu.make_async_copy(tmp_s.at[mine], tmp_out, loc_sem.at[5])
+    tmp_put.start()
+    gain = vec_s[0, 0:1, :].astype(f32)
+    shift = vec_s[0, 1:2, :].astype(f32)
+    bias_q = vec_s[0, 2:3, :].astype(f32)
+    bias_v = vec_s[1, 0:1, :].astype(f32)
+    wq_load.wait()
+
+    def normalise(shard, keep_x):
+        def slot(j, _):
+            x = t_s[shard, j].astype(f32) + (spatial[...] + tmp_s[shard, pl.ds(j, 1), :])
+            if keep_x:
+                x_s[j] = x
+            n_s[shard, j] = (norm_rows(x) * gain + shift).astype(bf)
+            return 0
+        lax.fori_loop(0, 4, slot, 0)
+
+    def project(shard):
+        rows = n_s[shard].reshape(4 * SP, D)
+        def keys(t, _):
+            cols = pl.ds(pl.multiple_of(t * 256, 256), 256)
+            k_s[shard, :, :, cols] = mm(rows, wq_s[:, pl.ds(pl.multiple_of(D + t * 256, 256), 256)]).astype(bf).reshape(4, SP, 256)
+            v_s[shard, :, :, cols] = (mm(rows, wq_s[:, pl.ds(pl.multiple_of(2 * D + t * 256, 256), 256)])
+                                      + vec_s[1, 0:1, cols].astype(f32)).astype(bf).reshape(4, SP, 256)
+            return 0
+        lax.fori_loop(0, 3, keys, 0)
+
+    def project_q(shard):
+        rows = n_s[shard].reshape(4 * SP, D)
+        def queries(t, _):
+            cols = pl.ds(pl.multiple_of(t * 256, 256), 256)
+            q = (mm(rows, wq_s[:, cols]) + vec_s[0, 2:3, cols].astype(f32)).astype(bf)
+            q_s[:, :, cols] = (q.astype(f32) * 0.125).astype(bf).reshape(4, SP, 256)
+            return 0
+        lax.fori_loop(0, 3, queries, 0)
+
+    outs = []
+    def put(src, dst):
+        copy = pltpu.make_async_copy(src, dst, out_sem.at[len(outs)])
+        copy.start()
+        outs.append(copy)
+
+    def put_shard(shard):
+        put(n_s.at[shard], n_out.at[shard])
+        put(k_s.at[shard], k_out.at[shard])
+        put(v_s.at[shard], v_out.at[shard])
+
+    normalise(mine, True)
+    put(x_s, x_out)
+    project_q(mine)
+    put(q_s, q_out)
+    project(mine)
+    put_shard(mine)
+    w_stage_one(1)
+    tmp_arrival(1).wait_recv()
+    for j in range(4):
+        tok_arrival(1, j).wait_recv()
+    normalise(3 - mine, False)
+    project(3 - mine)
+    put_shard(3 - mine)
+    tmp_arrival(2).wait_recv()
+    tmp_copy(3).start()
+    for j in range(4):
+        tok_arrival(2, j).wait_recv()
+        tok_copy(3, j).start()
+    w_stage_two(1)
+    w_stage_one(2)
+    normalise(far, False)
+    project(far)
+    put_shard(far)
+    w_stage_one(3)
+    tmp_arrival(3).wait_recv()
+    for j in range(4):
+        tok_arrival(3, j).wait_recv()
+    normalise(3 - far, False)
+    project(3 - far)
+    put_shard(3 - far)
+    w_stage_two(2)
+    w_stage_two(3)
+    for w in (1, 2, 3):
+        w_stage_three(w)
+    for w in (1, 2, 3):
+        w_stage_four(w)
+        own_put(w).wait()
+
+    @pl.when(jnp.logical_not(stay))
+    def _():
+        tmp_copy(0).wait_send()
+        for j in range(4):
+            tok_copy(0, j).wait_send()
+
+    for kind in (1, 2, 3):
+        tmp_copy(kind).wait_send()
+        for j in range(4):
+            tok_copy(kind, j).wait_send()
+    for d in range(3):
+        v_copy(d).wait_send()
+        for w in range(4):
+            for kind in range(9):
+                w_copy(w, d, kind).wait_send()
+    vec_put.wait()
+    tmp_put.wait()
+    for copy in outs:
+        copy.wait()
+
+
+def front(tok, tmp, vec, spatial, wq, wo, wu, wd):
+    bf, f32 = jnp.bfloat16, jnp.float32
+    S = jax.ShapeDtypeStruct
+    hb = pl.BlockSpec(memory_space=pltpu.HBM)
+    regs = [(w.shape[0] // 4, w.shape[1] // 2) for w in (wq, wo, wu, wd)]
+    full = [(4 * w.shape[0], w.shape[1]) for w in (wq, wo, wu, wd)]
+    dma = pltpu.SemaphoreType.DMA
+    return pl.pallas_call(
+        front_kernel,
+        out_shape=(
+            S((4, SP, D), bf), S((4, 4, SP, D), bf), S((4, 4, SP, D), bf), S((4, 4, SP, D), bf), S((4, SP, D), f32),
+            S((4, VEC_ROWS, D), bf), S((8, D), f32),
+        ) + tuple(S(s, bf) for s in full),
+        in_specs=[hb, hb, hb, VM, hb, hb, hb, hb],
+        out_specs=(hb,) * 11,
+        scratch_shapes=[
+            pltpu.VMEM((4, 4, SP, D), bf), pltpu.VMEM((4, 8, D), f32), pltpu.VMEM((4, VEC_ROWS, D), bf),
+            pltpu.VMEM((4, 4, SP, D), bf), pltpu.VMEM((4, SP, D), bf), pltpu.VMEM((4, 4, SP, D), bf),
+            pltpu.VMEM((4, 4, SP, D), bf), pltpu.VMEM((4, SP, D), f32), pltpu.VMEM(full[0], bf),
+        ]
+        + [pltpu.VMEM(r, f32) for r in regs] + [pltpu.VMEM(r, bf) for r in regs]
+        + [pltpu.VMEM(w.shape, f32) for w in (wq, wo, wu, wd)] + [pltpu.VMEM(w.shape, bf) for w in (wq, wo, wu, wd)]
+        + [dma((4, 4)), dma((4, 4)), dma((4,)), dma((4,)), dma((3,)), dma((3,)), dma((4, 3, 9)), dma((4, 3, 9)),
+           dma((4,)), dma((4,)), dma((4,)), dma((6,)), dma((16,))],
+        compiler_params=pltpu.CompilerParams(
+            collective_id=1, has_side_effects=True, vmem_limit_bytes=62 * 2**20),
+        cost_estimate=pl.CostEstimate(flops=2 * 9 * 784 * 768 * 768, bytes_accessed=40 * 2**20, transcendentals=0),
+        name="front",
+    )(tok, tmp, vec, spatial, wq, wo, wu, wd)
+
+
+def tail_kernel(
+    n_items, gd, gu, go, dk, dv, n_all, dq, x_in, dh, wq, vec, vp,
+    tg_out, vec_out, gq_out, go_out, gu_out, gd_out,
+    dk_s, dv_s, n_s, dq_s, x_s, dh_s, wq_s, vec_s, vp_s, nt_s, part_s, far_s, near_s, far_e, vb_s, gq_s,
+    sq, so, su, sd, cq, co, cu, cd, aq, ao, au, ad, bq, bo, bu, bd, zq, zo, zu, zd, fq, fo, fu, fd, eq, eo, eu, ed,
+    load_sem, n_sem, dh_sem, half_sem, put_sem, out_sem, p_send, p_recv, vb_send, vb_recv, g_send, g_recv, e_send, e_recv,
+):
+    bf, f32 = jnp.bfloat16, jnp.float32
+    i, f, core, stay, mine, other, far, flip = place()
+    ix, iy = halves(core, flip(i, 2), flip(i, 4)), halves(core, flip(i, 4), flip(i, 2))
+    xy = (i // 2) % 4
+    xy_x, xy_y = halves(core, flip(xy, 1), flip(xy, 2)), halves(core, flip(xy, 2), flip(xy, 1))
+    diag = flip(flip(xy, 1), 2)
+    c_dev, x_dev, y_dev, e_dev = (flip(i, 1), f), (ix, f), (iy, f), (i, other)
+    zs = [flip(f, 1), flip(f, 2), flip(flip(f, 1), 2)]
+    extra = []
+    bit = 8
+    while bit < n_items:
+        extra.append(bit)
+        bit *= 2
+
+    barrier = pltpu.get_barrier_semaphore()
+    partners = [c_dev, (flip(i, 2), f), (flip(i, 4), f)] + [(i, z) for z in zs] + [(flip(i, b), f) for b in extra]
+    for dev in partners:
+        pl.semaphore_signal(barrier, inc=1, device_id=dev, device_id_type=MESH)
+
+    loads = [pltpu.make_async_copy(a, b, load_sem.at[n]) for n, (a, b) in enumerate(
+        [(dk, dk_s), (dv, dv_s), (dq, dq_s), (x_in, x_s), (wq, wq_s), (vec, vec_s), (vp, vp_s)])]
+    for copy in loads:
+        copy.start()
+    def n_load(s):
+        return pltpu.make_async_copy(n_all.at[s], n_s.at[s % 2], n_sem.at[s % 2])
+
+    n_load(0).start()
+    n_load(1).start()
+    grads = (gq_s, go, gu, gd)
+    sums, crecv, r1, r2, r3, fin, ext = ((sq, so, su, sd), (cq, co, cu, cd), (aq, ao, au, ad), (bq, bo, bu, bd),
+                                         (zq, zo, zu, zd), (fq, fo, fu, fd), (eq, eo, eu, ed))
+    outs = (gq_out, go_out, gu_out, gd_out)
+
+    def cols_of(w, half):
+        width = sums[w].shape[-1]
+        return pl.ds(pl.multiple_of(half * width, 128), width)
+
+    def half_load(w):
+        return pltpu.make_async_copy(grads[w].at[:, :, :, cols_of(w, core)], sums[w], half_sem.at[w])
+
+    for w in (3, 2, 1):
+        half_load(w).start()
+    pl.semaphore_wait(barrier, len(partners))
+
+    def remote(src, dst, ssem, rsem, dev):
+        return pltpu.make_async_remote_copy(
+            src_ref=src, dst_ref=dst, send_sem=ssem, recv_sem=rsem, device_id=dev, device_id_type=MESH)
+
+    def rows_of(w):
+        unit = sums[w].shape[2] // 3
+        return (pl.ds(0, 2 * unit), pl.ds(2 * unit, unit))
+
+    def g_copies(w, stage):
+        s, base = sums[w], 0
+        ra, rb = rows_of(w)
+        found = []
+
+        def add(src, dst, dev):
+            found.append((src, dst, dev))
+
+        if stage == 0:
+            for z in range(4):
+                add(grads[w].at[z, :, :, cols_of(w, 1 - core)], crecv[w].at[z], c_dev)
+        elif stage == 1:
+            base = 4
+            for z in range(4):
+                add(s.at[z, xy_x, ra], r1[w].at[z, 0, ra], x_dev)
+                add(s.at[z, diag, ra], r1[w].at[z, 1, ra], x_dev)
+                add(s.at[z, xy_y, rb], r1[w].at[z, 0, rb], y_dev)
+                add(s.at[z, diag, rb], r1[w].at[z, 1, rb], y_dev)
+        elif stage == 2:
+            base = 20
+            for z in range(4):
+                add(s.at[z, xy_y, ra], r2[w].at[z, ra], y_dev)
+                add(s.at[z, xy_x, rb], r2[w].at[z, rb], x_dev)
+        elif stage == 3:
+            base = 28
+            for d in range(3):
+                add(s.at[zs[d], xy], r3[w].at[d], (i, zs[d]))
+        return [remote(src, dst, g_send.at[w, base + n], g_recv.at[w, base + n], dev)
+                for n, (src, dst, dev) in enumerate(found)]
+
+    AX, AY, AC0, ADA, ADB, AC1, AC2, AC3 = range(31, 39)
+
+    def region(w, at, half, piece):
+        rows = sums[w].shape[2]
+        unit = rows // 3
+        start, count = at * rows, rows
+        if piece == 1:
+            count = 2 * unit
+        elif piece == 2:
+            start, count = start + 2 * unit, unit
+        return outs[w].at[pl.ds(pl.multiple_of(start, 16), count), cols_of(w, half)]
+
+    def a_copy(w, kind):
+        at = {AX: xy, AY: xy, AC0: xy, ADA: xy_x, ADB: xy_y, AC1: xy_x, AC2: xy_y, AC3: diag}[kind]
+        piece = {ADA: 1, ADB: 2}.get(kind, 0)
+        dev = {AX: x_dev, AY: y_dev, ADA: y_dev, ADB: x_dev}.get(kind, c_dev)
+        dst = region(w, at, core, piece)
+        src = fin[w] if kind in (AX, AY, AC0) else dst
+        return remote(src, dst, g_send.at[w, kind], g_recv.at[w, kind], dev)
+
+    def a_arrival(w, kind):
+        at = {AX: xy_x, AY: xy_y, ADA: diag, ADB: diag, AC0: xy, AC1: xy_y, AC2: xy_x, AC3: diag}[kind]
+        piece = {ADA: 1, ADB: 2}.get(kind, 0)
+        ref = region(w, at, (1 - core) if kind >= AC1 or kind == AC0 else core, piece)
+        return remote(ref, ref, g_send.at[w, kind], g_recv.at[w, kind], c_dev)
+
+    def start(copies):
+        for copy in copies:
+            copy.start()
+
+    def plus(ref, where, other_ref, other_where):
+        ref[where] = (ref[where].astype(f32) + other_ref[other_where].astype(f32)).astype(bf)
+
+    def g_step(w, stage):
+        ra, rb = rows_of(w)
+        for copy in g_copies(w, stage):
+            copy.wait_recv()
+        s = sums[w]
+        if stage == 0:
+            half_load(w).wait()
+
+            def one(n, _):
+                plus(s, (n // 4, n % 4), crecv[w], (n // 4, n % 4))
+                return 0
+            lax.fori_loop(0, 16, one, 0)
+        elif stage == 1:
+            def one(z, _):
+                plus(s, (z, xy, ra), r1[w], (z, 0, ra))
+                plus(s, (z, xy_y, ra), r1[w], (z, 1, ra))
+                plus(s, (z, xy, rb), r1[w], (z, 0, rb))
+                plus(s, (z, xy_x, rb), r1[w], (z, 1, rb))
+                return 0
+            lax.fori_loop(0, 4, one, 0)
+        elif stage == 2:
+            def one(z, _):
+                plus(s, (z, xy), r2[w], (z,))
+                return 0
+            lax.fori_loop(0, 4, one, 0)
+        elif stage == 3:
+            total = s[f, xy].astype(f32)
+            for d in range(3):
+                total = total + r3[w][d].astype(f32)
+            fin[w][...] = total.astype(bf)
+            for n, b in enumerate(extra):
+                copy = remote(fin[w], ext[w].at[n], e_send.at[w, n], e_recv.at[w, n], (flip(i, b), f))
+                copy.start()
+                copy.wait()
+                fin[w][...] = (fin[w][...].astype(f32) + ext[w][n].astype(f32)).astype(bf)
+            pltpu.make_async_copy(fin[w], region(w, xy, core, 0), put_sem.at[w]).start()
+            start([a_copy(w, kind) for kind in (AX, AY, AC0)])
+        if stage < 3:
+            start(g_copies(w, stage + 1))
+
+    def a_step_one(w):
+        a_arrival(w, AX).wait_recv()
+        start([a_copy(w, ADA), a_copy(w, AC1)])
+        a_arrival(w, AY).wait_recv()
+        start([a_copy(w, ADB), a_copy(w, AC2)])
+
+    def a_step_two(w):
+        a_arrival(w, ADA).wait_recv()
+        a_arrival(w, ADB).wait_recv()
+        a_copy(w, AC3).start()
+
+    def a_step_three(w):
+        for kind in (AC0, AC1, AC2, AC3):
+            a_arrival(w, kind).wait_recv()
+        pltpu.make_async_copy(fin[w], region(w, xy, core, 0), put_sem.at[w]).wait()
+
+    def partial_rows(shard):
+        def tile(t, _):
+            at = pl.multiple_of(t * 256, 256)
+            keys = mm(dk_s[shard].reshape(4 * SP, D), wq_s[pl.ds(at, 256), D : 2 * D], NT)
+            values = mm(dv_s[shard].reshape(4 * SP, D), wq_s[pl.ds(at, 256), 2 * D :], NT)
+            part_s[shard, :, :, pl.ds(at, 256)] = (keys + values).astype(bf).reshape(4, SP, 256)
+            return 0
+        lax.fori_loop(0, 3, tile, 0)
+
+    far_copy = remote(part_s.at[3 - far], far_s, p_send.at[0], p_recv.at[0], c_dev)
+    near_copy = remote(part_s.at[3 - mine], near_s, p_send.at[1], p_recv.at[1], c_dev)
+    chip_copy = remote(part_s.at[far], far_e, p_send.at[2], p_recv.at[2], e_dev)
+
+    for w in (3, 2, 1):
+        start(g_copies(w, 0))
+    for n in (0, 1, 4):
+        loads[n].wait()
+    partial_rows(3 - far)
+    far_copy.start()
+    partial_rows(far)
+    far_copy.wait_recv()
+
+    def add_far(j, _):
+        plus(part_s, (far, j), far_s, (j,))
+        return 0
+    lax.fori_loop(0, 4, add_far, 0)
+    chip_copy.start()
+    g_step(3, 0)
+    g_step(2, 0)
+    g_step(1, 0)
+    loads[2].wait()
+    for s in range(4):
+        n_load(s).wait()
+        nt_s[s] = jnp.transpose(n_s[s % 2].reshape(4 * SP, D))
+        if s < 2:
+            n_load(s + 2).start()
+
+    def grad_q(t, _):
+        cols = pl.ds(pl.multiple_of(t * 256, 256), 256)
+        g = mm(nt_s[mine], dq_s[:, :, cols].reshape(4 * SP, 256))
+        gq_s[:, :, :, cols] = g.astype(bf).reshape(4, 4, D // 16, 256)
+        return 0
+    lax.fori_loop(0, 3, grad_q, 0)
+
+    def grad_kv(t, _):
+        cols = pl.ds(pl.multiple_of(t * 256, 256), 256)
+        gk = jnp.zeros((D, 256), f32)
+        gv = jnp.zeros((D, 256), f32)
+        for s in range(4):
+            gk = gk + mm(nt_s[s], dk_s[s, :, :, cols].reshape(4 * SP, 256))
+            gv = gv + mm(nt_s[s], dv_s[s, :, :, cols].reshape(4 * SP, 256))
+        gq_s[:, :, :, pl.ds(pl.multiple_of(D + t * 256, 256), 256)] = gk.astype(bf).reshape(4, 4, D // 16, 256)
+        gq_s[:, :, :, pl.ds(pl.multiple_of(2 * D + t * 256, 256), 256)] = gv.astype(bf).reshape(4, 4, D // 16, 256)
+        return 0
+    lax.fori_loop(0, 3, grad_kv, 0)
+    half_load(0).start()
+    start(g_copies(0, 0))
+    g_step(3, 1)
+    partial_rows(3 - mine)
+    near_copy.start()
+    partial_rows(mine)
+    g_step(0, 0)
+    g_step(2, 1)
+    g_step(1, 1)
+    g_step(3, 2)
+    for n in (3, 5, 6):
+        loads[n].wait()
+    near_copy.wait_recv()
+    chip_copy.wait_recv()
+    gain = vec_s[0, 0:1, :].astype(f32)
+
+    def column_sums(j, carry):
+        bias_q, bias_v = carry
+        bias_q = bias_q + jnp.sum(dq_s[j].astype(f32), axis=0, keepdims=True)
+        for s in range(4):
+            bias_v = bias_v + jnp.sum(dv_s[s, j].astype(f32), axis=0, keepdims=True)
+        return bias_q, bias_v
+    zero = jnp.zeros((1, D), f32)
+    bias_q, bias_v = lax.fori_loop(0, 4, column_sums, (zero, zero))
+    vp_s[0, 2:3, :] = bias_q
+    vp_s[1, 0:1, :] = bias_v
+
+    def dh_load(j):
+        return pltpu.make_async_copy(dh.at[j], dh_s.at[j % 2], dh_sem.at[j % 2])
+
+    dh_load(0).start()
+
+    def norm_back(j, carry):
+        gains, shifts = carry
+
+        @pl.when(j < 3)
+        def _():
+            dh_load(j + 1).start()
+
+        dh_load(j).wait()
+        dn = mm(dq_s[j], wq_s[:, :D], NT) + part_s[mine, j].astype(f32) + near_s[j].astype(f32) + far_e[j].astype(f32)
+        x = x_s[j]
+        centred = x - jnp.mean(x, axis=-1, keepdims=True)
+        scale = lax.rsqrt(jnp.mean(centred * centred, axis=-1, keepdims=True) + 1e-06)
+        unit = centred * scale
+        gains = gains + jnp.sum(dn * unit, axis=0, keepdims=True)
+        shifts = shifts + jnp.sum(dn, axis=0, keepdims=True)
+        dn = dn * gain
+        back = dn - jnp.mean(dn, axis=-1, keepdims=True) - unit * jnp.mean(dn * unit, axis=-1, keepdims=True)
+        x_s[j] = dh_s[j % 2] + back * scale
+        return gains, shifts
+    gains, shifts = lax.fori_loop(0, 4, norm_back, (zero, zero))
+    vp_s[0, 0:1, :] = gains
+    vp_s[0, 1:2, :] = shifts
+
+    tg_put = pltpu.make_async_copy(x_s, tg_out, out_sem.at[0])
+    tg_put.start()
+
+    ring = [c_dev, (flip(i, 2), f), (flip(i, 4), f), (i, zs[0]), (i, zs[1])] + [(flip(i, b), f) for b in extra]
+
+    def v_copy(n):
+        return remote(vp_s, vb_s.at[n], vb_send.at[n], vb_recv.at[n], ring[n])
+
+    def v_step(n):
+        v_copy(n).wait()
+        vp_s[...] = vp_s[...] + vb_s[n]
+        if n + 1 < len(ring):
+            v_copy(n + 1).start()
+
+    v_copy(0).start()
+    g_step(2, 2)
+    v_step(0)
+    g_step(1, 2)
+    v_step(1)
+    g_step(0, 1)
+    v_step(2)
+    g_step(3, 3)
+    g_step(2, 3)
+    v_step(3)
+    g_step(1, 3)
+    a_step_one(3)
+    a_step_one(2)
+    g_step(0, 2)
+    for n in range(4, len(ring)):
+        v_step(n)
+    a_step_one(1)
+    a_step_two(3)
+    a_step_two(2)
+    g_step(0, 3)
+    a_step_two(1)
+    a_step_three(3)
+    a_step_three(2)
+    a_step_one(0)
+    a_step_three(1)
+    a_step_two(0)
+    a_step_three(0)
+    vec_put = pltpu.make_async_copy(vp_s.at[f], vec_out, out_sem.at[1])
+    vec_put.start()
+    for w in range(4):
+        for stage in range(4):
+            for copy in g_copies(w, stage):
+                copy.wait_send()
+        for kind in (AX, AY, AC0, ADA, ADB, AC1, AC2, AC3):
+            a_copy(w, kind).wait_send()
+    far_copy.wait_send()
+    near_copy.wait_send()
+    chip_copy.wait_send()
+    tg_put.wait()
+    vec_put.wait()
+
+
+def tail(n_items, gd, gu, go, dk, dv, n_all, dq, x_in, dh, wq, vec, vp):
+    bf, f32 = jnp.bfloat16, jnp.float32
+    S = jax.ShapeDtypeStruct
+    hb = pl.BlockSpec(memory_space=pltpu.HBM)
+    dma = pltpu.SemaphoreType.DMA
+    n_extra = 0
+    while 8 * 2**n_extra < n_items:
+        n_extra += 1
+    shapes = [(D // 16, 3 * D // 2)] + [(g.shape[2], g.shape[3] // 2) for g in (go, gu, gd)]
+    v = lambda shape, dtype=bf: pltpu.VMEM(shape, dtype)
+    rows = (4, SP, D)
+    return pl.pallas_call(
+        functools.partial(tail_kernel, n_items),
+        out_shape=(S(rows, f32), S((8, D), f32), S((D // 4, 3 * D), bf))
+        + tuple(S((4 * g.shape[2], g.shape[3]), bf) for g in (go, gu, gd)),
+        in_specs=[hb] * 12,
+        out_specs=(hb,) * 6,
+        scratch_shapes=[
+            v((4,) + rows), v((4,) + rows), v((2,) + rows), v(rows), v(rows, f32), v((2, SP, D), f32), v((D, 3 * D)),
+            v((4, VEC_ROWS, D)), v((4, 8, D), f32), v((4, D, 4 * SP)), v((4,) + rows), v(rows), v(rows), v(rows),
+            v((5 + n_extra, 4, 8, D), f32), v((4, 4, D // 16, 3 * D)),
+        ]
+        + [v((4, 4) + s) for s in shapes] + [v((4, 4) + s) for s in shapes] + [v((4, 2) + s) for s in shapes]
+        + [v((4,) + s) for s in shapes] + [v((3,) + s) for s in shapes] + [v(s) for s in shapes]
+        + [v((max(n_extra, 1),) + (s if n_extra else (16, 128))) for s in shapes]
+        + [dma((7,)), dma((2,)), dma((2,)), dma((4,)), dma((4,)), dma((2,)), dma((3,)), dma((3,)), dma((5 + n_extra,)), dma((5 + n_extra,)),
+           dma((4, 39)), dma((4, 39)), dma((4, max(n_extra, 1))), dma((4, max(n_extra, 1)))],
+        compiler_params=pltpu.CompilerParams(
+            collective_id=2, has_side_effects=True, vmem_limit_bytes=63 * 2**20),
+        cost_estimate=pl.CostEstimate(flops=2 * 14 * 784 * 768 * 768, bytes_accessed=60 * 2**20, transcendentals=0),
+        name="tail",
+    )(gd, gu, go, dk, dv, n_all, dq, x_in, dh, wq, vec, vp)
 
 
 def on_device(
@@ -262,77 +1017,74 @@
     vector_first,
     vector_second,
 ):
-    frame_rank = lax.axis_index("frames")
     bf, f32 = jnp.bfloat16, jnp.float32
-    gather = lambda w: lax.all_gather(w.astype(bf), "frames", axis=0, tiled=True)
-    qkv_full, vector_full, out_full, up_full, down_full = (
-        gather(qkv_weight), gather(vectors), gather(out_weight), gather(up_weight), gather(down_weight))
-    (gain_one, shift_one, bias_query, bias_value, bias_output, gain_two, shift_two, bias_down, bias_up,
-    ) = unpack(vector_full.astype(f32))
-    pad = lambda a: jnp.pad(a[0], ((0, 0), (0, SP - FRAME_TOK), (0, 0))).reshape(4 * SP, D)
-    pos = jnp.pad(positions(date_year[0], date_day[0]), ((0, 0), (0, SP - FRAME_TOK), (0, 0))).reshape(4 * SP, D)
-    residual_in = pad(tokens).astype(f32) + pos
+    n_items = lax.axis_size("items")
+    i, f, core, stay, mine, other, far, flip = place()
+    swap = []
+    for k in range(n_items):
+        for z in range(4):
+            if k % 2 != z // 2:
+                swap.append((k * 4 + z, (k ^ 1) * 4 + 3 - z))
+
+    def to_worker(array):
+        return jnp.where(stay, array, lax.ppermute(array, ("items", "frames"), swap))
+
+    pad = lambda a: jnp.pad(a[0], ((0, 0), (0, SP - FRAME_TOK), (0, 0)))
     item_index, is_valid = slot_items(item_dates[0], slot_frame[0], frame_mask[0])
-    own_items = lax.dynamic_slice_in_dim(item_index, frame_rank * 4, 4)
-    idx, val = key_tables(item_index, is_valid, own_items)
-    normed, norm_one_back = jax.vjp(layer_norm, residual_in, gain_one, shift_one)
-    normed_low = normed.astype(bf)
-    normed_all = lax.all_gather(normed_low, "frames", axis=0, tiled=True)
-    query_low = (mm(normed_low, qkv_full[:, :D]) + bias_query).astype(bf)
-    key_value = mm(normed_all, qkv_full[:, D:]) + jnp.concatenate([jnp.zeros_like(bias_value), bias_value])
-    key_all = key_value[:, :D].astype(bf)
-    value_all = key_value[:, D:].astype(bf)
-    q3 = (query_low * jnp.asarray(0.125, bf)).reshape(4, SP, D)
-    k3 = key_all.reshape(16, SP, D)
-    v3 = value_all.reshape(16, SP, D)
+    own_items = lax.dynamic_slice_in_dim(item_index, f * 4, 4)
+    tables = jnp.concatenate(key_tables(item_index, is_valid, own_items)).astype(f32)
+    tmp = jnp.concatenate([temporal_rows(date_year[0], date_day[0]), jnp.pad(tables[None], ((0, 3), (0, D - 8 * NK)))])
+    vec = jnp.pad(vectors.astype(bf).reshape(3, D), ((0, VEC_ROWS - 3), (0, 0)))
+    q3, k4, v4, n4, x3, vec_all, tmp_own, wq, wo, wu, wd = front(
+        pad(tokens), tmp, vec, jnp.asarray(spatial_rows()), qkv_weight, out_weight, up_weight, down_weight)
+    tables = tmp_own[4, : 8 * NK].astype(jnp.int32)
+    idx, val = tables[: 4 * NK], tables[4 * NK :]
+    k3, v3 = k4.reshape(16, SP, D), v4.reshape(16, SP, D)
     o3, lse = attn_fwd(idx, val, q3, k3, v3)
+    grad_out_low = to_worker(pad(cotangent)).reshape(4 * SP, D)
+    v_rows = vec_all[:, :3].astype(f32).reshape(12, D)
+    bias_output, gain_two, shift_two, bias_down = v_rows[4], v_rows[5], v_rows[6], v_rows[7]
+    bias_up = v_rows[8:].reshape(4 * D)
+    residual_in = x3.reshape(4 * SP, D)
     attended_low = o3.reshape(4 * SP, D)
-    branch = mm(attended_low, out_full) + bias_output
+    branch = mm(attended_low, wo) + bias_output
     hidden = residual_in + branch
     normed_two, norm_two_back = jax.vjp(layer_norm, hidden, gain_two, shift_two)
     normed_two_low = normed_two.astype(bf)
-    inner = mm(normed_two_low, up_full) + bias_up
+    inner = mm(normed_two_low, wu) + bias_up
     active, gelu_back = jax.vjp(exact_gelu, inner)
     active_low = active.astype(bf)
-    mlp_out = mm(active_low, down_full) + bias_down
-    block_out = (hidden + mlp_out).astype(bf)
-    grad_out_low = pad(cotangent)
+    mlp_out = mm(active_low, wd) + bias_down
+    block_out = to_worker((hidden + mlp_out).astype(bf))
     grad_out = grad_out_low.astype(f32)
     TN = (((0,), (0,)), ((), ()))
     down_grad = mm(active_low, grad_out_low, TN)
     bias_down_grad = jnp.sum(grad_out, axis=0)
-    (inner_grad,) = gelu_back(mm(grad_out_low, down_full, NT))
+    (inner_grad,) = gelu_back(mm(grad_out_low, wd, NT))
     inner_grad_low = inner_grad.astype(bf)
     up_grad = mm(normed_two_low, inner_grad_low, TN)
     bias_up_grad = jnp.sum(inner_grad_low.astype(f32), axis=0)
-    hidden_from_norm, gain_two_grad, shift_two_grad = norm_two_back(mm(inner_grad_low, up_full, NT))
+    hidden_from_norm, gain_two_grad, shift_two_grad = norm_two_back(mm(inner_grad_low, wu, NT))
     hidden_grad = grad_out + hidden_from_norm
     branch_grad_low = hidden_grad.astype(bf)
     out_grad = mm(attended_low, branch_grad_low, TN)
     bias_output_grad = jnp.sum(branch_grad_low.astype(f32), axis=0)
-    attended_grad_low = mm(branch_grad_low, out_full, NT).astype(bf)
+    attended_grad_low = mm(branch_grad_low, wo, NT).astype(bf)
     dq3, dk3, dv3 = attn_bwd(idx, val, q3, k3, v3, o3, attended_grad_low.reshape(4, SP, D), lse)
-    dq = dq3.reshape(4 * SP, D)
-    dk = dk3.reshape(16 * SP, D).astype(bf)
-    dv = dv3.reshape(16 * SP, D).astype(bf)
-    bias_query_grad = jnp.sum(dq.astype(f32), axis=0)
-    bias_value_grad = jnp.sum(dv3, axis=(0, 1))
-    qkv_grad = jnp.concatenate([mm(normed_low, dq, TN), mm(normed_all, dk, TN), mm(normed_all, dv, TN)], axis=1)
-    part = (mm(dk, qkv_full[:, D : 2 * D], NT) + mm(dv, qkv_full[:, 2 * D :], NT)).astype(bf)
-    normed_grad = lax.psum_scatter(part, "frames", scatter_dimension=0, tiled=True).astype(f32)
-    normed_grad = normed_grad + mm(dq, qkv_full[:, :D], NT)
-    input_from_norm, gain_one_grad, shift_one_grad = norm_one_back(normed_grad)
-    token_grad = hidden_grad + input_from_norm
-    vector_grad = jnp.concatenate([gain_one_grad, shift_one_grad, bias_query_grad, bias_value_grad,
-        bias_output_grad, gain_two_grad, shift_two_grad, bias_down_grad, bias_up_grad])
-    scatter = lambda g: lax.psum_scatter(g.astype(bf), "frames", scatter_dimension=0, tiled=True)
-    vec_sum = lax.psum(lax.psum_scatter(vector_grad, "frames", scatter_dimension=0, tiled=True), "items")
-    sums = [lax.psum(scatter(g), "items").astype(f32) for g in (down_grad, up_grad, out_grad, qkv_grad)]
-    qkv_new = adamw(qkv_weight, qkv_first, qkv_second, sums[3], 0.05, 0.05)
-    out_new = adamw(out_weight, out_first, out_second, sums[2], 0.5, 0.05)
-    up_new = adamw(up_weight, up_first, up_second, sums[1], 0.05, 0.05)
-    down_new = adamw(down_weight, down_first, down_second, sums[0], 0.03, 0.05)
-    vector_new = adamw(vectors, vector_first, vector_second, vec_sum, 0.3, 0.0)
+    zero = jnp.zeros((4 * D,), f32)
+    vector_part = jnp.concatenate([zero, bias_output_grad, gain_two_grad, shift_two_grad, bias_down_grad, bias_up_grad])
+    vector_part = jnp.pad(vector_part.reshape(4, 3, D), ((0, 0), (0, 5), (0, 0)))
+    blocks = lambda g: g.astype(bf).reshape(4, 4, g.shape[0] // 16, g.shape[1])
+    token_grad, vector_sum, qkv_sum, out_sum, up_sum, down_sum = tail(
+        n_items, blocks(down_grad), blocks(up_grad), blocks(out_grad), dk3.reshape(4, 4, SP, D), dv3.reshape(4, 4, SP, D),
+        n4, dq3, x3, hidden_grad.reshape(4, SP, D), wq, vec_all, vector_part)
+    token_grad = jnp.where(
+        stay, token_grad, lax.ppermute(token_grad.astype(bf), ("items", "frames"), swap).astype(f32))
+    qkv_new = adamw(qkv_weight, qkv_first, qkv_second, qkv_sum.astype(f32), 0.05, 0.05)
+    out_new = adamw(out_weight, out_first, out_second, out_sum.astype(f32), 0.5, 0.05)
+    up_new = adamw(up_weight, up_first, up_second, up_sum.astype(f32), 0.05, 0.05)
+    down_new = adamw(down_weight, down_first, down_second, down_sum.astype(f32), 0.03, 0.05)
+    vector_new = adamw(vectors, vector_first, vector_second, vector_sum[:3].reshape(3 * D), 0.3, 0.0)
     cut = lambda a: a.reshape(1, 4, SP, D)[:, :, :FRAME_TOK]
     return (cut(block_out), cut(token_grad)) + qkv_new + out_new + up_new + down_new + vector_new
 

time: 974 us -> 515 us (0.53)
  waiting for transfers between devices: 553 us -> 33.7 us
  Pallas kernels: 88.3 us -> 330 us
  matrix products: 143 us -> 74.7 us
  blocking collectives: 47.5 us -> 0 us
  local copies, waits for them, and re-layouts: 47.2 us -> 15.6 us
  other arithmetic: 69.4 us -> 40.7 us
  between operations: 15.5 us -> 1.62 us
    reduce_scatter x5 -> x0, waiting for transfers between devices: 274 us -> none  [the longest x4 180 us: on_device(): lax.psum_scatter(g.astype(bf), 'frames', scatter_dimension=0, tiled=True)]
    all_gather x5 -> x0, waiting for transfers between devices: 266 us -> none  [the longest x4 173 us: on_device(): lax.all_gather(w.astype(bf), 'frames', axis=0, tiled=True)]
    pallas_call x0 -> x2, Pallas kernels: none -> 244 us  [the longest x1 132 us: front(): pl.pallas_call(front_kernel, out_shape=(S((4, SP, D), bf), S((4, 4, SP, D...]
    dot_general x17 -> x9, matrix products: 143 us -> 74.7 us  [mm(): return lax.dot_general(a, b, dims, preferred_element_type=jnp.float32)]
    ppermute x0 -> x3, waiting for transfers between devices: none -> 33.7 us  [the longest x1 22.9 us: on_device(): lax.ppermute(token_grad.astype(bf), ('items', 'frames'), swap).astype(f32)]
    psum x1 -> x0, blocking collectives: 23.3 us -> none  [on_device(): lax.psum(lax.psum_scatter(vector_grad, 'frames', scatter_dimension=0, til...]
    unnamed x158 -> x97, local copies, waits for them, and re-layouts: 31.8 us -> 8.63 us
    convert_element_type x12 -> x5, other arithmetic: 19 us -> 2.62 us  [the longest x1 1.85 us: on_device(): token_grad.astype(bf)]
  transfers between devices with their start and end apart: 11 -> 3, of which waited for: 9 -> 2; matrix products, arithmetic and copies ran while one was open for 20% -> 8% of each run, Pallas kernels for 9% -> 32%
where the time goes in v2:
time: 515 us; the launch traced here: 506 us
  Pallas kernels  330 us (64%)
  matrix products  74.7 us (15%)
  other arithmetic  40.7 us (8%)
  waiting for transfers between devices  33.7 us (7%)
  local copies, waits for them, and re-layouts  15.6 us (3%)
  starting transfers between devices  9.45 us (2%)
    pallas_call x1, Pallas kernels, front(): pl.pallas_call(front_kernel, out_shape=(S((4, SP, D), bf), S((4, 4, SP, D...  132 us
    pallas_call x1, Pallas kernels, tail(): pl.pallas_call(functools.partial(tail_kernel, n_items), out_shape=(S(rows...  112 us
    dot_general x9, matrix products, mm(): return lax.dot_general(a, b, dims, preferred_element_type=jnp.float32)  74.7 us
    pallas_call x1, Pallas kernels, attn_bwd(): pl.pallas_call(attn_bwd_kernel, out_shape=(jax.ShapeDtypeStruct((4, SP, D...  55.3 us
    pallas_call x1, Pallas kernels, attn_fwd(): pl.pallas_call(attn_fwd_kernel, out_shape=(jax.ShapeDtypeStruct((4, SP, D...  30.9 us
    ppermute x1, waiting for transfers between devices, on_device(): lax.ppermute(token_grad.astype(bf), ('items', 'frames'), swap).astype(f32)  22.9 us
    sub x5, other arithmetic, adamw(): weight - step_rate * (first_hat / (jnp.sqrt(second_hat) + 1e-08) + decay...  15.8 us
    convert_element_type x1, other arithmetic, on_device(): active_low = active.astype(bf)  11.7 us
  transfers between devices with their start and end apart: 3, of which 2 were waited for; matrix products, arithmetic and copies ran while one was open for 8% of the time, Pallas kernels for 32%

profile of v2, /device:TPU:13, one launch (start us, length us, event | category | flops | bytes accessed | tf_op | source)
XLA Modules:
  0.0 505.7 jit_solution(9239419758370568559)
XLA Ops:
  0.7 1.5 copy.56
  2.2 1.1 pad.27
  3.3 3.9 collective-permute-start.1
  8.7 0.6 pad.26.vec
  9.4 1.1 pad.23.tok
  10.8 0.6 select_maximum_fusion.tmp
  11.5 131.5 %front.1 = (bf16[4,208,768]{2,1,0:T(8,128)(2,1)}, bf16[4,4,208,768]{3,2,1,0:T(8,128)(2,1)}, bf16[4,4,208,768]{3,2,1,0:T(8,128)(2,1)}, bf16[4,4,208,768]{3,2,1,0:...) custom-call(bf16[4,208,768]{2,1,0:T(8,128)(2,1)} %pad.23.tok, ...), custom_call_target="tpu_custom_call" | custom-call | flops 8323596288 | bytes 41943040 | tf_op jit(solution)/shard_map/front/pallas_call | solution.py:594
  143.0 0.8 slice_convert_fusion
  143.8 0.6 slice_reduce_fusion
  144.4 0.7 slice_convert_fusion.1
  145.1 0.6 slice_bitcast_fusion
  145.7 30.9 %attn_fwd.1 = (bf16[4,208,768]{2,1,0:T(8,128)(2,1)}, f32[4,6,8,208]{3,2,1,0:T(8,128)}) custom-call(s32[24]{0:T(128)} %get-tuple-element.150.idx_ref, s32[24]{0:T(128)} %get-tuple-element.149.val_ref, bf16[4,208,768]{2,1,0:T(8,128)(2,1)} %get-tuple-element.41.q_ref, bf16[16,208,768]{2,1,0:T(8,128)(2,1)} %bitcast.70, bf16[16,208,768]{2,1,0:T(8,128)(2,1)} %bitcast.72), custom_call_target="tpu_custom_call" | custom-call | flops 12759072768 | bytes 14680064 | tf_op jit(solution)/shard_map/attn_fwd/pallas_call | solution.py:190
  176.6 4.8 fusion.35
  181.4 2.3 multiply_reduce_fusion.2
  183.7 0.6 broadcast_dynamic-update-slice_fusion
  184.3 6.5 %fusion.22 = f32[832,3072]{1,0:T(8,128)S(1)} fusion(bf16[768,3072]{1,0:T(8,128)(2,1)} %get-tuple-element.47, f32[832,768]{1,0:T(8,128)S(1)} %copy-done.1, f32[768]{0:T(1024)S(1)} %get-tuple-element.116, f32[768]{0:T(1024)S(1)} %get-tuple-element.117, f32[832]{0:T(1024)S(1)} %fusion.16, f32[832]{0:T(1024)S(1)} %broadcast_multiply_fusion), kind=kOutput, calls=%fused_computation.110 | convolution fusion | flops 3929063424 | bytes 17510912 | tf_op jit(solution)/shard_map/dot_general | solution.py:87
  190.8 3.9 convert_reduce_fusion.1
  194.8 28.7 %convert_reduce_fusion = (f32[3072]{0:T(1024)S(1)}, bf16[832,3072]{1,0:T(8,128)(2,1)S(1)}, f32[832,3072]{1,0:T(8,128)}) fusion(f32[832,3072]{1,0:T(8,128)S(1)} %fusion.22, f32[3072]{0:T(1024)S(1)} %add.179, bf16[832,768]{1,0:T(8,128)(2,1)S(1)} %bitcast.62, bf16[3072,768]{1,0:T(8,128)(2,1)S(1)} %bitcast.87), kind=kOutput, calls=%fused_computation.2 | convolution fusion | flops 4117558272 | bytes 31580160 | tf_op jit(solution)/shard_map/dot_general | solution.py:87
  223.5 4.7 multiply_reduce_fusion
  228.2 8.1 %convolution_convert_fusion = bf16[768,3072]{1,0:T(8,128)(2,1)} fusion(bf16[832,3072]{1,0:T(8,128)(2,1)S(1)} %get-tuple-element.135, f32[832,768]{1,0:T(8,128)S(1)} %copy-done.1, f32[768]{0:T(1024)S(1)} %get-tuple-element.116, f32[768]{0:T(1024)S(1)} %get-tuple-element.117, f32[832]{0:T(1024)S(1)} %fusion.16, f32[832]{0:T(1024)S(1)} %broadcast_multiply_fusion), kind=kOutput, calls=%fused_computation.18 | convolution fusion | flops 3931422720 | bytes 12399104 | tf_op jit(solution)/shard_map/dot_general | solution.py:87
  236.3 1.0 fusion.33
  237.3 0.4 convert_reduce_fusion.2
  237.8 0.8 copy-done.39
  238.6 2.3 convolution_convert_fusion.2
  240.9 2.5 convolution_convert_fusion.3
  243.3 11.7 %multiply_convert_fusion = bf16[832,3072]{1,0:T(8,128)(2,1)} fusion(f32[832,3072]{1,0:T(8,128)} %get-tuple-element.136, f32[832,3072]{1,0:T(8,128)} %copy-done, f32[3072]{0:T(1024)S(1)} %add.179), kind=kLoop, calls=%fused_computation.4 | loop fusion | flops 10223616 | bytes 25571328 | tf_op jit(solution)/shard_map/convert_element_type | solution.py:1056
  255.0 9.7 %convolution_convert_fusion.1 = bf16[3072,768]{1,0:T(8,128)(2,1)} fusion(bf16[832,3072]{1,0:T(8,128)(2,1)} %multiply_convert_fusion, bf16[832,768]{1,0:T(8,128)(2,1)S(1)} %bitcast.63), kind=kOutput, calls=%fused_computation.19 | convolution fusion | flops 3928227840 | bytes 11108352 | tf_op jit(solution)/shard_map/dot_general | solution.py:87
  264.8 7.5 %add_convert_fusion.1 = bf16[832,768]{1,0:T(8,128)(2,1)} fusion(f32[832,768]{1,0:T(8,128)S(1)} %copy-done.2, bf16[832,3072]{1,0:T(8,128)(2,1)S(1)} %copy-done.4, bf16[3072,768]{1,0:T(8,128)(2,1)} %get-tuple-element.48, f32[768]{0:T(1024)S(1)} %copy-done.31), kind=kOutput, calls=%fused_computation.32 | convolution fusion | flops 3927785472 | bytes 13667328 | tf_op jit(solution)/shard_map/dot_general | solution.py:87
  272.4 0.7 pad.28.vp
  273.0 55.3 %attn_bwd.1 = (bf16[4,208,768]{2,1,0:T(8,128)(2,1)}, bf16[16,208,768]{2,1,0:T(8,128)(2,1)}, bf16[16,208,768]{2,1,0:T(8,128)(2,1)}) custom-call(s32[24]{0:T(128)} %get-tuple-element.150.idx_ref, s32[24]{0:T(128)} %get-tuple-element.149.val_ref, bf16[4,208,768]{2,1,0:T(8,128)(2,1)} %get-tuple-element.41.q_ref, bf16[16,208,768]{2,1,0:T(8,128)(2,1)} %bitcast.71, ...), custom_call_target="tpu_custom_call" | custom-call | flops 31897681920 | bytes 41943040 | tf_op jit(solution)/shard_map/attn_bwd/pallas_call | solution.py:209
  328.4 112.2 %tail.1 = (f32[4,208,768]{2,1,0:T(8,128)}, f32[8,768]{1,0:T(8,128)}, bf16[192,2304]{1,0:T(8,128)(2,1)}, bf16[192,768]{1,0:T(8,128)(2,1)}, bf16[192,3072]{1,0:T(8,128)(2,1)}, /*index=5*/bf16[768,768]{1,0:T(8,128)(2,1)}) custom-call(bf16[4,4,192,768]{3,2,1,0:T(8,128)(2,1)} %bitcast.77, bf16[4,4,48,3072]{3,2,1,0:T(8,128)(2,1)} %bitcast.76, ...), custom_call_target="tpu_custom_call" | custom-call | flops 12947816448 | bytes 62914560 | tf_op jit(solution)/shard_map/tail/pallas_call | solution.py:973
  440.6 0.9 slice.55
  441.5 0.6 reshape.298
  442.1 1.8 convert_element_type.148
  444.0 1.9 collective-permute-start.2
  445.9 3.6 collective-permute-start
  449.6 5.1 %multiply_subtract_fusion.2 = (f32[192,2304]{1,0:T(8,128)}, f32[192,2304]{1,0:T(8,128)}, f32[192,2304]{1,0:T(8,128)}) fusion(f32[192,2304]{1,0:T(8,128)S(1)} %copy-done.12, bf16[192,2304]{1,0:T(8,128)(2,1)} %get-tuple-element.56, f32[192,2304]{1,0:T(8,128)S(1)} %copy-done.13, f32[192,2304]{1,0:T(8,128)} %param.31), kind=kLoop, calls=%fused_computation.45 | loop fusion | flops 7077888 | bytes 11501568 | tf_op jit(solution)/shard_map/sub | solution.py:246
  454.8 0.8 copy-done.17
  455.6 4.4 multiply_subtract_fusion.1
  460.0 1.5 multiply_subtract_fusion.3
  461.5 0.6 multiply_subtract_fusion.4
  462.2 0.4 copy-done.9
  462.6 0.3 copy-done.16
  462.9 4.1 multiply_subtract_fusion
  467.1 22.9 %collective-permute-done.2 = bf16[4,208,768]{2,1,0:T(8,128)(2,1)S(1)} collective-permute-done((bf16[4,208,768]{2,1,0:T(8,128)(2,1)S(1)}, bf16[4,208,768]{2,1,0:T(8,128)(2,1)S(1)}, u32[]{:S(2)}, u32[]{:S(2)}) %collective-permute-start.2) | collective-permute-done | bytes 1277984 | tf_op jit(solution)/shard_map/ppermute | solution.py:1082
  490.4 2.4 copy.52
  492.8 10.9 %collective-permute-done = bf16[832,768]{1,0:T(8,128)(2,1)S(1)} collective-permute-done((bf16[832,768]{1,0:T(8,128)(2,1)}, bf16[832,768]{1,0:T(8,128)(2,1)S(1)}, u32[]{:S(2)}, u32[]{:S(2)}) %collective-permute-start) | collective-permute-done | bytes 1277984 | tf_op jit(solution)/shard_map/ppermute | solution.py:1030
  503.9 1.5 copy.53
  (127 shorter events, 2.7 us)
Async XLA Ops:
  0.7 6.6 %copy-start.34 = (s32[1,3]{1,0:T(1,128)S(1)}, s32[1,3]{1,0:T(1,128)}, u32[]{:S(2)}) copy-start(s32[1,3]{1,0:T(1,128)} %param.27) | copy-start | bytes 40
  0.7 6.8 %copy-start.35 = (s32[1,16]{1,0:T(1,128)S(1)}, s32[1,16]{1,0:T(1,128)}, u32[]{:S(2)}) copy-start(s32[1,16]{1,0:T(1,128)} %param.28) | copy-start | bytes 196
  0.7 7.0 %copy-start.36 = (s32[1,16]{1,0:T(1,128)S(1)}, s32[1,16]{1,0:T(1,128)}, u32[]{:S(2)}) copy-start(s32[1,16]{1,0:T(1,128)} %param.29) | copy-start | bytes 196
  0.7 7.9 %copy-start.23 = (f32[2304]{0:T(1024)S(1)}, f32[2304]{0:T(1024)}, u32[]{:S(2)}) copy-start(f32[2304]{0:T(1024)} %param.42) | copy-start | bytes 27652
  0.7 8.6 %copy-start.15 = (bf16[1,4,196,768]{3,1,2,0:T(4,128)(2,1)S(1)}, bf16[1,4,196,768]{3,1,2,0:T(4,128)(2,1)}, u32[]{:S(2)}) copy-start(bf16[1,4,196,768]{3,1,2,0:T(4,128)(2,1)} %param.23) | copy-start | bytes 3612676
  3.3 7.2 %copy-start.32 = (s32[1,4]{1,0:T(1,128)S(1)}, s32[1,4]{1,0:T(1,128)}, u32[]{:S(2)}) copy-start(s32[1,4]{1,0:T(1,128)} %param.26) | copy-start | bytes 52
  3.3 7.2 %copy-start.33 = (s32[1,4]{1,0:T(1,128)S(1)}, s32[1,4]{1,0:T(1,128)}, u32[]{:S(2)}) copy-start(s32[1,4]{1,0:T(1,128)} %param.25) | copy-start | bytes 52
  3.3 187.5 %collective-permute-start.1 = (bf16[4,208,768]{2,1,0:T(8,128)(2,1)}, bf16[4,208,768]{2,1,0:T(8,128)(2,1)}, u32[]{:S(2)}, u32[]{:S(2)}) collective-permute-start(bf16[4,208,768]{2,1,0:T(8,128)(2,1)} %pad.27), channel_id=1, source_target_pairs={{2,5},{3,4},{4,3},{5,2},{10,13},{11,12},{12,11},{13,10},{18,21},{1... | collective-permute-start | bytes 3833864 | tf_op jit(solution)/shard_map/ppermute | solution.py:1030
  145.7 30.9 %copy-start.38 = (bf16[768,768]{1,0:T(8,128)(2,1)S(1)}, bf16[768,768]{1,0:T(8,128)(2,1)}, u32[]{:S(2)}) copy-start(bf16[768,768]{1,0:T(8,128)(2,1)} %get-tuple-element.45) | copy-start | bytes 3538948
  181.4 2.9 copy-start.1
  181.4 13.4 %slice-start.2 = ((s8[4718592]{0:T(1024)(128)(4,1)}), s8[4194304]{0:T(1024)(128)(4,1)S(1)}, s32[]{:S(2)}) async-start(s8[4718592]{0:T(1024)(128)(4,1)} %bitcast.86), calls=%async_computation.2 | async-start | bytes 8388608
  183.7 7.1 %copy-start.26 = (f32[832]{0:T(1024)}, f32[832]{0:T(1024)S(1)}, u32[]{:S(2)}) copy-start(f32[832]{0:T(1024)S(1)} %multiply_reduce_fusion.2) | copy-start | bytes 9988
  184.3 10.5 %slice-start.3 = ((s8[4718592]{0:T(1024)(128)(4,1)}), s8[524288]{0:T(1024)(128)(4,1)S(1)}, s32[]{:S(2)}) async-start(s8[4718592]{0:T(1024)(128)(4,1)} %bitcast.86), calls=%async_computation.3 | async-start | bytes 1048576
  184.3 39.2 %slice-start = ((s8[4718592]{0:T(1024)(128)(4,1)}), s8[4194304]{0:T(1024)(128)(4,1)S(1)}, s32[]{:S(2)}) async-start(s8[4718592]{0:T(1024)(128)(4,1)} %bitcast.84), calls=%async_computation | async-start | bytes 8388608
  190.8 32.7 %copy-start = (f32[832,3072]{1,0:T(8,128)}, f32[832,3072]{1,0:T(8,128)S(1)}, u32[]{:S(2)}) copy-start(f32[832,3072]{1,0:T(8,128)S(1)} %fusion.22) | copy-start | bytes 30670852
  194.8 28.7 %slice-start.1 = ((s8[4718592]{0:T(1024)(128)(4,1)}), s8[524288]{0:T(1024)(128)(4,1)S(1)}, s32[]{:S(2)}) async-start(s8[4718592]{0:T(1024)(128)(4,1)} %bitcast.84), calls=%async_computation.1 | async-start | bytes 1048576
  228.2 8.1 %copy-start.27 = (f32[832]{0:T(1024)S(1)}, f32[832]{0:T(1024)}, u32[]{:S(2)}) copy-start(f32[832]{0:T(1024)} %copy-done.26) | copy-start | bytes 9988
  237.3 1.3 copy-start.39
  237.8 3.1 copy-start.5
  238.6 2.3 copy-start.37
  255.0 9.7 %copy-start.2 = (f32[832,768]{1,0:T(8,128)S(1)}, f32[832,768]{1,0:T(8,128)}, u32[]{:S(2)}) copy-start(f32[832,768]{1,0:T(8,128)} %get-tuple-element.154) | copy-start | bytes 7667716
  255.0 9.7 %copy-start.4 = (bf16[832,3072]{1,0:T(8,128)(2,1)S(1)}, bf16[832,3072]{1,0:T(8,128)(2,1)}, u32[]{:S(2)}) copy-start(bf16[832,3072]{1,0:T(8,128)(2,1)} %multiply_convert_fusion) | copy-start | bytes 15335428
  255.0 9.7 %copy-start.31 = (f32[768]{0:T(1024)S(1)}, f32[768]{0:T(1024)}, u32[]{:S(2)}) copy-start(f32[768]{0:T(1024)} %get-tuple-element.115) | copy-start | bytes 9220
  264.7 7.5 %copy-start.22 = (f32[9216]{0:T(1024)S(1)}, f32[9216]{0:T(1024)}, u32[]{:S(2)}) copy-start(f32[9216]{0:T(1024)} %broadcast_dynamic-update-slice_fusion) | copy-start | bytes 110596
  264.7 7.6 %copy-start.28 = (f32[768]{0:T(1024)S(1)}, f32[768]{0:T(1024)}, u32[]{:S(2)}) copy-start(f32[768]{0:T(1024)} %get-tuple-element.137) | copy-start | bytes 9220
  440.6 9.0 %copy-start.12 = (f32[192,2304]{1,0:T(8,128)S(1)}, f32[192,2304]{1,0:T(8,128)}, u32[]{:S(2)}) copy-start(f32[192,2304]{1,0:T(8,128)} %wq.1) | copy-start | bytes 5308420
  440.6 9.0 %copy-start.13 = (f32[192,2304]{1,0:T(8,128)S(1)}, f32[192,2304]{1,0:T(8,128)}, u32[]{:S(2)}) copy-start(f32[192,2304]{1,0:T(8,128)} %param.32) | copy-start | bytes 5308420
  444.0 46.0 %collective-permute-start.2 = (bf16[4,208,768]{2,1,0:T(8,128)(2,1)S(1)}, bf16[4,208,768]{2,1,0:T(8,128)(2,1)S(1)}, u32[]{:S(2)}, u32[]{:S(2)}) collective-permute-start(bf16[4,208,768]{2,1,0:T(8,128)(2,1)S(1)} %convert_element_type.148), channel_id=1, source_target_pairs={{2,5},{3,4},{4,3},{5,2},{10,13},{11,12},{12,11},{13,10},{18,21},{1... | collective-permute-start | bytes 3833864 | tf_op jit(solution)/shard_map/ppermute | solution.py:1082
  445.9 57.7 %collective-permute-start = (bf16[832,768]{1,0:T(8,128)(2,1)}, bf16[832,768]{1,0:T(8,128)(2,1)S(1)}, u32[]{:S(2)}, u32[]{:S(2)}) collective-permute-start(bf16[832,768]{1,0:T(8,128)(2,1)} %add_convert_fusion.1), channel_id=1, source_target_pairs={{2,5},{3,4},{4,3},{5,2},{10,13},{11,12},{12,11},{13,10},{18,21},{1... | collective-permute-start | bytes 3833864 | tf_op jit(solution)/shard_map/ppermute | solution.py:1030
  449.6 5.2 %copy-start.6 = (f32[192,3072]{1,0:T(8,128)S(1)}, f32[192,3072]{1,0:T(8,128)}, u32[]{:S(2)}) copy-start(f32[192,3072]{1,0:T(8,128)} %wu.1) | copy-start | bytes 7077892
  449.6 5.2 %copy-start.7 = (f32[192,3072]{1,0:T(8,128)S(1)}, f32[192,3072]{1,0:T(8,128)}, u32[]{:S(2)}) copy-start(f32[192,3072]{1,0:T(8,128)} %param.38) | copy-start | bytes 7077892
  449.6 5.2 %copy-start.8 = (f32[192,3072]{1,0:T(8,128)S(1)}, f32[192,3072]{1,0:T(8,128)}, u32[]{:S(2)}) copy-start(f32[192,3072]{1,0:T(8,128)} %param.37) | copy-start | bytes 7077892
  449.6 5.9 %copy-start.17 = (bf16[192,3072]{1,0:T(8,128)(2,1)S(1)}, bf16[192,3072]{1,0:T(8,128)(2,1)}, u32[]{:S(2)}) copy-start(bf16[192,3072]{1,0:T(8,128)(2,1)} %get-tuple-element.58) | copy-start | bytes 3538948
  455.5 4.5 copy-start.18
  455.5 4.5 copy-start.19
  455.5 4.5 copy-start.20
  455.5 4.5 copy-start.21
  455.5 6.6 %copy-start.10 = (f32[768,768]{1,0:T(8,128)S(1)}, f32[768,768]{1,0:T(8,128)}, u32[]{:S(2)}) copy-start(f32[768,768]{1,0:T(8,128)} %param.41) | copy-start | bytes 7077892
  455.6 6.6 %copy-start.11 = (f32[768,768]{1,0:T(8,128)S(1)}, f32[768,768]{1,0:T(8,128)}, u32[]{:S(2)}) copy-start(f32[768,768]{1,0:T(8,128)} %param.40) | copy-start | bytes 7077892
  460.0 1.6 copy-start.24
  460.0 1.6 copy-start.25
  460.0 1.6 copy-start.29
  460.0 1.6 copy-start.30
  460.0 2.6 copy-start.9
  460.0 2.9 copy-start.16
  462.9 27.0 %copy-start.3 = (f32[4,208,768]{2,1,0:T(8,128)S(1)}, f32[4,208,768]{2,1,0:T(8,128)}, u32[]{:S(2)}) copy-start(f32[4,208,768]{2,1,0:T(8,128)} %get-tuple-element.55) | copy-start | bytes 7667716
  490.4 13.2 %copy-start.14 = (bf16[832,768]{1,0:T(8,128)(2,1)S(1)}, bf16[832,768]{1,0:T(8,128)(2,1)}, u32[]{:S(2)}) copy-start(bf16[832,768]{1,0:T(8,128)(2,1)} %add_convert_fusion.1) | copy-start | bytes 3833860

commit v3 on v2

v3 whole, which is shorter than its diff:
```python
import functools

import jax
import jax.numpy as jnp
import numpy as np
from jax import lax
from jax.experimental import pallas as pl
from jax.experimental.pallas import tpu as pltpu
from jax.sharding import PartitionSpec as P

D = 768
HEADS = 12
HEAD = 64
GRID = 14
STEP = 10
FRAME_TOK = 196


beta_one = 0.9
beta_two = 0.999


def sincos(values, length_out):
    half_width = length_out // 2
    frequency = 1.0 / 10000.0 ** (jnp.arange(half_width, dtype=jnp.float32) / half_width)
    angles = values[..., None] * frequency
    return jnp.concatenate([jnp.sin(angles), jnp.cos(angles)], axis=-1)


def temporal_rows(year_values, day_values):
    dates = jnp.concatenate(
        [
            sincos((year_values - 2000).astype(jnp.float32), D // 8),
            sincos(day_values.astype(jnp.float32), D // 8),
        ],
        axis=-1,
    )
    return jnp.pad(dates, ((0, 0), (3 * D // 4, 0)))


def spatial_rows():
    half = 3 * D // 16
    frequency = (1.0 / np.float32(10000.0) ** (np.arange(half, dtype=np.float32) / np.float32(half))).astype(np.float32)
    cells = np.arange(FRAME_TOK)
    parts = []
    for values in (cells // GRID, cells % GRID):
        angles = values.astype(np.float32)[:, None] * frequency
        parts += [np.sin(angles), np.cos(angles)]
    rows = np.zeros((SP, D), np.float32)
    rows[:FRAME_TOK, : 3 * D // 4] = np.concatenate(parts, axis=-1)
    return rows


def slot_items(dates_group, frames_group, mask_group):
    item_ends = jnp.cumsum(dates_group)
    starts = item_ends - dates_group
    item_index = jnp.sum((frames_group[:, None] >= item_ends[None, :]).astype(jnp.int32), axis=1)
    is_first = jnp.any(frames_group[:, None] == starts[None, :], axis=1)
    is_valid = jnp.logical_or(mask_group > 0, is_first)
    return (item_index, is_valid)


SP = 208
NK = 6
NEG = -1e30
NT = (((1,), (1,)), ((), ()))
NN = (((1,), (0,)), ((), ()))


def mm(a, b, dims=NN):
    return lax.dot_general(a, b, dims, preferred_element_type=jnp.float32)


def augmented_keys(parts, valid, bias_lane, mine):
    row = lax.broadcasted_iota(jnp.int32, (SP, 128), 0)
    lane = lax.broadcasted_iota(jnp.int32, (SP, 128), 1)
    blocks = []
    for part, live in zip(parts, valid):
        bias = jnp.where(row >= FRAME_TOK, NEG, live).astype(jnp.bfloat16)
        blocks.append(jnp.where(mine, part, jnp.where(lane == bias_lane, bias, jnp.zeros_like(part))))
    return jnp.concatenate(blocks, axis=0)


def attn_fwd_kernel(idx_ref, val_ref, q_ref, k_ref, v_ref, o_ref, lse_ref):
    lane = lax.broadcasted_iota(jnp.int32, (SP, 128), 1)

    def one(step, _):
        j, b = step // 6, step % 6
        cols = pl.ds(pl.multiple_of(b * 128, 128), 128)
        parts = [k_ref[idx_ref[j * NK + t], :, cols] for t in range(NK)]
        valid = [jnp.where(val_ref[j * NK + t] > 0, 0.0, NEG) for t in range(NK)]
        vg = jnp.concatenate([v_ref[idx_ref[j * NK + t], :, cols] for t in range(NK)], axis=0)
        q = q_ref[j, :, cols]
        scores = []
        for h in range(2):
            mine = (lane < 64) if h == 0 else (lane >= 64)
            spare = 64 if h == 0 else 0
            ka = augmented_keys(parts, valid, spare, mine)
            qa = jnp.where(mine, q, jnp.where(lane == spare, jnp.ones_like(q), jnp.zeros_like(q)))
            scores.append(mm(qa, ka, NT))
        peaks = [jnp.max(s, axis=1, keepdims=True) for s in scores]
        probs = [jnp.exp(s - m) for s, m in zip(scores, peaks)]
        sums = [jnp.sum(p, axis=1, keepdims=True) for p in probs]
        outs = [mm(p.astype(jnp.bfloat16), vg) / total for p, total in zip(probs, sums)]
        o_ref[j, :, cols] = jnp.where(lane < 64, outs[0], outs[1]).astype(jnp.bfloat16)
        logs = [m + jnp.log(total) for m, total in zip(peaks, sums)]
        lse_ref[j, b] = jnp.transpose(jnp.where(lane == 0, logs[0], logs[1]))[:8]
        return 0

    lax.fori_loop(0, 24, one, 0)


VM = pl.BlockSpec(memory_space=pltpu.VMEM)
SM = pl.BlockSpec(memory_space=pltpu.SMEM)


def attn_fwd(idx, val, q, k, v):
    return pl.pallas_call(
        attn_fwd_kernel,
        out_shape=(
            jax.ShapeDtypeStruct((4, SP, D), jnp.bfloat16),
            jax.ShapeDtypeStruct((4, 6, 8, SP), jnp.float32),
        ),
        in_specs=[SM, SM, VM, VM, VM],
        out_specs=(VM, VM),
        compiler_params=pltpu.CompilerParams(vmem_limit_bytes=60 * 2**20),
        cost_estimate=pl.CostEstimate(
            flops=2 * 2 * 24 * 12 * SP * SP * 256,
            bytes_accessed=14 * 2**20,
            transcendentals=24 * 12 * SP * SP,
        ),
        name="attn_fwd",
    )(idx, val, q, k, v)


def key_tables(item_index, is_valid, q_items):
    match = (q_items[:, None] == item_index[None, :]) & is_valid[None, :]
    rank = jnp.cumsum(match.astype(jnp.int32), axis=1) - 1
    count = jnp.sum(match.astype(jnp.int32), axis=1)
    place = jnp.arange(NK, dtype=jnp.int32)
    hit = match[:, None, :] & (rank[:, None, :] == place[None, :, None])
    slots = jnp.arange(item_index.shape[0], dtype=jnp.int32)
    idx = jnp.sum(jnp.where(hit, slots[None, None, :], 0), axis=2)
    val = (place[None, :] < count[:, None]).astype(jnp.int32)
    place_of = jnp.arange(4 * NK, dtype=jnp.int32)
    held = (idx.reshape(-1)[None, :] == slots[:, None]) & (val.reshape(-1)[None, :] > 0)
    first = jnp.min(jnp.where(held, place_of[None, :], 4 * NK), axis=1)
    last = jnp.max(jnp.where(held, place_of[None, :], -1), axis=1)
    has_first, has_last = first < 4 * NK, last > first
    rows = [jnp.where(has_first, first, 0), jnp.where(has_last, last, 0), has_first, has_last]
    return jnp.concatenate([idx.reshape(-1), val.reshape(-1)] + [r.astype(jnp.int32) for r in rows])


def adamw(weight, first_moment, second, gradient, step_rate, decay):
    first_new = beta_one * first_moment + (1.0 - beta_one) * gradient
    second_new = beta_two * second + (1.0 - beta_two) * gradient * gradient
    first_hat = first_new / (1.0 - beta_one**STEP)
    second_hat = second_new / (1.0 - beta_two**STEP)
    weight_new = weight - step_rate * (first_hat / (jnp.sqrt(second_hat) + 1e-08) + decay * weight)
    return (first_new, second_new, weight_new)


VEC_ROWS = 16
MESH = pl.DeviceIdType.MESH
Z, X, Y, DA, DB, C0, C1, C2, C3 = range(9)


def norm_rows(x):
    mean = jnp.mean(x, axis=-1, keepdims=True)
    centred = x - mean
    spread = jnp.mean(centred * centred, axis=-1, keepdims=True)
    return centred * lax.rsqrt(spread + 1e-06)


def place():
    i, f = lax.axis_index("items"), lax.axis_index("frames")
    core = i % 2
    upper = f // 2
    stay = core == upper
    mine = jnp.where(stay, f, 3 - f)
    other = f + 1 - 2 * (f % 2)
    far = jnp.where(stay, other, 3 - other)
    flip = lambda v, bit: v + bit - 2 * bit * ((v // bit) % 2)
    return i, f, core, stay, mine, other, far, flip


def halves(core, a, b):
    return jnp.where(core == 0, a, b)


def front_kernel(
    tok, tmp, vec, spatial, wq, wo, wu, wd,
    q_out, k_out, v_out, nt_out, x_out, vec_out, tmp_out, wq_out, wo_out, wu_out, wd_out,
    t_s, tmp_s, vec_s, n_s, nt_s, q_s, k_s, v_s, x_s, wq_s,
    rq32, ro32, ru32, rd32, rq, ro, ru, rd, sq32, so32, su32, sd32, sq, so, su, sd,
    t_send, t_recv, m_send, m_recv, v_send, v_recv, w_send, w_recv, reg_sem, own_sem, put_sem, loc_sem, out_sem,
):
    bf, f32 = jnp.bfloat16, jnp.float32
    i, f, core, stay, mine, other, far, flip = place()
    c_dev = (flip(i, 1), f)
    x_dev = (halves(core, flip(i, 2), flip(i, 4)), f)
    y_dev = (halves(core, flip(i, 4), flip(i, 2)), f)
    e_dev = (i, other)
    m_dev = (flip(i, 1), 3 - f)
    xy = (i // 2) % 4
    xy_x, xy_y = halves(core, flip(xy, 1), flip(xy, 2)), halves(core, flip(xy, 2), flip(xy, 1))
    diag = flip(flip(xy, 1), 2)
    zs = [flip(f, 1), flip(f, 2), flip(flip(f, 1), 2)]

    barrier = pltpu.get_barrier_semaphore()
    partners = [c_dev, x_dev, y_dev, m_dev] + [(i, z) for z in zs]
    for dev in partners:
        pl.semaphore_signal(barrier, inc=1, device_id=dev, device_id_type=MESH)

    weights = [(wq, wq_out, rq32, rq, sq32, sq), (wo, wo_out, ro32, ro, so32, so),
               (wu, wu_out, ru32, ru, su32, su), (wd, wd_out, rd32, rd, sd32, sd)]

    def region_load(w):
        src, _, r32, _, _, _ = weights[w]
        rows, cols = r32.shape
        return pltpu.make_async_copy(
            src.at[pl.ds(pl.multiple_of(xy * rows, rows), rows), pl.ds(pl.multiple_of(core * cols, 128), cols)],
            r32, reg_sem.at[w])

    def own_load(w):
        return pltpu.make_async_copy(weights[w][0], weights[w][4], own_sem.at[w])

    def own_put(w):
        out, small = weights[w][1], weights[w][5]
        rows = small.shape[0]
        return pltpu.make_async_copy(small, out.at[pl.ds(pl.multiple_of(f * rows, rows), rows), :], put_sem.at[w])

    for w in range(4):
        region_load(w).start()
    for w in range(4):
        own_load(w).start()
    tok_load = pltpu.make_async_copy(tok, t_s.at[mine], loc_sem.at[0])
    tmp_load = pltpu.make_async_copy(tmp, tmp_s.at[mine], loc_sem.at[1])
    vec_load = pltpu.make_async_copy(vec, vec_s.at[f], loc_sem.at[2])

    @pl.when(stay)
    def _():
        tok_load.start()
        tmp_load.start()

    vec_load.start()
    pl.semaphore_wait(barrier, len(partners))

    def remote(src, dst, ssem, rsem, dev):
        return pltpu.make_async_remote_copy(
            src_ref=src, dst_ref=dst, send_sem=ssem, recv_sem=rsem, device_id=dev, device_id_type=MESH)

    def tok_copy(kind, j):
        if kind == 0:
            return remote(tok.at[j], t_s.at[f, j], t_send.at[0, j], t_recv.at[0, j], m_dev)
        if kind == 3:
            return remote(t_s.at[far, j], t_s.at[far, j], t_send.at[3, j], t_recv.at[3, j], c_dev)
        return remote(t_s.at[mine, j], t_s.at[mine, j], t_send.at[kind, j], t_recv.at[kind, j],
                      c_dev if kind == 1 else e_dev)

    def tok_arrival(kind, j):
        shard = (mine, 3 - mine, far, 3 - far)[kind]
        return remote(t_s.at[shard, j], t_s.at[shard, j], t_send.at[kind, j], t_recv.at[kind, j], c_dev)

    def tmp_copy(kind):
        if kind == 0:
            return remote(tmp, tmp_s.at[f], m_send.at[0], m_recv.at[0], m_dev)
        if kind == 3:
            return remote(tmp_s.at[far], tmp_s.at[far], m_send.at[3], m_recv.at[3], c_dev)
        return remote(tmp_s.at[mine], tmp_s.at[mine], m_send.at[kind], m_recv.at[kind], c_dev if kind == 1 else e_dev)

    def tmp_arrival(kind):
        shard = (mine, 3 - mine, far, 3 - far)[kind]
        return remote(tmp_s.at[shard], tmp_s.at[shard], m_send.at[kind], m_recv.at[kind], c_dev)

    def part(w, z, at, half, piece):
        out, r = weights[w][1], weights[w][3]
        rows, cols = r.shape
        unit = rows // 3
        start = z * 4 * rows + at * rows
        if piece == 0:
            return out.at[pl.ds(pl.multiple_of(start, 16), rows), pl.ds(pl.multiple_of(half * cols, 128), cols)]
        if piece == 1:
            return out.at[pl.ds(pl.multiple_of(start, 16), 2 * unit), pl.ds(pl.multiple_of(half * cols, 128), cols)]
        return out.at[pl.ds(pl.multiple_of(start + 2 * unit, 16), unit), pl.ds(pl.multiple_of(half * cols, 128), cols)]

    def w_copy(w, d, kind):
        sems = (w_send.at[w, d, kind], w_recv.at[w, d, kind])
        z = zs[d]
        if kind == Z:
            return remote(weights[w][3], part(w, f, xy, core, 0), *sems, (i, z))
        at = {X: xy, Y: xy, DA: xy_x, DB: xy_y, C0: xy, C1: xy_x, C2: xy_y, C3: diag}[kind]
        piece = {DA: 1, DB: 2}.get(kind, 0)
        dev = {X: x_dev, Y: y_dev, DA: y_dev, DB: x_dev}.get(kind, c_dev)
        ref = part(w, z, at, core, piece)
        return remote(ref, ref, *sems, dev)

    def w_arrival(w, d, kind):
        sems = (w_send.at[w, d, kind], w_recv.at[w, d, kind])
        z = zs[d]
        at = {Z: xy, X: xy_x, Y: xy_y, DA: diag, DB: diag, C0: xy, C1: xy_y, C2: xy_x, C3: diag}[kind]
        piece = {DA: 1, DB: 2}.get(kind, 0)
        half = (1 - core) if kind >= C0 else core
        ref = part(w, z, at, half, piece)
        return remote(ref, ref, *sems, c_dev)

    def w_send_region(w):
        region_load(w).wait()
        weights[w][3][...] = weights[w][2][...].astype(bf)
        for d in range(3):
            w_copy(w, d, Z).start()

    def w_stage_one(w):
        for d in range(3):
            w_arrival(w, d, Z).wait_recv()
            for kind in (X, Y, C0):
                w_copy(w, d, kind).start()

    def w_stage_two(w):
        for d in range(3):
            w_arrival(w, d, X).wait_recv()
            w_copy(w, d, DA).start()
            w_copy(w, d, C1).start()
            w_arrival(w, d, Y).wait_recv()
            w_copy(w, d, DB).start()
            w_copy(w, d, C2).start()

    def w_stage_three(w):
        for d in range(3):
            w_arrival(w, d, DA).wait_recv()
            w_arrival(w, d, DB).wait_recv()
            w_copy(w, d, C3).start()

    def w_stage_four(w):
        for d in range(3):
            for kind in (C0, C1, C2, C3):
                w_arrival(w, d, kind).wait_recv()

    def w_own(w):
        own_load(w).wait()
        weights[w][5][...] = weights[w][4][...].astype(bf)
        own_put(w).start()

    w_send_region(0)

    @pl.when(jnp.logical_not(stay))
    def _():
        tmp_copy(0).start()
        for j in range(4):
            tok_copy(0, j).start()

    @pl.when(stay)
    def _():
        tok_load.wait()
        tmp_load.wait()
        for kind in (2, 1):
            tmp_copy(kind).start()
            for j in range(4):
                tok_copy(kind, j).start()

    vec_load.wait()
    def v_copy(d):
        return remote(vec_s.at[f], vec_s.at[f], v_send.at[d], v_recv.at[d], (i, zs[d]))
    def v_arrival(d):
        return remote(vec_s.at[zs[d]], vec_s.at[zs[d]], v_send.at[d], v_recv.at[d], (i, zs[d]))
    for d in range(3):
        v_copy(d).start()
    for w in range(4):
        w_own(w)
    w_stage_one(0)
    w_stage_two(0)
    w_stage_three(0)

    @pl.when(jnp.logical_not(stay))
    def _():
        tmp_arrival(0).wait_recv()
        for kind in (2, 1):
            tmp_copy(kind).start()
        for j in range(4):
            tok_arrival(0, j).wait_recv()
            for kind in (2, 1):
                tok_copy(kind, j).start()

    for w in (1, 2, 3):
        w_send_region(w)
    w_stage_four(0)
    own_put(0).wait()
    wq_load = pltpu.make_async_copy(wq_out, wq_s, loc_sem.at[3])
    wq_load.start()
    for d in range(3):
        v_arrival(d).wait_recv()
    vec_put = pltpu.make_async_copy(vec_s, vec_out, loc_sem.at[4])
    vec_put.start()
    tmp_put = pltpu.make_async_copy(tmp_s.at[mine], tmp_out, loc_sem.at[5])
    tmp_put.start()
    gain = vec_s[0, 0:1, :].astype(f32)
    shift = vec_s[0, 1:2, :].astype(f32)
    bias_q = vec_s[0, 2:3, :].astype(f32)
    bias_v = vec_s[1, 0:1, :].astype(f32)
    wq_load.wait()

    def normalise(shard, keep_x):
        def slot(j, _):
            x = t_s[shard, j].astype(f32) + (spatial[...] + tmp_s[shard, pl.ds(j, 1), :])
            if keep_x:
                x_s[j] = x
            n_s[shard, j] = (norm_rows(x) * gain + shift).astype(bf)
            return 0
        lax.fori_loop(0, 4, slot, 0)

    def project(shard):
        rows = n_s[shard].reshape(4 * SP, D)
        def keys(t, _):
            cols = pl.ds(pl.multiple_of(t * 256, 256), 256)
            k_s[shard, :, :, cols] = mm(rows, wq_s[:, pl.ds(pl.multiple_of(D + t * 256, 256), 256)]).astype(bf).reshape(4, SP, 256)
            v_s[shard, :, :, cols] = (mm(rows, wq_s[:, pl.ds(pl.multiple_of(2 * D + t * 256, 256), 256)])
                                      + vec_s[1, 0:1, cols].astype(f32)).astype(bf).reshape(4, SP, 256)
            return 0
        lax.fori_loop(0, 3, keys, 0)

    def project_q(shard):
        rows = n_s[shard].reshape(4 * SP, D)
        def queries(t, _):
            cols = pl.ds(pl.multiple_of(t * 256, 256), 256)
            q = (mm(rows, wq_s[:, cols]) + vec_s[0, 2:3, cols].astype(f32)).astype(bf)
            q_s[:, :, cols] = (q.astype(f32) * 0.125).astype(bf).reshape(4, SP, 256)
            return 0
        lax.fori_loop(0, 3, queries, 0)

    outs = []
    def put(src, dst):
        copy = pltpu.make_async_copy(src, dst, out_sem.at[len(outs)])
        copy.start()
        outs.append(copy)

    def put_shard(shard):
        nt_s[shard] = jnp.transpose(n_s[shard].reshape(4 * SP, D))
        put(nt_s.at[shard], nt_out.at[shard])
        put(k_s.at[shard], k_out.at[shard])
        put(v_s.at[shard], v_out.at[shard])

    normalise(mine, True)
    put(x_s, x_out)
    project_q(mine)
    put(q_s, q_out)
    project(mine)
    put_shard(mine)
    w_stage_one(1)
    tmp_arrival(1).wait_recv()
    for j in range(4):
        tok_arrival(1, j).wait_recv()
    normalise(3 - mine, False)
    project(3 - mine)
    put_shard(3 - mine)
    tmp_arrival(2).wait_recv()
    tmp_copy(3).start()
    for j in range(4):
        tok_arrival(2, j).wait_recv()
        tok_copy(3, j).start()
    w_stage_two(1)
    w_stage_one(2)
    normalise(far, False)
    project(far)
    put_shard(far)
    w_stage_one(3)
    tmp_arrival(3).wait_recv()
    for j in range(4):
        tok_arrival(3, j).wait_recv()
    normalise(3 - far, False)
    project(3 - far)
    put_shard(3 - far)
    w_stage_two(2)
    w_stage_two(3)
    for w in (1, 2, 3):
        w_stage_three(w)
    for w in (1, 2, 3):
        w_stage_four(w)
        own_put(w).wait()

    @pl.when(jnp.logical_not(stay))
    def _():
        tmp_copy(0).wait_send()
        for j in range(4):
            tok_copy(0, j).wait_send()

    for kind in (1, 2, 3):
        tmp_copy(kind).wait_send()
        for j in range(4):
            tok_copy(kind, j).wait_send()
    for d in range(3):
        v_copy(d).wait_send()
        for w in range(4):
            for kind in range(9):
                w_copy(w, d, kind).wait_send()
    vec_put.wait()
    tmp_put.wait()
    for copy in outs:
        copy.wait()


def front(tok, tmp, vec, spatial, wq, wo, wu, wd):
    bf, f32 = jnp.bfloat16, jnp.float32
    S = jax.ShapeDtypeStruct
    hb = pl.BlockSpec(memory_space=pltpu.HBM)
    regs = [(w.shape[0] // 4, w.shape[1] // 2) for w in (wq, wo, wu, wd)]
    full = [(4 * w.shape[0], w.shape[1]) for w in (wq, wo, wu, wd)]
    dma = pltpu.SemaphoreType.DMA
    return pl.pallas_call(
        front_kernel,
        out_shape=(
            S((4, SP, D), bf), S((4, 4, SP, D), bf), S((4, 4, SP, D), bf), S((4, D, 4 * SP), bf), S((4, SP, D), f32),
            S((4, VEC_ROWS, D), bf), S((8, D), f32),
        ) + tuple(S(s, bf) for s in full),
        in_specs=[hb, hb, hb, VM, hb, hb, hb, hb],
        out_specs=(hb,) * 11,
        scratch_shapes=[
            pltpu.VMEM((4, 4, SP, D), bf), pltpu.VMEM((4, 8, D), f32), pltpu.VMEM((4, VEC_ROWS, D), bf),
            pltpu.VMEM((4, 4, SP, D), bf), pltpu.VMEM((4, D, 4 * SP), bf), pltpu.VMEM((4, SP, D), bf), pltpu.VMEM((4, 4, SP, D), bf),
            pltpu.VMEM((4, 4, SP, D), bf), pltpu.VMEM((4, SP, D), f32), pltpu.VMEM(full[0], bf),
        ]
        + [pltpu.VMEM(r, f32) for r in regs] + [pltpu.VMEM(r, bf) for r in regs]
        + [pltpu.VMEM(w.shape, f32) for w in (wq, wo, wu, wd)] + [pltpu.VMEM(w.shape, bf) for w in (wq, wo, wu, wd)]
        + [dma((4, 4)), dma((4, 4)), dma((4,)), dma((4,)), dma((3,)), dma((3,)), dma((4, 3, 9)), dma((4, 3, 9)),
           dma((4,)), dma((4,)), dma((4,)), dma((6,)), dma((16,))],
        compiler_params=pltpu.CompilerParams(
            collective_id=1, has_side_effects=True, vmem_limit_bytes=62 * 2**20),
        cost_estimate=pl.CostEstimate(flops=2 * 9 * 784 * 768 * 768, bytes_accessed=40 * 2**20, transcendentals=0),
        name="front",
    )(tok, tmp, vec, spatial, wq, wo, wu, wd)


def norm_parts(x):
    centred = x - jnp.mean(x, axis=-1, keepdims=True)
    scale = lax.rsqrt(jnp.mean(centred * centred, axis=-1, keepdims=True) + 1e-06)
    return centred * scale, scale


def norm_grad(dn, unit, scale):
    return (dn - jnp.mean(dn, axis=-1, keepdims=True) - unit * jnp.mean(dn * unit, axis=-1, keepdims=True)) * scale


def mid_kernel(
    o_in, x_in, dy_in, vec, wo, wu, wd,
    y_out, dh_out, do_out, gd_out, gu_out, go_out, vp_out,
    o_s, h_s, dy_s, vec_s, wo_s, wu_s, wd_s, n_s, nt_s, a_s, du_s, mlp_s, dn_s, gd_s, gu_s, go_s, y_s, db_s, do_s, vp_s,
    bu_s, gbu_s, in_sem, out_sem,
):
    bf, f32 = jnp.bfloat16, jnp.float32
    loads = [pltpu.make_async_copy(a, b, in_sem.at[n]) for n, (a, b) in enumerate(
        [(o_in, o_s), (wo, wo_s), (vec, vec_s), (x_in, h_s), (dy_in, dy_s), (wu, wu_s), (wd, wd_s)])]
    for copy in loads:
        copy.start()
    vp_s[...] = jnp.zeros_like(vp_s)
    zero = jnp.zeros((1, D), f32)
    for n in range(4):
        loads[n].wait()
    flat = lambda ref: ref[...].reshape(4 * SP, D)

    def branch(t, _):
        cols = pl.ds(pl.multiple_of(t * 256, 256), 256)
        out = mm(flat(o_s), wo_s[:, cols]) + vec_s[1, 1:2, cols].astype(f32)
        h_s[:, :, cols] = h_s[:, :, cols] + out.reshape(4, SP, 256)
        return 0
    lax.fori_loop(0, 3, branch, 0)
    gain, shift = vec_s[1, 2:3, :].astype(f32), vec_s[2, 0:1, :].astype(f32)

    def norm(j, _):
        unit, _scale = norm_parts(h_s[j])
        n_s[j] = (unit * gain + shift).astype(bf)
        return 0
    lax.fori_loop(0, 4, norm, 0)
    nt_s[...] = jnp.transpose(flat(n_s))
    spots = [(n, (n // 3 + 8) // 3, (n // 3 + 8) % 3, (n % 3) * 256) for n in range(12)]
    for n, z, r, at in spots:
        bu_s[n, 0:1, :] = vec_s[z, r : r + 1, at : at + 256].astype(f32)
    mlp_s[...] = jnp.zeros_like(mlp_s)
    dn_s[...] = jnp.zeros_like(dn_s)
    for n in range(4, 7):
        loads[n].wait()

    def tile(n, _):
        at = pl.multiple_of(n * 256, 256)
        cols = pl.ds(at, 256)
        low = pl.ds(pl.multiple_of((n % 3) * 256, 256), 256)
        u = mm(flat(n_s), wu_s[:, cols]) + bu_s[n, 0:1, :]
        cdf = 0.5 * (1.0 + lax.erf(u * 0.7071067811865476))
        a = (u * cdf).astype(bf)
        slope = cdf + u * (jnp.exp(u * u * -0.5) * 0.3989422804014327)
        da = mm(flat(dy_s), wd_s[cols, :], NT)
        du = (da * slope).astype(bf)
        a_s[:, low] = a
        du_s[:, low] = du
        gd_s[cols, :] = mm(jnp.transpose(a), flat(dy_s)).astype(bf)
        gu_s[:, cols] = mm(nt_s[...], du).astype(bf)
        gbu_s[n, 0:1, :] = jnp.sum(du.astype(f32), axis=0, keepdims=True)

        @pl.when(n % 3 == 2)
        def _():
            start = pl.multiple_of((n // 3) * D, D)

            def add(t, _):
                out = pl.ds(pl.multiple_of(t * 256, 256), 256)
                mlp_s[:, out] += mm(a_s[...], wd_s[pl.ds(start, D), out])
                dn_s[:, out] += mm(du_s[...], wu_s[out, pl.ds(start, D)], NT)
                return 0
            lax.fori_loop(0, 3, add, 0)
        return 0
    lax.fori_loop(0, 12, tile, 0)
    for n, z, r, at in spots:
        vp_s[z, r : r + 1, at : at + 256] = gbu_s[n, 0:1, :]
    puts = []

    def put(src, dst):
        copy = pltpu.make_async_copy(src, dst, out_sem.at[len(puts)])
        copy.start()
        puts.append(copy)

    put(gd_s, gd_out)
    put(gu_s, gu_out)
    bias_down = vec_s[2, 1:2, :].astype(f32)

    def back(j, carry):
        gains, shifts, bias_o, bias_d = carry
        rows = pl.ds(pl.multiple_of(j * SP, 16), SP)
        h = h_s[j]
        y_s[j] = (h + (mlp_s[rows, :] + bias_down)).astype(bf)
        unit, scale = norm_parts(h)
        dn = dn_s[rows, :]
        gains = gains + jnp.sum(dn * unit, axis=0, keepdims=True)
        shifts = shifts + jnp.sum(dn, axis=0, keepdims=True)
        dy = dy_s[j].astype(f32)
        dh = dy + norm_grad(dn * gain, unit, scale)
        h_s[j] = dh
        db = dh.astype(bf)
        db_s[j] = db
        bias_o = bias_o + jnp.sum(db.astype(f32), axis=0, keepdims=True)
        return gains, shifts, bias_o, bias_d + jnp.sum(dy, axis=0, keepdims=True)
    gains, shifts, bias_o, bias_d = lax.fori_loop(0, 4, back, (zero,) * 4)
    put(y_s, y_out)
    put(h_s, dh_out)
    vp_s[1, 1:2, :] = bias_o
    vp_s[1, 2:3, :] = gains
    vp_s[2, 0:1, :] = shifts
    vp_s[2, 1:2, :] = bias_d
    put(vp_s, vp_out)

    def attended(t, _):
        cols = pl.ds(pl.multiple_of(t * 256, 256), 256)
        do_s[:, :, cols] = mm(flat(db_s), wo_s[cols, :], NT).astype(bf).reshape(4, SP, 256)
        return 0
    lax.fori_loop(0, 3, attended, 0)
    put(do_s, do_out)

    def out_grad(t, _):
        cols = pl.ds(pl.multiple_of(t * 256, 256), 256)
        turned = jnp.transpose(o_s[:, :, cols].reshape(4 * SP, 256))
        go_s[cols, :] = mm(turned, flat(db_s)).astype(bf)
        return 0
    lax.fori_loop(0, 3, out_grad, 0)
    put(go_s, go_out)
    for copy in puts:
        copy.wait()


def mid(o, x, dy, vec, wo, wu, wd):
    bf, f32 = jnp.bfloat16, jnp.float32
    S = jax.ShapeDtypeStruct
    hb = pl.BlockSpec(memory_space=pltpu.HBM)
    dma = pltpu.SemaphoreType.DMA
    v = lambda shape, dtype=bf: pltpu.VMEM(shape, dtype)
    rows = (4, SP, D)
    return pl.pallas_call(
        mid_kernel,
        out_shape=(S(rows, bf), S(rows, f32), S(rows, bf), S((4 * D, D), bf), S((D, 4 * D), bf), S((D, D), bf),
                   S((4, 8, D), f32)),
        in_specs=[hb] * 7,
        out_specs=(hb,) * 7,
        scratch_shapes=[
            v(rows), v(rows, f32), v(rows), v((4, VEC_ROWS, D)), v((D, D)), v((D, 4 * D)), v((4 * D, D)),
            v(rows), v((D, 4 * SP)), v((4 * SP, D)), v((4 * SP, D)), v((4 * SP, D), f32), v((4 * SP, D), f32),
            v((4 * D, D)), v((D, 4 * D)), v((D, D)), v(rows), v(rows), v(rows), v((4, 8, D), f32),
            v((12, 8, 256), f32), v((12, 8, 256), f32), dma((7,)), dma((7,)),
        ],
        compiler_params=pltpu.CompilerParams(vmem_limit_bytes=62 * 2**20),
        cost_estimate=pl.CostEstimate(flops=2 * 27 * 832 * 768 * 768, bytes_accessed=40 * 2**20, transcendentals=832 * 3072 * 2),
        name="mid",
    )(o, x, dy, vec, wo, wu, wd)


class Sums:
    AX, AY, AC0, ADA, ADB, AC1, AC2, AC3 = range(31, 39)

    def __init__(self, n_items, grads, outs, bufs, sems):
        self.grads, self.outs = grads, outs
        self.sums, self.crecv, self.r1, self.r2, self.r3, self.fin, self.ext = bufs
        self.g_send, self.g_recv, self.e_send, self.e_recv, self.half_sem, self.put_sem = sems
        i, f, core, stay, mine, other, far, flip = place()
        self.i, self.f, self.core, self.flip = i, f, core, flip
        xy = (i // 2) % 4
        self.xy, self.diag = xy, flip(flip(xy, 1), 2)
        self.xy_x, self.xy_y = halves(core, flip(xy, 1), flip(xy, 2)), halves(core, flip(xy, 2), flip(xy, 1))
        self.c_dev = (flip(i, 1), f)
        self.x_dev = (halves(core, flip(i, 2), flip(i, 4)), f)
        self.y_dev = (halves(core, flip(i, 4), flip(i, 2)), f)
        self.e_dev = (i, other)
        self.zs = [flip(f, 1), flip(f, 2), flip(flip(f, 1), 2)]
        self.extra = []
        bit = 8
        while bit < n_items:
            self.extra.append(bit)
            bit *= 2

    def greet(self):
        barrier = pltpu.get_barrier_semaphore()
        partners = [self.c_dev, self.x_dev, self.y_dev] + [(self.i, z) for z in self.zs]
        partners += [(self.flip(self.i, b), self.f) for b in self.extra]
        for dev in partners:
            pl.semaphore_signal(barrier, inc=1, device_id=dev, device_id_type=MESH)
        return lambda: pl.semaphore_wait(barrier, len(partners))

    @staticmethod
    def remote(src, dst, ssem, rsem, dev):
        return pltpu.make_async_remote_copy(
            src_ref=src, dst_ref=dst, send_sem=ssem, recv_sem=rsem, device_id=dev, device_id_type=MESH)

    def cols_of(self, w, half):
        width = self.sums[w].shape[-1]
        return pl.ds(pl.multiple_of(half * width, 128), width)

    def half_load(self, w):
        return pltpu.make_async_copy(
            self.grads[w].at[:, :, :, self.cols_of(w, self.core)], self.sums[w], self.half_sem.at[w])

    def rows_of(self, w):
        unit = self.sums[w].shape[2] // 3
        return (pl.ds(0, 2 * unit), pl.ds(2 * unit, unit))

    def copies(self, w, stage):
        s, base = self.sums[w], (0, 4, 20, 28)[stage]
        ra, rb = self.rows_of(w)
        found = []
        if stage == 0:
            for z in range(4):
                found.append((self.grads[w].at[z, :, :, self.cols_of(w, 1 - self.core)], self.crecv[w].at[z], self.c_dev))
        elif stage == 1:
            for z in range(4):
                found.append((s.at[z, self.xy_x, ra], self.r1[w].at[z, 0, ra], self.x_dev))
                found.append((s.at[z, self.diag, ra], self.r1[w].at[z, 1, ra], self.x_dev))
                found.append((s.at[z, self.xy_y, rb], self.r1[w].at[z, 0, rb], self.y_dev))
                found.append((s.at[z, self.diag, rb], self.r1[w].at[z, 1, rb], self.y_dev))
        elif stage == 2:
            for z in range(4):
                found.append((s.at[z, self.xy_y, ra], self.r2[w].at[z, ra], self.y_dev))
                found.append((s.at[z, self.xy_x, rb], self.r2[w].at[z, rb], self.x_dev))
        else:
            for d in range(3):
                found.append((s.at[self.zs[d], self.xy], self.r3[w].at[d], (self.i, self.zs[d])))
        return [self.remote(src, dst, self.g_send.at[w, base + n], self.g_recv.at[w, base + n], dev)
                for n, (src, dst, dev) in enumerate(found)]

    def region(self, w, at, half, piece):
        rows = self.sums[w].shape[2]
        unit = rows // 3
        start, count = at * rows, rows
        if piece == 1:
            count = 2 * unit
        elif piece == 2:
            start, count = start + 2 * unit, unit
        return self.outs[w].at[pl.ds(pl.multiple_of(start, 16), count), self.cols_of(w, half)]

    def a_copy(self, w, kind):
        at = {self.AX: self.xy, self.AY: self.xy, self.AC0: self.xy, self.ADA: self.xy_x, self.ADB: self.xy_y,
              self.AC1: self.xy_x, self.AC2: self.xy_y, self.AC3: self.diag}[kind]
        piece = {self.ADA: 1, self.ADB: 2}.get(kind, 0)
        dev = {self.AX: self.x_dev, self.AY: self.y_dev, self.ADA: self.y_dev, self.ADB: self.x_dev}.get(kind, self.c_dev)
        dst = self.region(w, at, self.core, piece)
        src = self.fin[w] if kind in (self.AX, self.AY, self.AC0) else dst
        return self.remote(src, dst, self.g_send.at[w, kind], self.g_recv.at[w, kind], dev)

    def a_arrival(self, w, kind):
        at = {self.AX: self.xy_x, self.AY: self.xy_y, self.ADA: self.diag, self.ADB: self.diag, self.AC0: self.xy,
              self.AC1: self.xy_y, self.AC2: self.xy_x, self.AC3: self.diag}[kind]
        piece = {self.ADA: 1, self.ADB: 2}.get(kind, 0)
        half = (1 - self.core) if kind in (self.AC0, self.AC1, self.AC2, self.AC3) else self.core
        ref = self.region(w, at, half, piece)
        return self.remote(ref, ref, self.g_send.at[w, kind], self.g_recv.at[w, kind], self.c_dev)

    def begin(self, w):
        self.half_load(w).start()
        for copy in self.copies(w, 0):
            copy.start()

    @staticmethod
    def plus(ref, where, other_ref, other_where):
        ref[where] = (ref[where].astype(jnp.float32) + other_ref[other_where].astype(jnp.float32)).astype(jnp.bfloat16)

    def step(self, w, stage):
        f32 = jnp.float32
        ra, rb = self.rows_of(w)
        plus, s, xy, xy_x, xy_y = self.plus, self.sums[w], self.xy, self.xy_x, self.xy_y
        for copy in self.copies(w, stage):
            copy.wait_recv()
        if stage == 0:
            self.half_load(w).wait()

            def one(n, _):
                plus(s, (n // 4, n % 4), self.crecv[w], (n // 4, n % 4))
                return 0
            lax.fori_loop(0, 16, one, 0)
        elif stage == 1:
            def one(z, _):
                plus(s, (z, xy, ra), self.r1[w], (z, 0, ra))
                plus(s, (z, xy_y, ra), self.r1[w], (z, 1, ra))
                plus(s, (z, xy, rb), self.r1[w], (z, 0, rb))
                plus(s, (z, xy_x, rb), self.r1[w], (z, 1, rb))
                return 0
            lax.fori_loop(0, 4, one, 0)
        elif stage == 2:
            def one(z, _):
                plus(s, (z, xy), self.r2[w], (z,))
                return 0
            lax.fori_loop(0, 4, one, 0)
        else:
            fin = self.fin[w]
            total = s[self.f, xy].astype(f32)
            for d in range(3):
                total = total + self.r3[w][d].astype(f32)
            fin[...] = total.astype(jnp.bfloat16)
            for n, b in enumerate(self.extra):
                copy = self.remote(fin, self.ext[w].at[n], self.e_send.at[w, n], self.e_recv.at[w, n],
                                   (self.flip(self.i, b), self.f))
                copy.start()
                copy.wait()
                fin[...] = (fin[...].astype(f32) + self.ext[w][n].astype(f32)).astype(jnp.bfloat16)
            pltpu.make_async_copy(fin, self.region(w, xy, self.core, 0), self.put_sem.at[w]).start()
            for kind in (self.AX, self.AY, self.AC0):
                self.a_copy(w, kind).start()
        if stage < 3:
            for copy in self.copies(w, stage + 1):
                copy.start()

    def gather_one(self, w):
        self.a_arrival(w, self.AX).wait_recv()
        self.a_copy(w, self.ADA).start()
        self.a_copy(w, self.AC1).start()
        self.a_arrival(w, self.AY).wait_recv()
        self.a_copy(w, self.ADB).start()
        self.a_copy(w, self.AC2).start()

    def gather_two(self, w):
        self.a_arrival(w, self.ADA).wait_recv()
        self.a_arrival(w, self.ADB).wait_recv()
        self.a_copy(w, self.AC3).start()

    def gather_three(self, w):
        for kind in (self.AC0, self.AC1, self.AC2, self.AC3):
            self.a_arrival(w, kind).wait_recv()
        pltpu.make_async_copy(self.fin[w], self.region(w, self.xy, self.core, 0), self.put_sem.at[w]).wait()

    def finish(self, w):
        for stage in range(4):
            for copy in self.copies(w, stage):
                copy.wait_send()
        for kind in range(self.AX, self.AC3 + 1):
            self.a_copy(w, kind).wait_send()


def sums_scratch(n_items, shapes):
    v = lambda shape: pltpu.VMEM(shape, jnp.bfloat16)
    dma = pltpu.SemaphoreType.DMA
    n_extra, n = 0, len(shapes)
    while 8 * 2**n_extra < n_items:
        n_extra += 1
    bufs = []
    for lead in ((4, 4), (4, 4), (4, 2), (4,), (3,), ()):
        bufs += [v(lead + s) for s in shapes]
    bufs += [v((n_extra,) + s) if n_extra else v((1, 16, 128)) for s in shapes]
    sems = [dma((n, 39)), dma((n, 39)), dma((n, max(n_extra, 1))), dma((n, max(n_extra, 1))), dma((n,)), dma((n,))]
    return bufs, sems


def split_refs(refs, n):
    return [refs[k * n : (k + 1) * n] for k in range(7)]


def back_kernel(
    n_items, idx_ref, val_ref, src_ref, q_in, k_in, v_in, o_in, do_in, lse_in, nt_in, wq_in, gd, gu, go,
    dq_out, part_out, gq_out, bias_out, gd_out, gu_out, go_out,
    q_s, k_s, v_s, o_s, do_s, lse_s, nt_s, wq_s, pk_s, pv_s, gq_s, bias_s, load_sem, out_sem, *rest,
):
    bf, f32 = jnp.bfloat16, jnp.float32
    net = Sums(n_items, (gd, gu, go), (gd_out, gu_out, go_out), split_refs(rest[:21], 3), rest[21:])
    ready = net.greet()
    loads = [pltpu.make_async_copy(a, b, load_sem.at[n]) for n, (a, b) in enumerate(
        [(q_in, q_s), (k_in, k_s), (v_in, v_s), (o_in, o_s), (do_in, do_s), (lse_in, lse_s), (nt_in, nt_s), (wq_in, wq_s)])]
    for copy in loads:
        copy.start()
    ready()
    for w in range(3):
        net.begin(w)
    for n in range(6):
        loads[n].wait()
    lane = lax.broadcasted_iota(jnp.int32, (SP, 128), 1)
    row = lax.broadcasted_iota(jnp.int32, (SP, D), 0)
    plan = ((2, 0, 0), (4, 1, 0), (6, 2, 0), (9, 0, 1), (14, 1, 1), (16, 2, 1), (18, 0, 2), (22, 1, 2))

    def one(step, _):
        for at, w, stage in plan:
            @pl.when(step == at)
            def _():
                net.step(w, stage)
        j, b = step // 6, step % 6
        cols = pl.ds(pl.multiple_of(b * 128, 128), 128)
        parts = [k_s[idx_ref[j * NK + t], :, cols] for t in range(NK)]
        valid = [jnp.where(val_ref[j * NK + t] > 0, 0.0, NEG) for t in range(NK)]
        kg = jnp.concatenate(parts, axis=0)
        vg = jnp.concatenate([v_s[idx_ref[j * NK + t], :, cols] for t in range(NK)], axis=0)
        kg_t = jnp.transpose(kg)
        q, do, o = q_s[j, :, cols], do_s[j, :, cols], o_s[j, :, cols]
        prod_t = jnp.transpose(do.astype(f32) * o.astype(f32))
        logs = lse_s[j, b]
        dk = jnp.zeros((NK * SP, 128), f32)
        dv = jnp.zeros((NK * SP, 128), f32)
        dq_t = []
        for h in range(2):
            mine = (lane < 64) if h == 0 else (lane >= 64)
            spare = 64 if h == 0 else 0
            ka = augmented_keys(parts, valid, spare, mine)
            qm = jnp.where(mine, q, jnp.zeros_like(q))
            qa = jnp.where(lane == spare, jnp.ones_like(q), qm)
            dom = jnp.where(mine, do, jnp.zeros_like(do))
            centre = jnp.sum(prod_t[h * 64 : (h + 1) * 64], axis=0, keepdims=True)
            s_t = mm(ka, qa, NT)
            da_t = mm(vg, dom, NT)
            p = jnp.exp(s_t - logs[h : h + 1])
            ds = (p * (da_t - centre)).astype(bf)
            dv = dv + mm(p.astype(bf), dom)
            dk = dk + mm(ds, qm)
            dq_t.append(mm(kg_t, ds))
        dq = jnp.transpose(jnp.concatenate([dq_t[0][:64], dq_t[1][64:]], axis=0))
        q_s[j, :, cols] = (dq * 0.125).astype(bf)
        for t in range(NK):
            pk_s[j * NK + t, :, cols] = dk[t * SP : (t + 1) * SP].astype(bf)
            pv_s[j * NK + t, :, cols] = dv[t * SP : (t + 1) * SP].astype(bf)
        return 0

    lax.fori_loop(0, 24, one, 0)
    puts = []

    def put(src, dst):
        copy = pltpu.make_async_copy(src, dst, out_sem.at[len(puts)])
        copy.start()
        puts.append(copy)

    put(q_s, dq_out)
    net.step(2, 2)

    def combine(slot, _):
        first, second = src_ref[slot], src_ref[16 + slot]
        keep_a = jnp.logical_and(row < FRAME_TOK, src_ref[32 + slot] > 0)
        keep_b = jnp.logical_and(row < FRAME_TOK, src_ref[48 + slot] > 0)
        for out, part in ((k_s, pk_s), (v_s, pv_s)):
            total = jnp.where(keep_a, part[first].astype(f32), 0.0) + jnp.where(keep_b, part[second].astype(f32), 0.0)
            out[slot] = total.astype(bf)
        return 0

    lax.fori_loop(0, 16, combine, 0)
    net.step(0, 3)
    for n in (6, 7):
        loads[n].wait()

    def slots(ref, shard):
        return ref[pl.ds(4 * shard, 4)].reshape(4 * SP, D)

    def partial_rows(shard, _):
        def tile(t, _):
            at = pl.multiple_of(t * 256, 256)
            keys = mm(slots(k_s, shard), wq_s[pl.ds(at, 256), D : 2 * D], NT)
            values = mm(slots(v_s, shard), wq_s[pl.ds(at, 256), 2 * D :], NT)
            pk_s[pl.ds(4 * shard, 4), :, pl.ds(at, 256)] = (keys + values).astype(bf).reshape(4, SP, 256)
            return 0
        lax.fori_loop(0, 3, tile, 0)
        return 0

    lax.fori_loop(0, 2, partial_rows, 0)
    net.step(1, 3)
    net.step(2, 3)
    lax.fori_loop(2, 4, partial_rows, 0)
    put(pk_s.at[pl.ds(0, 16)], part_out)
    net.gather_one(0)
    mine = place()[4]

    def grad_q(t, _):
        cols = pl.ds(pl.multiple_of(t * 256, 256), 256)
        g = mm(nt_s[mine], q_s[:, :, cols].reshape(4 * SP, 256))
        gq_s[:, :, :, cols] = g.astype(bf).reshape(4, 4, D // 16, 256)
        return 0
    lax.fori_loop(0, 3, grad_q, 0)

    def grad_kv(t, _):
        cols = pl.ds(pl.multiple_of((t % 3) * 256, 256), 256)
        for at, ref in ((0, k_s), (1, v_s)):
            @pl.when(t // 3 == at)
            def _():
                g = jnp.zeros((D, 256), f32)
                for s in range(4):
                    g = g + mm(nt_s[s], ref[4 * s : 4 * s + 4, :, cols].reshape(4 * SP, 256))
                gq_s[:, :, :, pl.ds(pl.multiple_of(D + t * 256, 256), 256)] = g.astype(bf).reshape(4, 4, D // 16, 256)
        return 0
    lax.fori_loop(0, 3, grad_kv, 0)
    net.gather_one(1)
    net.gather_two(0)
    lax.fori_loop(3, 6, grad_kv, 0)
    put(gq_s, gq_out)
    net.gather_one(2)

    def bias_sums(slot, carry):
        bias_q, bias_v = carry
        bias_v = bias_v + jnp.sum(v_s[slot].astype(f32), axis=0, keepdims=True)
        return bias_q, bias_v
    zero = jnp.zeros((1, D), f32)
    bias_q, bias_v = lax.fori_loop(0, 16, bias_sums, (zero, zero))
    for j in range(4):
        bias_q = bias_q + jnp.sum(q_s[j].astype(f32), axis=0, keepdims=True)
    bias_s[0:1, :] = bias_q
    bias_s[1:2, :] = bias_v
    bias_s[2:8, :] = jnp.zeros((6, D), f32)
    put(bias_s, bias_out)
    net.gather_two(1)
    net.gather_two(2)
    for w in range(3):
        net.gather_three(w)
    for w in range(3):
        net.finish(w)
    for copy in puts:
        copy.wait()


def back(n_items, idx, val, src, q, k, v_, o, do, lse, nt, wq, gd, gu, go):
    bf, f32 = jnp.bfloat16, jnp.float32
    S = jax.ShapeDtypeStruct
    hb = pl.BlockSpec(memory_space=pltpu.HBM)
    dma = pltpu.SemaphoreType.DMA
    v = lambda shape, dtype=bf: pltpu.VMEM(shape, dtype)
    rows = (4, SP, D)
    bufs, sems = sums_scratch(n_items, [(g.shape[2], g.shape[3] // 2) for g in (gd, gu, go)])
    return pl.pallas_call(
        functools.partial(back_kernel, n_items),
        out_shape=(S(rows, bf), S((16, SP, D), bf), S((4, 4, D // 16, 3 * D), bf), S((8, D), f32))
        + tuple(S((4 * g.shape[2], g.shape[3]), bf) for g in (gd, gu, go)),
        in_specs=[SM, SM, SM] + [hb] * 11,
        out_specs=(hb,) * 7,
        scratch_shapes=[
            v(rows), v((16, SP, D)), v((16, SP, D)), v(rows), v(rows), v((4, 6, 8, SP), f32), v((4, D, 4 * SP)),
            v((D, 3 * D)), v((24, SP, D)), v((24, SP, D)), v((4, 4, D // 16, 3 * D)), v((8, D), f32), dma((8,)), dma((4,)),
        ] + bufs + sems,
        compiler_params=pltpu.CompilerParams(
            collective_id=3, has_side_effects=True, vmem_limit_bytes=63 * 2**20),
        cost_estimate=pl.CostEstimate(
            flops=2 * 5 * 24 * 12 * SP * SP * 256, bytes_accessed=60 * 2**20, transcendentals=24 * 12 * SP * SP),
        name="back",
    )(idx, val, src, q, k, v_, o, do, lse, nt, wq, gd, gu, go)


def tail_kernel(
    n_items, gq, part, dq, x_in, dh, wq, vec, vp, bias,
    tg_out, vec_out, gq_out,
    dq_s, x_s, dh_s, wq_s, vec_s, vp_s, bias_s, mine_s, far_mine_s, far_s, near_s, far_e, vb_s,
    load_sem, out_sem, p_send, p_recv, vb_send, vb_recv, *rest,
):
    bf, f32 = jnp.bfloat16, jnp.float32
    net = Sums(n_items, (gq,), (gq_out,), split_refs(rest[:7], 1), rest[7:])
    i, f, core, stay, mine, other, far, flip = place()
    ready = net.greet()
    loads = [pltpu.make_async_copy(a, b, load_sem.at[n]) for n, (a, b) in enumerate(
        [(part.at[far], far_mine_s), (dq, dq_s), (wq.at[:, pl.ds(0, D)], wq_s), (part.at[mine], mine_s), (vec, vec_s),
         (vp, vp_s), (bias, bias_s), (x_in, x_s), (dh, dh_s)])]
    for copy in loads:
        copy.start()
    ready()

    def far_copy(j):
        return net.remote(part.at[3 - far, j], far_s.at[j], p_send.at[0, j], p_recv.at[0, j], net.c_dev)

    def near_copy(j):
        return net.remote(part.at[3 - mine, j], near_s.at[j], p_send.at[1, j], p_recv.at[1, j], net.c_dev)

    def chip_copy(j):
        return net.remote(far_mine_s.at[j], far_e.at[j], p_send.at[2, j], p_recv.at[2, j], net.e_dev)

    for j in range(4):
        far_copy(j).start()
    net.begin(0)
    for j in range(4):
        near_copy(j).start()
    loads[0].wait()
    for j in range(4):
        far_copy(j).wait_recv()
        net.plus(far_mine_s, (j,), far_s, (j,))
        chip_copy(j).start()
    net.step(0, 0)
    for n in range(1, 9):
        loads[n].wait()
    zero = jnp.zeros((1, D), f32)
    gain = vec_s[0, 0:1, :].astype(f32)
    vp_s[0, 2:3, :] = bias_s[0:1, :]
    vp_s[1, 0:1, :] = bias_s[1:2, :]

    def norm_back(j, carry):
        gains, shifts = carry
        near_copy(j).wait_recv()
        dn = mm(dq_s[j], wq_s[...], NT) + mine_s[j].astype(f32) + near_s[j].astype(f32)
        unit, scale = norm_parts(x_s[j])
        chip_copy(j).wait_recv()
        dn = dn + far_e[j].astype(f32)
        gains = gains + jnp.sum(dn * unit, axis=0, keepdims=True)
        shifts = shifts + jnp.sum(dn, axis=0, keepdims=True)
        x_s[j] = dh_s[j] + norm_grad(dn * gain, unit, scale)
        return gains, shifts

    def slot_out(j):
        return pltpu.make_async_copy(x_s.at[j], tg_out.at[j], out_sem.at[j])

    carry = (zero, zero)
    for j in range(4):
        if j == 2:
            net.step(0, 1)
        carry = norm_back(j, carry)
        slot_out(j).start()
    vp_s[0, 0:1, :] = carry[0]
    vp_s[0, 1:2, :] = carry[1]
    ring = [net.c_dev, net.x_dev, net.y_dev, (i, net.zs[0]), (i, net.zs[1])] + [(flip(i, b), f) for b in net.extra]

    def v_copy(n):
        return net.remote(vp_s, vb_s.at[n], vb_send.at[n], vb_recv.at[n], ring[n])

    def v_step(n):
        v_copy(n).wait()
        vp_s[...] = vp_s[...] + vb_s[n]
        if n + 1 < len(ring):
            v_copy(n + 1).start()

    v_copy(0).start()
    net.step(0, 2)
    v_step(0)
    v_step(1)
    net.step(0, 3)
    v_step(2)
    net.gather_one(0)
    v_step(3)
    net.gather_two(0)
    for n in range(4, len(ring)):
        v_step(n)
    vec_put = pltpu.make_async_copy(vp_s.at[f], vec_out, out_sem.at[4])
    vec_put.start()
    net.gather_three(0)
    net.finish(0)
    for j in range(4):
        far_copy(j).wait_send()
        near_copy(j).wait_send()
        chip_copy(j).wait_send()
        slot_out(j).wait()
    vec_put.wait()


def tail(n_items, gq, part, dq, x_in, dh, wq, vec, vp, bias):
    bf, f32 = jnp.bfloat16, jnp.float32
    S = jax.ShapeDtypeStruct
    hb = pl.BlockSpec(memory_space=pltpu.HBM)
    dma = pltpu.SemaphoreType.DMA
    v = lambda shape, dtype=bf: pltpu.VMEM(shape, dtype)
    rows = (4, SP, D)
    bufs, sems = sums_scratch(n_items, [(gq.shape[2], gq.shape[3] // 2)])
    steps = 5
    while 2 ** (steps - 2) < n_items:
        steps += 1
    return pl.pallas_call(
        functools.partial(tail_kernel, n_items),
        out_shape=(S(rows, f32), S((8, D), f32), S((D // 4, 3 * D), bf)),
        in_specs=[hb] * 9,
        out_specs=(hb,) * 3,
        scratch_shapes=[
            v(rows), v(rows, f32), v(rows, f32), v((D, D)), v((4, VEC_ROWS, D)), v((4, 8, D), f32), v((8, D), f32),
            v(rows), v(rows), v(rows), v(rows), v(rows), v((steps, 4, 8, D), f32),
            dma((9,)), dma((5,)), dma((3, 4)), dma((3, 4)), dma((steps,)), dma((steps,)),
        ] + bufs + sems,
        compiler_params=pltpu.CompilerParams(
            collective_id=2, has_side_effects=True, vmem_limit_bytes=60 * 2**20),
        cost_estimate=pl.CostEstimate(flops=2 * 14 * 784 * 768 * 768, bytes_accessed=60 * 2**20, transcendentals=0),
        name="tail",
    )(gq, part, dq, x_in, dh, wq, vec, vp, bias)


def on_device(
    tokens,
    cotangent,
    date_year,
    date_day,
    item_dates,
    slot_frame,
    frame_mask,
    qkv_weight,
    qkv_first,
    qkv_second,
    out_weight,
    out_first,
    out_second,
    up_weight,
    up_first,
    up_second,
    down_weight,
    down_first,
    down_second,
    vectors,
    vector_first,
    vector_second,
):
    bf, f32 = jnp.bfloat16, jnp.float32
    n_items = lax.axis_size("items")
    i, f, core, stay, mine, other, far, flip = place()
    swap = []
    for k in range(n_items):
        for z in range(4):
            if k % 2 != z // 2:
                swap.append((k * 4 + z, (k ^ 1) * 4 + 3 - z))

    def to_worker(array):
        return jnp.where(stay, array, lax.ppermute(array, ("items", "frames"), swap))

    pad = lambda a: jnp.pad(a[0], ((0, 0), (0, SP - FRAME_TOK), (0, 0)))
    item_index, is_valid = slot_items(item_dates[0], slot_frame[0], frame_mask[0])
    own_items = lax.dynamic_slice_in_dim(item_index, f * 4, 4)
    tables = key_tables(item_index, is_valid, own_items).astype(f32)
    tmp = jnp.concatenate([temporal_rows(date_year[0], date_day[0]), jnp.pad(tables[None], ((0, 3), (0, D - tables.shape[0])))])
    vec = jnp.pad(vectors.astype(bf).reshape(3, D), ((0, VEC_ROWS - 3), (0, 0)))
    q3, k4, v4, nt, x3, vec_all, tmp_own, wq, wo, wu, wd = front(
        pad(tokens), tmp, vec, jnp.asarray(spatial_rows()), qkv_weight, out_weight, up_weight, down_weight)
    tables = tmp_own[4, : 8 * NK + 64].astype(jnp.int32)
    idx, val, src = tables[: 4 * NK], tables[4 * NK : 8 * NK], tables[8 * NK :]
    k3, v3 = k4.reshape(16, SP, D), v4.reshape(16, SP, D)
    o3, lse = attn_fwd(idx, val, q3, k3, v3)
    block_out, hidden_grad, do3, down_grad, up_grad, out_grad, vector_part = mid(
        o3, x3, to_worker(pad(cotangent)), vec_all, wo, wu, wd)
    block_out = to_worker(block_out)
    blocks = lambda g: g.reshape(4, 4, g.shape[0] // 16, g.shape[1])
    dq3, part, gq, bias_part, down_sum, up_sum, out_sum = back(
        n_items, idx, val, src, q3, k3, v3, o3, do3, lse, nt, wq, blocks(down_grad), blocks(up_grad), blocks(out_grad))
    token_grad, vector_sum, qkv_sum = tail(
        n_items, gq, part.reshape(4, 4, SP, D), dq3, x3, hidden_grad, wq, vec_all, vector_part, bias_part)
    token_grad = jnp.where(
        stay, token_grad, lax.ppermute(token_grad.astype(bf), ("items", "frames"), swap).astype(f32))
    qkv_new = adamw(qkv_weight, qkv_first, qkv_second, qkv_sum.astype(f32), 0.05, 0.05)
    out_new = adamw(out_weight, out_first, out_second, out_sum.astype(f32), 0.5, 0.05)
    up_new = adamw(up_weight, up_first, up_second, up_sum.astype(f32), 0.05, 0.05)
    down_new = adamw(down_weight, down_first, down_second, down_sum.astype(f32), 0.03, 0.05)
    vector_new = adamw(vectors, vector_first, vector_second, vector_sum[:3].reshape(3 * D), 0.3, 0.0)
    cut = lambda a: a.reshape(1, 4, SP, D)[:, :, :FRAME_TOK]
    return (cut(block_out), cut(token_grad)) + qkv_new + out_new + up_new + down_new + vector_new


def solution(mesh):
    placed = (
        P("items", "frames", None, None),
        P("items", "frames", None, None),
        P("items", "frames"),
        P("items", "frames"),
        P("items", None),
        P("items", None),
        P("items", None),
        P("frames", None),
        P("frames", None),
        P("frames", None),
        P("frames", None),
        P("frames", None),
        P("frames", None),
        P("frames", None),
        P("frames", None),
        P("frames", None),
        P("frames", None),
        P("frames", None),
        P("frames", None),
        P("frames"),
        P("frames"),
        P("frames"),
    )
    return jax.shard_map(
        on_device,
        mesh=mesh,
        in_specs=placed,
        out_specs=(
            P("items", "frames", None, None),
            P("items", "frames", None, None),
            P("frames", None),
            P("frames", None),
            P("frames", None),
            P("frames", None),
            P("frames", None),
            P("frames", None),
            P("frames", None),
            P("frames", None),
            P("frames", None),
            P("frames", None),
            P("frames", None),
            P("frames", None),
            P("frames"),
            P("frames"),
            P("frames"),
        ),
        check_vma=False,
    )
```

time: 515 us -> 433 us (0.84); the launches traced: 506 us -> 429 us
  matrix products: 74.7 us -> 0 us
  Pallas kernels: 330 us -> 371 us
  waiting for transfers between devices: 33.7 us -> 7.78 us
  other arithmetic: 40.7 us -> 27.3 us
    pallas_call x1 -> x2, Pallas kernels: 55.3 us -> 154 us  [the longest x1 105 us: back(): pl.pallas_call(functools.partial(back_kernel, n_items), out_shape=(S(rows...]
    dot_general x9 -> x0, matrix products: 74.7 us -> none  [mm(): return lax.dot_general(a, b, dims, preferred_element_type=jnp.float32)]
    pallas_call x1, Pallas kernels: 112 us -> 54.5 us  [tail(): pl.pallas_call(functools.partial(tail_kernel, n_items), out_shape=(S(rows...]
    ppermute x1, waiting for transfers between devices: 22.9 us -> 7.77 us  [on_device(): lax.ppermute(token_grad.astype(bf), ('items', 'frames'), swap).astype(f32)]
    convert_element_type x3 -> x2, other arithmetic: 12.4 us -> 0.69 us  [the longest x1 0.68 us: on_device(): tables = tmp_own[4, :8 * NK + 64].astype(jnp.int32)]
    ppermute x2, waiting for transfers between devices: 10.9 us -> 0.01 us  [to_worker(): lax.ppermute(array, ('items', 'frames'), swap)]
    reduce_sum x4 -> x0, other arithmetic: 7.62 us -> none  [the longest x1 3.93 us: on_device(): bias_down_grad = jnp.sum(grad_out, axis=0)]
  transfers between devices with their start and end apart: 3 -> 3, of which waited for: 2 -> 1; matrix products, arithmetic and copies ran while one was open for 8% -> 7% of each run, Pallas kernels for 32% -> 75%
where the time goes in v3:
time: 433 us; the launch traced here: 429 us
  Pallas kernels  371 us (86%)
  other arithmetic  27.3 us (6%)
  local copies, waits for them, and re-layouts  13.2 us (3%)
  starting transfers between devices  8.83 us (2%)
  waiting for transfers between devices  7.78 us (2%)
    pallas_call x1, Pallas kernels, front(): pl.pallas_call(front_kernel, out_shape=(S((4, SP, D), bf), S((4, 4, SP, D...  132 us
    pallas_call x1, Pallas kernels, back(): pl.pallas_call(functools.partial(back_kernel, n_items), out_shape=(S(rows...  105 us
    pallas_call x1, Pallas kernels, tail(): pl.pallas_call(functools.partial(tail_kernel, n_items), out_shape=(S(rows...  54.5 us
    pallas_call x1, Pallas kernels, mid(): pl.pallas_call(mid_kernel, out_shape=(S(rows, bf), S(rows, f32), S(rows,...  48.4 us
    pallas_call x1, Pallas kernels, attn_fwd(): pl.pallas_call(attn_fwd_kernel, out_shape=(jax.ShapeDtypeStruct((4, SP, D...  30.7 us
    sub x5, other arithmetic, adamw(): weight - step_rate * (first_hat / (jnp.sqrt(second_hat) + 1e-08) + decay...  15.8 us
  transfers between devices with their start and end apart: 3, of which 1 were waited for; matrix products, arithmetic and copies ran while one was open for 7% of the time, Pallas kernels for 75%

profile of v3, /device:TPU:13, one launch (start us, length us, event | category | flops | bytes accessed | tf_op | source)
XLA Modules:
  0.0 429.3 jit_solution(2771704281213272999)
XLA Ops:
  0.7 1.5 copy.52
  2.2 1.1 pad.23
  3.3 3.8 collective-permute-start
  7.1 0.2 reduce-window.4
  7.3 0.1 compare_reduce_fusion
  7.4 0.1 convert_reduce_fusion
  7.6 0.2 convert_reduce_fusion.1
  7.8 0.2 reduce_window_sum.18
  8.0 0.2 select_reduce_fusion
  8.1 0.1 copy.45
  8.2 0.1 concatenate.33
  8.5 0.1 gt.32
  8.6 0.1 select_reduce_fusion.1
  8.8 0.1 copy.53
  8.9 1.1 pad.19.tok
  10.0 0.1 concatenate.34
  10.1 0.1 concatenate.41
  10.3 0.6 pad.22.vec
  10.9 0.1 multiply_sine_fusion.1
  11.1 0.6 select_maximum_fusion.tmp
  11.7 132.0 %front.1 = (bf16[4,208,768]{2,1,0:T(8,128)(2,1)}, bf16[4,4,208,768]{3,2,1,0:T(8,128)(2,1)}, bf16[4,4,208,768]{3,2,1,0:T(8,128)(2,1)}, bf16[4,768,832]{2,1,0:T(8,...) custom-call(bf16[4,208,768]{2,1,0:T(8,128)(2,1)} %pad.19.tok, ...), custom_call_target="tpu_custom_call" | custom-call | flops 8323596288 | bytes 41943040 | tf_op jit(solution)/shard_map/front/pallas_call | solution.py:508
  143.7 0.7 slice_convert_fusion
  144.4 0.6 slice_bitcast_fusion.1
  145.0 0.6 slice_bitcast_fusion.src_ref
  145.5 30.7 %attn_fwd.1 = (bf16[4,208,768]{2,1,0:T(8,128)(2,1)}, f32[4,6,8,208]{3,2,1,0:T(8,128)}) custom-call(s32[24]{0:T(128)} %get-tuple-element.135.idx_ref, s32[24]{0:T(128)} %get-tuple-element.134.val_ref, bf16[4,208,768]{2,1,0:T(8,128)(2,1)} %get-tuple-element.48.q_ref.q_in, bf16[16,208,768]{2,1,0:T(8,128)(2,1)} %bitcast.55, bf16[16,208,768]{2,1,0:T(8,128)(2,1)} %bitcast.57), custom_call_target="tpu_custom_call" | custom-call | flops 12759072768 | bytes 14680064 | tf_op jit(solution)/shard_map/attn_fwd/pallas_call | solution.py:118
  176.3 2.6 broadcast_select_fusion.dy_in
  178.9 48.4 %mid.1 = (bf16[4,208,768]{2,1,0:T(8,128)(2,1)}, f32[4,208,768]{2,1,0:T(8,128)}, bf16[4,208,768]{2,1,0:T(8,128)(2,1)}, bf16[3072,768]{1,0:T(8,128)(2,1)}, bf16[76...) custom-call(bf16[4,208,768]{2,1,0:T(8,128)(2,1)} %get-tuple-element.51.o_in, ...), custom_call_target="tpu_custom_call" | custom-call | flops 26499612672 | bytes 41943040 | tf_op jit(solution)/shard_map/mid/pallas_call | solution.py:672
  227.4 1.9 collective-permute-start.1
  229.3 105.3 %back.1 = (bf16[4,208,768]{2,1,0:T(8,128)(2,1)}, bf16[16,208,768]{2,1,0:T(8,128)(2,1)}, bf16[4,4,48,2304]{3,2,1,0:T(8,128)(2,1)}, f32[8,768]{1,0:T(8,128)}, bf16...) custom-call(s32[24]{0:T(128)} %get-tuple-element.135.idx_ref, ...), custom_call_target="tpu_custom_call" | custom-call | flops 31897681920 | bytes 62914560 | tf_op jit(solution)/shard_map/back/pallas_call | solution.py:1047
  334.7 54.5 %tail.1 = (f32[4,208,768]{2,1,0:T(8,128)}, f32[8,768]{1,0:T(8,128)}, bf16[192,2304]{1,0:T(8,128)(2,1)}) custom-call(bf16[4,4,48,2304]{3,2,1,0:T(8,128)(2,1)} %get-tuple-element.65.gq, bf16[4,4,208,768]{3,2,1,0:T(8,128)(2,1)} %bitcast.59, bf16[4,208,768]{2,1,0:T(8,128)(2,1)} %get-tuple-element.67.dq, f32[4,208,768]{2,1,0:T(8,128)} %get-tuple-element.52.x_in, ...), custom_call_target="tpu_custom_call" | custom-call | flops 12947816448 | bytes 62914560 | tf_op jit(solution)/shard_map/tail/pallas_call | solution.py:1177
  389.2 3.1 convert_element_type.115
  392.3 3.2 collective-permute-start.2
  395.5 0.6 reshape.297
  396.2 5.1 %multiply_subtract_fusion.2 = (f32[192,2304]{1,0:T(8,128)}, f32[192,2304]{1,0:T(8,128)}, f32[192,2304]{1,0:T(8,128)}) fusion(f32[192,2304]{1,0:T(8,128)S(1)} %copy-done.7, bf16[192,2304]{1,0:T(8,128)(2,1)} %get-tuple-element.72, f32[192,2304]{1,0:T(8,128)S(1)} %copy-done.8, f32[192,2304]{1,0:T(8,128)} %param.31), kind=kLoop, calls=%fused_computation.15 | loop fusion | flops 7077888 | bytes 11501568 | tf_op jit(solution)/shard_map/sub | solution.py:159
  401.3 1.5 multiply_subtract_fusion.3
  402.8 0.8 copy-done.1
  403.6 0.3 copy-done.12
  404.0 4.4 %multiply_subtract_fusion = (f32[768,768]{1,0:T(8,128)}, f32[768,768]{1,0:T(8,128)}, f32[768,768]{1,0:T(8,128)}) fusion(f32[768,768]{1,0:T(8,128)S(1)} %copy-done.1, bf16[768,768]{1,0:T(8,128)(2,1)S(1)} %copy-done.12, f32[768,768]{1,0:T(8,128)S(1)} %copy-done.2, f32[768,768]{1,0:T(8,128)S(1)} %copy-done.3), kind=kLoop, calls=%fused_computation.10 | loop fusion | flops 9437184 | bytes 15335424 | tf_op jit(solution)/shard_map/sub | solution.py:159
  408.4 0.6 multiply_subtract_fusion.4
  409.0 0.6 copy-done.6
  409.6 0.3 copy-done.11
  409.9 4.2 multiply_subtract_fusion.1
  414.1 1.4 select_bitcast_fusion.1
  415.6 1.5 copy.48
  417.1 7.8 %collective-permute-done.2 = bf16[4,208,768]{2,1,0:T(8,128)(2,1)} collective-permute-done((bf16[4,208,768]{2,1,0:T(8,128)(2,1)}, bf16[4,208,768]{2,1,0:T(8,128)(2,1)}, u32[]{:S(2)}, u32[]{:S(2)}) %collective-permute-start.2) | collective-permute-done | bytes 1277984 | tf_op jit(solution)/shard_map/ppermute | solution.py:1251
  424.9 1.6 select_bitcast_fusion
  426.5 0.2 slice.41
  426.7 2.4 copy.49
  (71 shorter events, 0.6 us)
Async XLA Ops:
  0.7 6.4 %copy-start.25 = (s32[1,3]{1,0:T(1,128)S(1)}, s32[1,3]{1,0:T(1,128)}, u32[]{:S(2)}) copy-start(s32[1,3]{1,0:T(1,128)} %param.27) | copy-start | bytes 40
  0.7 6.6 %copy-start.26 = (s32[1,16]{1,0:T(1,128)S(1)}, s32[1,16]{1,0:T(1,128)}, u32[]{:S(2)}) copy-start(s32[1,16]{1,0:T(1,128)} %param.28) | copy-start | bytes 196
  0.7 6.8 %copy-start.27 = (s32[1,16]{1,0:T(1,128)S(1)}, s32[1,16]{1,0:T(1,128)}, u32[]{:S(2)}) copy-start(s32[1,16]{1,0:T(1,128)} %param.29) | copy-start | bytes 196
  0.7 8.0 %copy-start.10 = (bf16[1,4,196,768]{3,1,2,0:T(4,128)(2,1)S(1)}, bf16[1,4,196,768]{3,1,2,0:T(4,128)(2,1)}, u32[]{:S(2)}) copy-start(bf16[1,4,196,768]{3,1,2,0:T(4,128)(2,1)} %param.23) | copy-start | bytes 3612676
  3.3 173.0 %collective-permute-start = (bf16[4,208,768]{2,1,0:T(8,128)(2,1)}, bf16[4,208,768]{2,1,0:T(8,128)(2,1)}, u32[]{:S(2)}, u32[]{:S(2)}) collective-permute-start(bf16[4,208,768]{2,1,0:T(8,128)(2,1)} %pad.23), channel_id=1, source_target_pairs={{2,5},{3,4},{4,3},{5,2},{10,13},{11,12},{12,11},{13,10},{18,21},{1... | collective-permute-start | bytes 3833864 | tf_op jit(solution)/shard_map/ppermute | solution.py:1228
  8.7 1.5 copy-start.17
  8.7 2.1 copy-start.23
  8.8 2.1 copy-start.24
  227.4 186.7 %collective-permute-start.1 = (bf16[4,208,768]{2,1,0:T(8,128)(2,1)}, bf16[4,208,768]{2,1,0:T(8,128)(2,1)}, u32[]{:S(2)}, u32[]{:S(2)}) collective-permute-start(bf16[4,208,768]{2,1,0:T(8,128)(2,1)} %get-tuple-element.57), channel_id=1, source_target_pairs={{2,5},{3,4},{4,3},{5,2},{10,13},{11,12},{12,11},{13,10},{18,21},{1... | collective-permute-start | bytes 3833864 | tf_op jit(solution)/shard_map/ppermute | solution.py:1228
  389.1 6.4 %copy-start.22 = (f32[8,768]{1,0:T(8,128)S(1)}, f32[8,768]{1,0:T(8,128)}, u32[]{:S(2)}) copy-start(f32[8,768]{1,0:T(8,128)} %get-tuple-element.76) | copy-start | bytes 73732
  389.1 7.0 %copy-start.7 = (f32[192,2304]{1,0:T(8,128)S(1)}, f32[192,2304]{1,0:T(8,128)}, u32[]{:S(2)}) copy-start(f32[192,2304]{1,0:T(8,128)} %wq.1) | copy-start | bytes 5308420
  389.1 7.0 %copy-start.8 = (f32[192,2304]{1,0:T(8,128)S(1)}, f32[192,2304]{1,0:T(8,128)}, u32[]{:S(2)}) copy-start(f32[192,2304]{1,0:T(8,128)} %param.32) | copy-start | bytes 5308420
  392.3 32.6 %collective-permute-start.2 = (bf16[4,208,768]{2,1,0:T(8,128)(2,1)}, bf16[4,208,768]{2,1,0:T(8,128)(2,1)}, u32[]{:S(2)}, u32[]{:S(2)}) collective-permute-start(bf16[4,208,768]{2,1,0:T(8,128)(2,1)} %convert_element_type.115), channel_id=1, source_target_pairs={{2,5},{3,4},{4,3},{5,2},{10,13},{11,12},{12,11},{13,10},{18,21},{1... | collective-permute-start | bytes 3833864 | tf_op jit(solution)/shard_map/ppermute | solution.py:1251
  396.1 5.2 %copy-start.13 = (f32[192,768]{1,0:T(8,128)S(1)}, f32[192,768]{1,0:T(8,128)}, u32[]{:S(2)}) copy-start(f32[192,768]{1,0:T(8,128)} %wo.1) | copy-start | bytes 1769476
  396.1 5.2 %copy-start.14 = (f32[192,768]{1,0:T(8,128)S(1)}, f32[192,768]{1,0:T(8,128)}, u32[]{:S(2)}) copy-start(f32[192,768]{1,0:T(8,128)} %param.35) | copy-start | bytes 1769476
  396.1 5.2 %copy-start.15 = (f32[192,768]{1,0:T(8,128)S(1)}, f32[192,768]{1,0:T(8,128)}, u32[]{:S(2)}) copy-start(f32[192,768]{1,0:T(8,128)} %param.34) | copy-start | bytes 1769476
  396.1 5.2 %copy-start.16 = (bf16[192,768]{1,0:T(8,128)(2,1)S(1)}, bf16[192,768]{1,0:T(8,128)(2,1)}, u32[]{:S(2)}) copy-start(bf16[192,768]{1,0:T(8,128)(2,1)} %get-tuple-element.73) | copy-start | bytes 884740
  396.1 6.7 %copy-start.2 = (f32[768,768]{1,0:T(8,128)S(1)}, f32[768,768]{1,0:T(8,128)}, u32[]{:S(2)}) copy-start(f32[768,768]{1,0:T(8,128)} %param.41) | copy-start | bytes 7077892
  396.2 6.7 %copy-start.3 = (f32[768,768]{1,0:T(8,128)S(1)}, f32[768,768]{1,0:T(8,128)}, u32[]{:S(2)}) copy-start(f32[768,768]{1,0:T(8,128)} %param.40) | copy-start | bytes 7077892
  401.3 2.3 copy-start.1
  401.3 2.6 copy-start.12
  403.9 4.4 %copy-start.18 = (f32[2304]{0:T(1024)S(1)}, f32[2304]{0:T(1024)}, u32[]{:S(2)}) copy-start(f32[2304]{0:T(1024)} %param.42) | copy-start | bytes 27652
  403.9 4.4 %copy-start.19 = (f32[2304]{0:T(1024)S(1)}, f32[2304]{0:T(1024)}, u32[]{:S(2)}) copy-start(f32[2304]{0:T(1024)} %reshape.297) | copy-start | bytes 27652
  403.9 4.4 %copy-start.20 = (f32[2304]{0:T(1024)S(1)}, f32[2304]{0:T(1024)}, u32[]{:S(2)}) copy-start(f32[2304]{0:T(1024)} %param.44) | copy-start | bytes 27652
  403.9 4.4 %copy-start.21 = (f32[2304]{0:T(1024)S(1)}, f32[2304]{0:T(1024)}, u32[]{:S(2)}) copy-start(f32[2304]{0:T(1024)} %param.43) | copy-start | bytes 27652
  403.9 5.1 %copy-start.4 = (f32[192,3072]{1,0:T(8,128)S(1)}, f32[192,3072]{1,0:T(8,128)}, u32[]{:S(2)}) copy-start(f32[192,3072]{1,0:T(8,128)} %wu.1) | copy-start | bytes 7077892
  403.9 5.1 %copy-start.5 = (f32[192,3072]{1,0:T(8,128)S(1)}, f32[192,3072]{1,0:T(8,128)}, u32[]{:S(2)}) copy-start(f32[192,3072]{1,0:T(8,128)} %param.38) | copy-start | bytes 7077892
  403.9 5.7 %copy-start.6 = (f32[192,3072]{1,0:T(8,128)S(1)}, f32[192,3072]{1,0:T(8,128)}, u32[]{:S(2)}) copy-start(f32[192,3072]{1,0:T(8,128)} %param.37) | copy-start | bytes 7077892
  404.0 5.9 %copy-start.11 = (bf16[192,3072]{1,0:T(8,128)(2,1)S(1)}, bf16[192,3072]{1,0:T(8,128)(2,1)}, u32[]{:S(2)}) copy-start(bf16[192,3072]{1,0:T(8,128)(2,1)} %get-tuple-element.74) | copy-start | bytes 3538948
  409.9 4.2 copy-start.9
  415.5 9.4 %copy-start = (f32[4,208,768]{2,1,0:T(8,128)S(1)}, f32[4,208,768]{2,1,0:T(8,128)}, u32[]{:S(2)}) copy-start(f32[4,208,768]{2,1,0:T(8,128)} %get-tuple-element.71) | copy-start | bytes 7667716

commit v4 on v3

--- a/solution.py
+++ b/solution.py
@@ -81,56 +81,32 @@
     return jnp.concatenate(blocks, axis=0)
 
 
-def attn_fwd_kernel(idx_ref, val_ref, q_ref, k_ref, v_ref, o_ref, lse_ref):
+def attention_step(step, tab_ref, q_ref, k_ref, v_ref, o_ref, lse_ref):
     lane = lax.broadcasted_iota(jnp.int32, (SP, 128), 1)
-
-    def one(step, _):
-        j, b = step // 6, step % 6
-        cols = pl.ds(pl.multiple_of(b * 128, 128), 128)
-        parts = [k_ref[idx_ref[j * NK + t], :, cols] for t in range(NK)]
-        valid = [jnp.where(val_ref[j * NK + t] > 0, 0.0, NEG) for t in range(NK)]
-        vg = jnp.concatenate([v_ref[idx_ref[j * NK + t], :, cols] for t in range(NK)], axis=0)
-        q = q_ref[j, :, cols]
-        scores = []
-        for h in range(2):
-            mine = (lane < 64) if h == 0 else (lane >= 64)
-            spare = 64 if h == 0 else 0
-            ka = augmented_keys(parts, valid, spare, mine)
-            qa = jnp.where(mine, q, jnp.where(lane == spare, jnp.ones_like(q), jnp.zeros_like(q)))
-            scores.append(mm(qa, ka, NT))
-        peaks = [jnp.max(s, axis=1, keepdims=True) for s in scores]
-        probs = [jnp.exp(s - m) for s, m in zip(scores, peaks)]
-        sums = [jnp.sum(p, axis=1, keepdims=True) for p in probs]
-        outs = [mm(p.astype(jnp.bfloat16), vg) / total for p, total in zip(probs, sums)]
-        o_ref[j, :, cols] = jnp.where(lane < 64, outs[0], outs[1]).astype(jnp.bfloat16)
-        logs = [m + jnp.log(total) for m, total in zip(peaks, sums)]
-        lse_ref[j, b] = jnp.transpose(jnp.where(lane == 0, logs[0], logs[1]))[:8]
-        return 0
-
-    lax.fori_loop(0, 24, one, 0)
+    j, b = step // 6, step % 6
+    cols = pl.ds(pl.multiple_of(b * 128, 128), 128)
+    parts = [k_ref[tab_ref[0, j * NK + t], :, cols] for t in range(NK)]
+    valid = [jnp.where(tab_ref[0, (4 + j) * NK + t] > 0, 0.0, NEG) for t in range(NK)]
+    vg = jnp.concatenate([v_ref[tab_ref[0, j * NK + t], :, cols] for t in range(NK)], axis=0)
+    q = q_ref[j, :, cols]
+    scores = []
+    for h in range(2):
+        mine = (lane < 64) if h == 0 else (lane >= 64)
+        spare = 64 if h == 0 else 0
+        ka = augmented_keys(parts, valid, spare, mine)
+        qa = jnp.where(mine, q, jnp.where(lane == spare, jnp.ones_like(q), jnp.zeros_like(q)))
+        scores.append(mm(qa, ka, NT))
+    peaks = [jnp.max(s, axis=1, keepdims=True) for s in scores]
+    probs = [jnp.exp(s - m) for s, m in zip(scores, peaks)]
+    sums = [jnp.sum(p, axis=1, keepdims=True) for p in probs]
+    outs = [mm(p.astype(jnp.bfloat16), vg) / total for p, total in zip(probs, sums)]
+    o_ref[j, :, cols] = jnp.where(lane < 64, outs[0], outs[1]).astype(jnp.bfloat16)
+    logs = [m + jnp.log(total) for m, total in zip(peaks, sums)]
+    lse_ref[j, b] = jnp.transpose(jnp.where(lane == 0, logs[0], logs[1]))[:8]
 
 
 VM = pl.BlockSpec(memory_space=pltpu.VMEM)
 SM = pl.BlockSpec(memory_space=pltpu.SMEM)
-
-
-def attn_fwd(idx, val, q, k, v):
-    return pl.pallas_call(
-        attn_fwd_kernel,
-        out_shape=(
-            jax.ShapeDtypeStruct((4, SP, D), jnp.bfloat16),
-            jax.ShapeDtypeStruct((4, 6, 8, SP), jnp.float32),
-        ),
-        in_specs=[SM, SM, VM, VM, VM],
-        out_specs=(VM, VM),
-        compiler_params=pltpu.CompilerParams(vmem_limit_bytes=60 * 2**20),
-        cost_estimate=pl.CostEstimate(
-            flops=2 * 2 * 24 * 12 * SP * SP * 256,
-            bytes_accessed=14 * 2**20,
-            transcendentals=24 * 12 * SP * SP,
-        ),
-        name="attn_fwd",
-    )(idx, val, q, k, v)
 
 
 def key_tables(item_index, is_valid, q_items):
@@ -189,11 +165,12 @@
 
 
 def front_kernel(
-    tok, tmp, vec, spatial, wq, wo, wu, wd,
-    q_out, k_out, v_out, nt_out, x_out, vec_out, tmp_out, wq_out, wo_out, wu_out, wd_out,
-    t_s, tmp_s, vec_s, n_s, nt_s, q_s, k_s, v_s, x_s, wq_s,
+    tok, cot, tmp, tab, vec, spatial, wq, wo, wu, wd,
+    q_out, k_out, v_out, o_out, lse_out, nt_out, x_out, dy_out, vec_out, tab_out, wq_out, wo_out, wu_out, wd_out,
+    t_s, tmp_s, vec_s, n_s, nt_s, q_s, k_s, v_s, o_s, lse_s, x_s, tab_s, wq_s,
     rq32, ro32, ru32, rd32, rq, ro, ru, rd, sq32, so32, su32, sd32, sq, so, su, sd,
-    t_send, t_recv, m_send, m_recv, v_send, v_recv, w_send, w_recv, reg_sem, own_sem, put_sem, loc_sem, out_sem,
+    t_send, t_recv, m_send, m_recv, d_send, d_recv, v_send, v_recv, w_send, w_recv, z_send, z_recv,
+    reg_sem, own_sem, put_sem, loc_sem, out_sem, nt_sem,
 ):
     bf, f32 = jnp.bfloat16, jnp.float32
     i, f, core, stay, mine, other, far, flip = place()
@@ -205,7 +182,7 @@
     xy = (i // 2) % 4
     xy_x, xy_y = halves(core, flip(xy, 1), flip(xy, 2)), halves(core, flip(xy, 2), flip(xy, 1))
     diag = flip(flip(xy, 1), 2)
-    zs = [flip(f, 1), flip(f, 2), flip(flip(f, 1), 2)]
+    zs = [flip(f, 1), jnp.where(f < 2, 2, 1), jnp.where(f < 2, 3, 0)]
 
     barrier = pltpu.get_barrier_semaphore()
     partners = [c_dev, x_dev, y_dev, m_dev] + [(i, z) for z in zs]
@@ -236,12 +213,15 @@
         own_load(w).start()
     tok_load = pltpu.make_async_copy(tok, t_s.at[mine], loc_sem.at[0])
     tmp_load = pltpu.make_async_copy(tmp, tmp_s.at[mine], loc_sem.at[1])
+    tab_load = pltpu.make_async_copy(tab, tab_out, loc_sem.at[5])
+    cot_load = pltpu.make_async_copy(cot, dy_out, loc_sem.at[6])
     vec_load = pltpu.make_async_copy(vec, vec_s.at[f], loc_sem.at[2])
 
     @pl.when(stay)
     def _():
         tok_load.start()
         tmp_load.start()
+        tab_load.start()
 
     vec_load.start()
     pl.semaphore_wait(barrier, len(partners))
@@ -272,6 +252,12 @@
     def tmp_arrival(kind):
         shard = (mine, 3 - mine, far, 3 - far)[kind]
         return remote(tmp_s.at[shard], tmp_s.at[shard], m_send.at[kind], m_recv.at[kind], c_dev)
+
+    def tab_copy():
+        return remote(tab, tab_out, d_send.at[4], d_recv.at[4], m_dev)
+
+    def cot_copy(j):
+        return remote(cot.at[j], dy_out.at[j], d_send.at[j], d_recv.at[j], m_dev)
 
     def part(w, z, at, half, piece):
         out, r = weights[w][1], weights[w][3]
@@ -287,8 +273,6 @@
     def w_copy(w, d, kind):
         sems = (w_send.at[w, d, kind], w_recv.at[w, d, kind])
         z = zs[d]
-        if kind == Z:
-            return remote(weights[w][3], part(w, f, xy, core, 0), *sems, (i, z))
         at = {X: xy, Y: xy, DA: xy_x, DB: xy_y, C0: xy, C1: xy_x, C2: xy_y, C3: diag}[kind]
         piece = {DA: 1, DB: 2}.get(kind, 0)
         dev = {X: x_dev, Y: y_dev, DA: y_dev, DB: x_dev}.get(kind, c_dev)
@@ -298,21 +282,28 @@
     def w_arrival(w, d, kind):
         sems = (w_send.at[w, d, kind], w_recv.at[w, d, kind])
         z = zs[d]
-        at = {Z: xy, X: xy_x, Y: xy_y, DA: diag, DB: diag, C0: xy, C1: xy_y, C2: xy_x, C3: diag}[kind]
+        at = {X: xy_x, Y: xy_y, DA: diag, DB: diag, C0: xy, C1: xy_y, C2: xy_x, C3: diag}[kind]
         piece = {DA: 1, DB: 2}.get(kind, 0)
         half = (1 - core) if kind >= C0 else core
         ref = part(w, z, at, half, piece)
         return remote(ref, ref, *sems, c_dev)
 
+    def z_copy(w, d):
+        return remote(weights[w][3], part(w, f, xy, core, 0), z_send.at[w, d], z_recv.at[w, f], (i, zs[d]))
+
+    def z_arrival(w, d):
+        ref = part(w, zs[d], xy, core, 0)
+        return remote(ref, ref, z_send.at[w, d], z_recv.at[w, zs[d]], (i, zs[d]))
+
     def w_send_region(w):
         region_load(w).wait()
         weights[w][3][...] = weights[w][2][...].astype(bf)
         for d in range(3):
-            w_copy(w, d, Z).start()
+            z_copy(w, d).start()
 
     def w_stage_one(w):
         for d in range(3):
-            w_arrival(w, d, Z).wait_recv()
+            z_arrival(w, d).wait_recv()
             for kind in (X, Y, C0):
                 w_copy(w, d, kind).start()
 
@@ -342,12 +333,21 @@
         own_put(w).start()
 
     w_send_region(0)
+    vec_load.wait()
+
+    def v_copy(d):
+        return remote(vec_s.at[f], vec_s.at[f], v_send.at[d], v_recv.at[f], (i, zs[d]))
+
+    def v_arrival(d):
+        return remote(vec_s.at[zs[d]], vec_s.at[zs[d]], v_send.at[d], v_recv.at[zs[d]], (i, zs[d]))
+
+    for d in range(3):
+        v_copy(d).start()
 
     @pl.when(jnp.logical_not(stay))
     def _():
         tmp_copy(0).start()
-        for j in range(4):
-            tok_copy(0, j).start()
+        tab_copy().start()
 
     @pl.when(stay)
     def _():
@@ -355,34 +355,26 @@
         tmp_load.wait()
         for kind in (2, 1):
             tmp_copy(kind).start()
-            for j in range(4):
-                tok_copy(kind, j).start()
-
-    vec_load.wait()
-    def v_copy(d):
-        return remote(vec_s.at[f], vec_s.at[f], v_send.at[d], v_recv.at[d], (i, zs[d]))
-    def v_arrival(d):
-        return remote(vec_s.at[zs[d]], vec_s.at[zs[d]], v_send.at[d], v_recv.at[d], (i, zs[d]))
-    for d in range(3):
-        v_copy(d).start()
-    for w in range(4):
+        for j in range(4):
+            tok_copy(1, j).start()
+
+    w_own(0)
+    w_stage_one(0)
+
+    @pl.when(jnp.logical_not(stay))
+    def _():
+        for j in range(4):
+            tok_copy(0, j).start()
+
+    @pl.when(stay)
+    def _():
+        for j in range(4):
+            tok_copy(2, j).start()
+
+    for w in (1, 2, 3):
         w_own(w)
-    w_stage_one(0)
     w_stage_two(0)
     w_stage_three(0)
-
-    @pl.when(jnp.logical_not(stay))
-    def _():
-        tmp_arrival(0).wait_recv()
-        for kind in (2, 1):
-            tmp_copy(kind).start()
-        for j in range(4):
-            tok_arrival(0, j).wait_recv()
-            for kind in (2, 1):
-                tok_copy(kind, j).start()
-
-    for w in (1, 2, 3):
-        w_send_region(w)
     w_stage_four(0)
     own_put(0).wait()
     wq_load = pltpu.make_async_copy(wq_out, wq_s, loc_sem.at[3])
@@ -391,35 +383,36 @@
         v_arrival(d).wait_recv()
     vec_put = pltpu.make_async_copy(vec_s, vec_out, loc_sem.at[4])
     vec_put.start()
-    tmp_put = pltpu.make_async_copy(tmp_s.at[mine], tmp_out, loc_sem.at[5])
-    tmp_put.start()
     gain = vec_s[0, 0:1, :].astype(f32)
     shift = vec_s[0, 1:2, :].astype(f32)
     bias_q = vec_s[0, 2:3, :].astype(f32)
     bias_v = vec_s[1, 0:1, :].astype(f32)
     wq_load.wait()
 
-    def normalise(shard, keep_x):
+    def normalise(shard):
         def slot(j, _):
             x = t_s[shard, j].astype(f32) + (spatial[...] + tmp_s[shard, pl.ds(j, 1), :])
-            if keep_x:
+
+            @pl.when(shard == mine)
+            def _():
                 x_s[j] = x
-            n_s[shard, j] = (norm_rows(x) * gain + shift).astype(bf)
+            n_s[j] = (norm_rows(x) * gain + shift).astype(bf)
             return 0
         lax.fori_loop(0, 4, slot, 0)
 
     def project(shard):
-        rows = n_s[shard].reshape(4 * SP, D)
+        rows = n_s[...].reshape(4 * SP, D)
+        at = pl.ds(4 * shard, 4)
         def keys(t, _):
             cols = pl.ds(pl.multiple_of(t * 256, 256), 256)
-            k_s[shard, :, :, cols] = mm(rows, wq_s[:, pl.ds(pl.multiple_of(D + t * 256, 256), 256)]).astype(bf).reshape(4, SP, 256)
-            v_s[shard, :, :, cols] = (mm(rows, wq_s[:, pl.ds(pl.multiple_of(2 * D + t * 256, 256), 256)])
+            k_s[at, :, cols] = mm(rows, wq_s[:, pl.ds(pl.multiple_of(D + t * 256, 256), 256)]).astype(bf).reshape(4, SP, 256)
+            v_s[at, :, cols] = (mm(rows, wq_s[:, pl.ds(pl.multiple_of(2 * D + t * 256, 256), 256)])
                                       + vec_s[1, 0:1, cols].astype(f32)).astype(bf).reshape(4, SP, 256)
             return 0
         lax.fori_loop(0, 3, keys, 0)
 
     def project_q(shard):
-        rows = n_s[shard].reshape(4 * SP, D)
+        rows = n_s[...].reshape(4 * SP, D)
         def queries(t, _):
             cols = pl.ds(pl.multiple_of(t * 256, 256), 256)
             q = (mm(rows, wq_s[:, cols]) + vec_s[0, 2:3, cols].astype(f32)).astype(bf)
@@ -433,46 +426,124 @@
         copy.start()
         outs.append(copy)
 
+    turned = []
+
     def put_shard(shard):
-        nt_s[shard] = jnp.transpose(n_s[shard].reshape(4 * SP, D))
-        put(nt_s.at[shard], nt_out.at[shard])
-        put(k_s.at[shard], k_out.at[shard])
-        put(v_s.at[shard], v_out.at[shard])
-
-    normalise(mine, True)
+        n = len(turned)
+        if n >= 2:
+            turned[n - 2].wait()
+        nt_s[n % 2] = jnp.transpose(n_s[...].reshape(4 * SP, D))
+        copy = pltpu.make_async_copy(nt_s.at[n % 2], nt_out.at[shard], nt_sem.at[n % 2])
+        copy.start()
+        turned.append(copy)
+        at = pl.ds(4 * shard, 4)
+        put(k_s.at[at], k_out.at[at])
+        put(v_s.at[at], v_out.at[at])
+
+    moved = jnp.logical_not(stay)
+
+    def arrive(kind):
+        tmp_arrival(kind).wait_recv()
+        if kind == 2:
+            tmp_copy(3).start()
+        if kind == 0:
+            for then in (2, 1):
+                tmp_copy(then).start()
+        for j in range(4):
+            tok_arrival(kind, j).wait_recv()
+            if kind == 2:
+                tok_copy(3, j).start()
+            if kind == 0:
+                for then in (2, 1):
+                    tok_copy(then, j).start()
+
+    def work(shard):
+        normalise(shard)
+
+        @pl.when(shard == mine)
+        def _():
+            project_q(shard)
+
+        project(shard)
+        put_shard(shard)
+
+    stayed_here, stayed_there = jnp.where(stay, mine, 3 - mine), jnp.where(stay, far, 3 - far)
+
+    @pl.when(moved)
+    def _():
+        arrive(1)
+
+    work(stayed_here)
+
+    @pl.when(moved)
+    def _():
+        arrive(0)
+
+    @pl.when(stay)
+    def _():
+        arrive(1)
+
+    for w in (1, 2, 3):
+        w_send_region(w)
+    work(3 - stayed_here)
     put(x_s, x_out)
-    project_q(mine)
     put(q_s, q_out)
-    project(mine)
-    put_shard(mine)
-    w_stage_one(1)
-    tmp_arrival(1).wait_recv()
-    for j in range(4):
-        tok_arrival(1, j).wait_recv()
-    normalise(3 - mine, False)
-    project(3 - mine)
-    put_shard(3 - mine)
-    tmp_arrival(2).wait_recv()
-    tmp_copy(3).start()
-    for j in range(4):
-        tok_arrival(2, j).wait_recv()
-        tok_copy(3, j).start()
-    w_stage_two(1)
-    w_stage_one(2)
-    normalise(far, False)
-    project(far)
-    put_shard(far)
-    w_stage_one(3)
-    tmp_arrival(3).wait_recv()
-    for j in range(4):
-        tok_arrival(3, j).wait_recv()
-    normalise(3 - far, False)
-    project(3 - far)
-    put_shard(3 - far)
-    w_stage_two(2)
-    w_stage_two(3)
-    for w in (1, 2, 3):
-        w_stage_three(w)
+
+    @pl.when(stay)
+    def _():
+        arrive(2)
+
+    @pl.when(moved)
+    def _():
+        arrive(3)
+
+    work(stayed_there)
+
+    @pl.when(moved)
+    def _():
+        arrive(2)
+
+    @pl.when(stay)
+    def _():
+        arrive(3)
+
+    @pl.when(moved)
+    def _():
+        for j in range(4):
+            cot_copy(j).start()
+
+    @pl.when(stay)
+    def _():
+        cot_load.start()
+
+    work(3 - stayed_there)
+
+    @pl.when(stay)
+    def _():
+        tab_load.wait()
+
+    @pl.when(jnp.logical_not(stay))
+    def _():
+        tab_copy().wait_recv()
+
+    to_scalars = pltpu.make_async_copy(tab_out, tab_s, loc_sem.at[7])
+    to_scalars.start()
+    to_scalars.wait()
+    plan = ((0, w_stage_one, 1), (3, w_stage_one, 2), (5, w_stage_two, 1), (8, w_stage_one, 3), (14, w_stage_two, 2), (16, w_stage_three, 1), (22, w_stage_two, 3))
+
+    def attend(step, _):
+        for at, act, w in plan:
+            @pl.when(step == at)
+            def _():
+                act(w)
+        attention_step(step, tab_s, q_s, k_s, v_s, o_s, lse_s)
+        return 0
+
+    lax.fori_loop(0, 24, attend, 0)
+    put(o_s, o_out)
+    put(lse_s, lse_out)
+    for act, w in ((w_stage_three, 2), (w_stage_three, 3)):
+        act(w)
     for w in (1, 2, 3):
         w_stage_four(w)
         own_put(w).wait()
@@ -480,8 +551,14 @@
     @pl.when(jnp.logical_not(stay))
     def _():
         tmp_copy(0).wait_send()
+        tab_copy().wait_send()
         for j in range(4):
             tok_copy(0, j).wait_send()
+            cot_copy(j).wait()
+
+    @pl.when(stay)
+    def _():
+        cot_load.wait()
 
     for kind in (1, 2, 3):
         tmp_copy(kind).wait_send()
@@ -490,43 +567,48 @@
     for d in range(3):
         v_copy(d).wait_send()
         for w in range(4):
-            for kind in range(9):
+            z_copy(w, d).wait_send()
+            for kind in range(X, C3 + 1):
                 w_copy(w, d, kind).wait_send()
+    for copy in turned[2:]:
+        copy.wait()
     vec_put.wait()
-    tmp_put.wait()
     for copy in outs:
         copy.wait()
 
 
-def front(tok, tmp, vec, spatial, wq, wo, wu, wd):
+def front(tok, cot, tmp, tab, vec, spatial, wq, wo, wu, wd):
     bf, f32 = jnp.bfloat16, jnp.float32
     S = jax.ShapeDtypeStruct
     hb = pl.BlockSpec(memory_space=pltpu.HBM)
     regs = [(w.shape[0] // 4, w.shape[1] // 2) for w in (wq, wo, wu, wd)]
     full = [(4 * w.shape[0], w.shape[1]) for w in (wq, wo, wu, wd)]
     dma = pltpu.SemaphoreType.DMA
+    v = lambda shape, dtype=bf: pltpu.VMEM(shape, dtype)
+    rows, every, stats = (4, SP, D), (16, SP, D), (4, 6, 8, SP)
     return pl.pallas_call(
         front_kernel,
         out_shape=(
-            S((4, SP, D), bf), S((4, 4, SP, D), bf), S((4, 4, SP, D), bf), S((4, D, 4 * SP), bf), S((4, SP, D), f32),
-            S((4, VEC_ROWS, D), bf), S((8, D), f32),
+            S(rows, bf), S(every, bf), S(every, bf), S(rows, bf), S(stats, f32), S((4, D, 4 * SP), bf), S(rows, f32),
+            S(rows, bf), S((4, VEC_ROWS, D), bf), S(tab.shape, jnp.int32),
         ) + tuple(S(s, bf) for s in full),
-        in_specs=[hb, hb, hb, VM, hb, hb, hb, hb],
-        out_specs=(hb,) * 11,
+        in_specs=[hb] * 5 + [VM] + [hb] * 4,
+        out_specs=(hb,) * 14,
         scratch_shapes=[
-            pltpu.VMEM((4, 4, SP, D), bf), pltpu.VMEM((4, 8, D), f32), pltpu.VMEM((4, VEC_ROWS, D), bf),
-            pltpu.VMEM((4, 4, SP, D), bf), pltpu.VMEM((4, D, 4 * SP), bf), pltpu.VMEM((4, SP, D), bf), pltpu.VMEM((4, 4, SP, D), bf),
-            pltpu.VMEM((4, 4, SP, D), bf), pltpu.VMEM((4, SP, D), f32), pltpu.VMEM(full[0], bf),
+            v((4,) + rows), v((4, 8, D), f32), v((4, VEC_ROWS, D)), v(rows), v((2, D, 4 * SP)), v(rows), v(every), v(every),
+            v(rows), v(stats, f32), v(rows, f32), pltpu.SMEM(tab.shape, jnp.int32), v(full[0]),
         ]
-        + [pltpu.VMEM(r, f32) for r in regs] + [pltpu.VMEM(r, bf) for r in regs]
-        + [pltpu.VMEM(w.shape, f32) for w in (wq, wo, wu, wd)] + [pltpu.VMEM(w.shape, bf) for w in (wq, wo, wu, wd)]
-        + [dma((4, 4)), dma((4, 4)), dma((4,)), dma((4,)), dma((3,)), dma((3,)), dma((4, 3, 9)), dma((4, 3, 9)),
-           dma((4,)), dma((4,)), dma((4,)), dma((6,)), dma((16,))],
+        + [v(r, f32) for r in regs] + [v(r) for r in regs]
+        + [v(w.shape, f32) for w in (wq, wo, wu, wd)] + [v(w.shape) for w in (wq, wo, wu, wd)]
+        + [dma((4, 4)), dma((4, 4)), dma((4,)), dma((4,)), dma((5,)), dma((5,)), dma((3,)), dma((4,)), dma((4, 3, 9)),
+           dma((4, 3, 9)), dma((4, 3)), dma((4, 4)), dma((4,)), dma((4,)), dma((4,)), dma((8,)), dma((16,)),
+           dma((2,))],
         compiler_params=pltpu.CompilerParams(
             collective_id=1, has_side_effects=True, vmem_limit_bytes=62 * 2**20),
-        cost_estimate=pl.CostEstimate(flops=2 * 9 * 784 * 768 * 768, bytes_accessed=40 * 2**20, transcendentals=0),
+        cost_estimate=pl.CostEstimate(
+            flops=2 * 9 * 784 * 768 * 768, bytes_accessed=40 * 2**20, transcendentals=24 * 12 * SP * SP),
         name="front",
-    )(tok, tmp, vec, spatial, wq, wo, wu, wd)
+    )(tok, cot, tmp, tab, vec, spatial, wq, wo, wu, wd)
 
 
 def norm_parts(x):
@@ -884,7 +966,7 @@
 
 
 def back_kernel(
-    n_items, idx_ref, val_ref, src_ref, q_in, k_in, v_in, o_in, do_in, lse_in, nt_in, wq_in, gd, gu, go,
+    n_items, tab_ref, q_in, k_in, v_in, o_in, do_in, lse_in, nt_in, wq_in, gd, gu, go,
     dq_out, part_out, gq_out, bias_out, gd_out, gu_out, go_out,
     q_s, k_s, v_s, o_s, do_s, lse_s, nt_s, wq_s, pk_s, pv_s, gq_s, bias_s, load_sem, out_sem, *rest,
 ):
@@ -911,10 +993,10 @@
                 net.step(w, stage)
         j, b = step // 6, step % 6
         cols = pl.ds(pl.multiple_of(b * 128, 128), 128)
-        parts = [k_s[idx_ref[j * NK + t], :, cols] for t in range(NK)]
-        valid = [jnp.where(val_ref[j * NK + t] > 0, 0.0, NEG) for t in range(NK)]
+        parts = [k_s[tab_ref[0, j * NK + t], :, cols] for t in range(NK)]
+        valid = [jnp.where(tab_ref[0, (4 + j) * NK + t] > 0, 0.0, NEG) for t in range(NK)]
         kg = jnp.concatenate(parts, axis=0)
-        vg = jnp.concatenate([v_s[idx_ref[j * NK + t], :, cols] for t in range(NK)], axis=0)
+        vg = jnp.concatenate([v_s[tab_ref[0, j * NK + t], :, cols] for t in range(NK)], axis=0)
         kg_t = jnp.transpose(kg)
         q, do, o = q_s[j, :, cols], do_s[j, :, cols], o_s[j, :, cols]
         prod_t = jnp.transpose(do.astype(f32) * o.astype(f32))
@@ -956,9 +1038,9 @@
     net.step(2, 2)
 
     def combine(slot, _):
-        first, second = src_ref[slot], src_ref[16 + slot]
-        keep_a = jnp.logical_and(row < FRAME_TOK, src_ref[32 + slot] > 0)
-        keep_b = jnp.logical_and(row < FRAME_TOK, src_ref[48 + slot] > 0)
+        first, second = tab_ref[0, 8 * NK + slot], tab_ref[0, 8 * NK + 16 + slot]
+        keep_a = jnp.logical_and(row < FRAME_TOK, tab_ref[0, 8 * NK + 32 + slot] > 0)
+        keep_b = jnp.logical_and(row < FRAME_TOK, tab_ref[0, 8 * NK + 48 + slot] > 0)
         for out, part in ((k_s, pk_s), (v_s, pv_s)):
             total = jnp.where(keep_a, part[first].astype(f32), 0.0) + jnp.where(keep_b, part[second].astype(f32), 0.0)
             out[slot] = total.astype(bf)
@@ -1036,7 +1118,7 @@
         copy.wait()
 
 
-def back(n_items, idx, val, src, q, k, v_, o, do, lse, nt, wq, gd, gu, go):
+def back(n_items, tab, q, k, v_, o, do, lse, nt, wq, gd, gu, go):
     bf, f32 = jnp.bfloat16, jnp.float32
     S = jax.ShapeDtypeStruct
     hb = pl.BlockSpec(memory_space=pltpu.HBM)
@@ -1048,7 +1130,7 @@
         functools.partial(back_kernel, n_items),
         out_shape=(S(rows, bf), S((16, SP, D), bf), S((4, 4, D // 16, 3 * D), bf), S((8, D), f32))
         + tuple(S((4 * g.shape[2], g.shape[3]), bf) for g in (gd, gu, go)),
-        in_specs=[SM, SM, SM] + [hb] * 11,
+        in_specs=[SM] + [hb] * 11,
         out_specs=(hb,) * 7,
         scratch_shapes=[
             v(rows), v((16, SP, D)), v((16, SP, D)), v(rows), v(rows), v((4, 6, 8, SP), f32), v((4, D, 4 * SP)),
@@ -1059,7 +1141,7 @@
         cost_estimate=pl.CostEstimate(
             flops=2 * 5 * 24 * 12 * SP * SP * 256, bytes_accessed=60 * 2**20, transcendentals=24 * 12 * SP * SP),
         name="back",
-    )(idx, val, src, q, k, v_, o, do, lse, nt, wq, gd, gu, go)
+    )(tab, q, k, v_, o, do, lse, nt, wq, gd, gu, go)
 
 
 def tail_kernel(
@@ -1230,21 +1312,19 @@
     pad = lambda a: jnp.pad(a[0], ((0, 0), (0, SP - FRAME_TOK), (0, 0)))
     item_index, is_valid = slot_items(item_dates[0], slot_frame[0], frame_mask[0])
     own_items = lax.dynamic_slice_in_dim(item_index, f * 4, 4)
-    tables = key_tables(item_index, is_valid, own_items).astype(f32)
-    tmp = jnp.concatenate([temporal_rows(date_year[0], date_day[0]), jnp.pad(tables[None], ((0, 3), (0, D - tables.shape[0])))])
+    tables = key_tables(item_index, is_valid, own_items)
+    tab = jnp.pad(tables[None], ((0, 7), (0, 128 - tables.shape[0])))
+    tmp = jnp.pad(temporal_rows(date_year[0], date_day[0]), ((0, 4), (0, 0)))
     vec = jnp.pad(vectors.astype(bf).reshape(3, D), ((0, VEC_ROWS - 3), (0, 0)))
-    q3, k4, v4, nt, x3, vec_all, tmp_own, wq, wo, wu, wd = front(
-        pad(tokens), tmp, vec, jnp.asarray(spatial_rows()), qkv_weight, out_weight, up_weight, down_weight)
-    tables = tmp_own[4, : 8 * NK + 64].astype(jnp.int32)
-    idx, val, src = tables[: 4 * NK], tables[4 * NK : 8 * NK], tables[8 * NK :]
-    k3, v3 = k4.reshape(16, SP, D), v4.reshape(16, SP, D)
-    o3, lse = attn_fwd(idx, val, q3, k3, v3)
+    q3, k3, v3, o3, lse, nt, x3, dy, vec_all, tab_own, wq, wo, wu, wd = front(
+        pad(tokens), pad(cotangent), tmp, tab, vec, jnp.asarray(spatial_rows()),
+        qkv_weight, out_weight, up_weight, down_weight)
     block_out, hidden_grad, do3, down_grad, up_grad, out_grad, vector_part = mid(
-        o3, x3, to_worker(pad(cotangent)), vec_all, wo, wu, wd)
+        o3, x3, dy, vec_all, wo, wu, wd)
     block_out = to_worker(block_out)
     blocks = lambda g: g.reshape(4, 4, g.shape[0] // 16, g.shape[1])
     dq3, part, gq, bias_part, down_sum, up_sum, out_sum = back(
-        n_items, idx, val, src, q3, k3, v3, o3, do3, lse, nt, wq, blocks(down_grad), blocks(up_grad), blocks(out_grad))
+        n_items, tab_own, q3, k3, v3, o3, do3, lse, nt, wq, blocks(down_grad), blocks(up_grad), blocks(out_grad))
     token_grad, vector_sum, qkv_sum = tail(
         n_items, gq, part.reshape(4, 4, SP, D), dq3, x3, hidden_grad, wq, vec_all, vector_part, bias_part)
     token_grad = jnp.where(

time: 433 us -> 388 us (0.90)
  Pallas kernels: 371 us -> 324 us
    pallas_call x2 -> x1, Pallas kernels: 163 us -> 113 us  [front(): pl.pallas_call(front_kernel, out_shape=(S(rows, bf), S(every, bf), S(ever...]
  transfers between devices with their start and end apart: 3 -> 2, of which waited for: 1 -> 1; matrix products, arithmetic and copies ran while one was open for 7% -> 6% of each run, Pallas kernels for 75% -> 43%
where the time goes in v4:
time: 388 us; the launch traced here: 381 us
  Pallas kernels  324 us (84%)
  other arithmetic  26.6 us (7%)
  local copies, waits for them, and re-layouts  13.7 us (4%)
  waiting for transfers between devices  7.65 us (2%)
  starting transfers between devices  6.84 us (2%)
    pallas_call x1, Pallas kernels, front(): pl.pallas_call(front_kernel, out_shape=(S(rows, bf), S(every, bf), S(ever...  113 us
    pallas_call x1, Pallas kernels, back(): pl.pallas_call(functools.partial(back_kernel, n_items), out_shape=(S(rows...  108 us
    pallas_call x1, Pallas kernels, tail(): pl.pallas_call(functools.partial(tail_kernel, n_items), out_shape=(S(rows...  54.8 us
    pallas_call x1, Pallas kernels, mid(): pl.pallas_call(mid_kernel, out_shape=(S(rows, bf), S(rows, f32), S(rows,...  48 us
    sub x5, other arithmetic, adamw(): weight - step_rate * (first_hat / (jnp.sqrt(second_hat) + 1e-08) + decay...  15.8 us
  transfers between devices with their start and end apart: 2, of which 1 were waited for; matrix products, arithmetic and copies ran while one was open for 6% of the time, Pallas kernels for 43%

profile of v4, /device:TPU:13, one launch (start us, length us, event | category | flops | bytes accessed | tf_op | source)
XLA Modules:
  0.0 380.7 jit_solution(9791942826395634293)
XLA Ops:
  0.7 0.9 reduce-window.4
  1.6 0.7 fusion.13
  2.3 0.7 compare_reduce_fusion
  3.0 0.7 convert_reduce_fusion
  3.7 0.7 fusion.12
  4.4 0.1 dynamic_slice.3
  4.5 0.2 convert_reduce_fusion.1
  4.7 0.2 reduce_window_sum.18
  4.9 0.2 select_reduce_fusion
  5.0 0.1 copy.46
  5.1 0.1 reshape.194
  5.3 0.1 reshape.203
  5.4 0.1 select_reduce_fusion.1
  5.5 1.4 copy.52
  7.0 0.1 copy.51
  7.1 1.1 pad.23.tok
  8.3 1.1 pad.24.cot
  9.4 0.1 concatenate.7
  9.5 0.6 pad.27.tab
  10.1 0.6 pad.28.vec
  10.7 0.1 multiply_sine_fusion.1
  10.9 0.1 select_maximum_fusion
  10.9 0.6 pad.26.tmp
  11.5 113.1 %front.1 = (bf16[4,208,768]{2,1,0:T(8,128)(2,1)}, bf16[16,208,768]{2,1,0:T(8,128)(2,1)}, bf16[16,208,768]{2,1,0:T(8,128)(2,1)}, bf16[4,208,768]{2,1,0:T(8,128)(2...) custom-call(bf16[4,208,768]{2,1,0:T(8,128)(2,1)} %pad.23.tok, ...), custom_call_target="tpu_custom_call" | custom-call | flops 8323596288 | bytes 41943040 | tf_op jit(solution)/shard_map/front/pallas_call | solution.py:589
  124.6 48.0 %mid.1 = (bf16[4,208,768]{2,1,0:T(8,128)(2,1)}, f32[4,208,768]{2,1,0:T(8,128)}, bf16[4,208,768]{2,1,0:T(8,128)(2,1)}, bf16[3072,768]{1,0:T(8,128)(2,1)}, bf16[76...) custom-call(bf16[4,208,768]{2,1,0:T(8,128)(2,1)} %get-tuple-element.48.o_in, ...), custom_call_target="tpu_custom_call" | custom-call | flops 26499612672 | bytes 41943040 | tf_op jit(solution)/shard_map/mid/pallas_call | solution.py:754
  172.7 4.3 %collective-permute-start = (bf16[4,208,768]{2,1,0:T(8,128)(2,1)}, bf16[4,208,768]{2,1,0:T(8,128)(2,1)}, u32[]{:S(2)}, u32[]{:S(2)}) collective-permute-start(bf16[4,208,768]{2,1,0:T(8,128)(2,1)} %get-tuple-element.55), channel_id=1, source_target_pairs={{2,5},{3,4},{4,3},{5,2},{10,13},{11,12},{12,11},{13,10},{18,21},{1... | collective-permute-start | bytes 3833864 | tf_op jit(solution)/shard_map/ppermute | solution.py:1310
  177.0 108.5 %back.1 = (bf16[4,208,768]{2,1,0:T(8,128)(2,1)}, bf16[16,208,768]{2,1,0:T(8,128)(2,1)}, bf16[4,4,48,2304]{3,2,1,0:T(8,128)(2,1)}, f32[8,768]{1,0:T(8,128)}, bf16...) custom-call(s32[8,128]{1,0:T(8,128)} %get-tuple-element.56.tab_ref, ...), custom_call_target="tpu_custom_call" | custom-call | flops 31897681920 | bytes 62914560 | tf_op jit(solution)/shard_map/back/pallas_call | solution.py:1129
  285.5 54.8 %tail.1 = (f32[4,208,768]{2,1,0:T(8,128)}, f32[8,768]{1,0:T(8,128)}, bf16[192,2304]{1,0:T(8,128)(2,1)}) custom-call(bf16[4,4,48,2304]{3,2,1,0:T(8,128)(2,1)} %get-tuple-element.67.gq, bf16[4,4,208,768]{3,2,1,0:T(8,128)(2,1)} %bitcast.40, bf16[4,208,768]{2,1,0:T(8,128)(2,1)} %get-tuple-element.69.dq, f32[4,208,768]{2,1,0:T(8,128)} %get-tuple-element.49.x_in, ...), custom_call_target="tpu_custom_call" | custom-call | flops 12947816448 | bytes 62914560 | tf_op jit(solution)/shard_map/tail/pallas_call | solution.py:1259
  340.3 3.1 convert_element_type.90
  343.5 2.5 collective-permute-start.1
  346.0 0.7 slice.11
  346.8 0.6 reshape.202
  347.4 5.1 %multiply_subtract_fusion.2 = (f32[192,2304]{1,0:T(8,128)}, f32[192,2304]{1,0:T(8,128)}, f32[192,2304]{1,0:T(8,128)}) fusion(f32[192,2304]{1,0:T(8,128)S(1)} %copy-done.7, bf16[192,2304]{1,0:T(8,128)(2,1)} %get-tuple-element.74, f32[192,2304]{1,0:T(8,128)S(1)} %copy-done.8, f32[192,2304]{1,0:T(8,128)} %param.31), kind=kLoop, calls=%fused_computation.15 | loop fusion | flops 7077888 | bytes 11501568 | tf_op jit(solution)/shard_map/sub | solution.py:135
  352.6 1.5 multiply_subtract_fusion.3
  354.1 0.8 copy-done.1
  354.9 0.3 copy-done.12
  355.2 4.4 %multiply_subtract_fusion = (f32[768,768]{1,0:T(8,128)}, f32[768,768]{1,0:T(8,128)}, f32[768,768]{1,0:T(8,128)}) fusion(f32[768,768]{1,0:T(8,128)S(1)} %copy-done.1, bf16[768,768]{1,0:T(8,128)(2,1)S(1)} %copy-done.12, f32[768,768]{1,0:T(8,128)S(1)} %copy-done.2, f32[768,768]{1,0:T(8,128)S(1)} %copy-done.3), kind=kLoop, calls=%fused_computation.10 | loop fusion | flops 9437184 | bytes 15335424 | tf_op jit(solution)/shard_map/sub | solution.py:135
  359.6 0.6 multiply_subtract_fusion.4
  360.3 0.6 copy-done.6
  360.9 0.3 copy-done.11
  361.2 4.2 %multiply_subtract_fusion.1 = (f32[192,3072]{1,0:T(8,128)}, f32[192,3072]{1,0:T(8,128)}, f32[192,3072]{1,0:T(8,128)}) fusion(f32[192,3072]{1,0:T(8,128)S(1)} %copy-done.4, bf16[192,3072]{1,0:T(8,128)(2,1)S(1)} %copy-done.11, f32[192,3072]{1,0:T(8,128)S(1)} %copy-done.5, f32[192,3072]{1,0:T(8,128)S(1)} %copy-done.6), kind=kLoop, calls=%fused_computation.11 | loop fusion | flops 9437184 | bytes 15335424 | tf_op jit(solution)/shard_map/sub | solution.py:135
  365.4 1.4 select_bitcast_fusion.1
  366.8 0.1 slice.12
  366.9 1.5 copy.47
  368.4 7.7 %collective-permute-done.1 = bf16[4,208,768]{2,1,0:T(8,128)(2,1)} collective-permute-done((bf16[4,208,768]{2,1,0:T(8,128)(2,1)}, bf16[4,208,768]{2,1,0:T(8,128)(2,1)}, u32[]{:S(2)}, u32[]{:S(2)}) %collective-permute-start.1) | collective-permute-done | bytes 1277984 | tf_op jit(solution)/shard_map/ppermute | solution.py:1331
  376.0 1.6 select_bitcast_fusion
  377.6 0.2 slice.13
  377.9 2.4 copy.48
  (55 shorter events, 0.2 us)
Async XLA Ops:
  0.7 6.3 %copy-start.10 = (bf16[1,4,196,768]{3,1,2,0:T(4,128)(2,1)S(1)}, bf16[1,4,196,768]{3,1,2,0:T(4,128)(2,1)}, u32[]{:S(2)}) copy-start(bf16[1,4,196,768]{3,1,2,0:T(4,128)(2,1)} %param.24) | copy-start | bytes 3612676
  7.1 3.0 copy-start.17
  7.1 3.6 copy-start.22
  7.1 3.6 copy-start.23
  172.7 192.7 %collective-permute-start = (bf16[4,208,768]{2,1,0:T(8,128)(2,1)}, bf16[4,208,768]{2,1,0:T(8,128)(2,1)}, u32[]{:S(2)}, u32[]{:S(2)}) collective-permute-start(bf16[4,208,768]{2,1,0:T(8,128)(2,1)} %get-tuple-element.55), channel_id=1, source_target_pairs={{2,5},{3,4},{4,3},{5,2},{10,13},{11,12},{12,11},{13,10},{18,21},{1... | collective-permute-start | bytes 3833864 | tf_op jit(solution)/shard_map/ppermute | solution.py:1310
  340.3 7.1 %copy-start.7 = (f32[192,2304]{1,0:T(8,128)S(1)}, f32[192,2304]{1,0:T(8,128)}, u32[]{:S(2)}) copy-start(f32[192,2304]{1,0:T(8,128)} %wq.1) | copy-start | bytes 5308420
  340.3 7.1 %copy-start.8 = (f32[192,2304]{1,0:T(8,128)S(1)}, f32[192,2304]{1,0:T(8,128)}, u32[]{:S(2)}) copy-start(f32[192,2304]{1,0:T(8,128)} %param.32) | copy-start | bytes 5308420
  343.5 32.6 %collective-permute-start.1 = (bf16[4,208,768]{2,1,0:T(8,128)(2,1)}, bf16[4,208,768]{2,1,0:T(8,128)(2,1)}, u32[]{:S(2)}, u32[]{:S(2)}) collective-permute-start(bf16[4,208,768]{2,1,0:T(8,128)(2,1)} %convert_element_type.90), channel_id=1, source_target_pairs={{2,5},{3,4},{4,3},{5,2},{10,13},{11,12},{12,11},{13,10},{18,21},{1... | collective-permute-start | bytes 3833864 | tf_op jit(solution)/shard_map/ppermute | solution.py:1331
  347.4 5.2 %copy-start.13 = (f32[192,768]{1,0:T(8,128)S(1)}, f32[192,768]{1,0:T(8,128)}, u32[]{:S(2)}) copy-start(f32[192,768]{1,0:T(8,128)} %wo.1) | copy-start | bytes 1769476
  347.4 5.2 %copy-start.14 = (f32[192,768]{1,0:T(8,128)S(1)}, f32[192,768]{1,0:T(8,128)}, u32[]{:S(2)}) copy-start(f32[192,768]{1,0:T(8,128)} %param.35) | copy-start | bytes 1769476
  347.4 5.2 %copy-start.15 = (f32[192,768]{1,0:T(8,128)S(1)}, f32[192,768]{1,0:T(8,128)}, u32[]{:S(2)}) copy-start(f32[192,768]{1,0:T(8,128)} %param.34) | copy-start | bytes 1769476
  347.4 5.2 %copy-start.16 = (bf16[192,768]{1,0:T(8,128)(2,1)S(1)}, bf16[192,768]{1,0:T(8,128)(2,1)}, u32[]{:S(2)}) copy-start(bf16[192,768]{1,0:T(8,128)(2,1)} %get-tuple-element.75) | copy-start | bytes 884740
  347.4 6.7 %copy-start.2 = (f32[768,768]{1,0:T(8,128)S(1)}, f32[768,768]{1,0:T(8,128)}, u32[]{:S(2)}) copy-start(f32[768,768]{1,0:T(8,128)} %param.41) | copy-start | bytes 7077892
  347.4 6.7 %copy-start.3 = (f32[768,768]{1,0:T(8,128)S(1)}, f32[768,768]{1,0:T(8,128)}, u32[]{:S(2)}) copy-start(f32[768,768]{1,0:T(8,128)} %param.40) | copy-start | bytes 7077892
  352.6 2.3 copy-start.1
  352.6 2.6 copy-start.12
  355.2 4.4 %copy-start.18 = (f32[2304]{0:T(1024)S(1)}, f32[2304]{0:T(1024)}, u32[]{:S(2)}) copy-start(f32[2304]{0:T(1024)} %param.42) | copy-start | bytes 27652
  355.2 4.4 %copy-start.19 = (f32[2304]{0:T(1024)S(1)}, f32[2304]{0:T(1024)}, u32[]{:S(2)}) copy-start(f32[2304]{0:T(1024)} %reshape.202) | copy-start | bytes 27652
  355.2 4.4 %copy-start.20 = (f32[2304]{0:T(1024)S(1)}, f32[2304]{0:T(1024)}, u32[]{:S(2)}) copy-start(f32[2304]{0:T(1024)} %param.44) | copy-start | bytes 27652
  355.2 4.4 %copy-start.21 = (f32[2304]{0:T(1024)S(1)}, f32[2304]{0:T(1024)}, u32[]{:S(2)}) copy-start(f32[2304]{0:T(1024)} %param.43) | copy-start | bytes 27652
  355.2 5.1 %copy-start.4 = (f32[192,3072]{1,0:T(8,128)S(1)}, f32[192,3072]{1,0:T(8,128)}, u32[]{:S(2)}) copy-start(f32[192,3072]{1,0:T(8,128)} %wu.1) | copy-start | bytes 7077892
  355.2 5.1 %copy-start.5 = (f32[192,3072]{1,0:T(8,128)S(1)}, f32[192,3072]{1,0:T(8,128)}, u32[]{:S(2)}) copy-start(f32[192,3072]{1,0:T(8,128)} %param.38) | copy-start | bytes 7077892
  355.2 5.7 %copy-start.6 = (f32[192,3072]{1,0:T(8,128)S(1)}, f32[192,3072]{1,0:T(8,128)}, u32[]{:S(2)}) copy-start(f32[192,3072]{1,0:T(8,128)} %param.37) | copy-start | bytes 7077892
  355.2 5.9 %copy-start.11 = (bf16[192,3072]{1,0:T(8,128)(2,1)S(1)}, bf16[192,3072]{1,0:T(8,128)(2,1)}, u32[]{:S(2)}) copy-start(bf16[192,3072]{1,0:T(8,128)(2,1)} %get-tuple-element.76) | copy-start | bytes 3538948
  361.2 4.2 %copy-start.9 = (bf16[4,208,768]{2,1,0:T(8,128)(2,1)S(1)}, bf16[4,208,768]{2,1,0:T(8,128)(2,1)}, u32[]{:S(2)}) copy-start(bf16[4,208,768]{2,1,0:T(8,128)(2,1)} %get-tuple-element.55) | copy-start | bytes 3833860
  366.8 9.2 %copy-start = (f32[4,208,768]{2,1,0:T(8,128)S(1)}, f32[4,208,768]{2,1,0:T(8,128)}, u32[]{:S(2)}) copy-start(f32[4,208,768]{2,1,0:T(8,128)} %get-tuple-element.73) | copy-start | bytes 7667716

commit v5 on v4

--- a/solution.py
+++ b/solution.py
@@ -630,12 +630,14 @@
     bf, f32 = jnp.bfloat16, jnp.float32
     loads = [pltpu.make_async_copy(a, b, in_sem.at[n]) for n, (a, b) in enumerate(
         [(o_in, o_s), (wo, wo_s), (vec, vec_s), (x_in, h_s), (dy_in, dy_s), (wu, wu_s), (wd, wd_s)])]
-    for copy in loads:
+    for copy in loads[:4]:
         copy.start()
     vp_s[...] = jnp.zeros_like(vp_s)
     zero = jnp.zeros((1, D), f32)
     for n in range(4):
         loads[n].wait()
+    for copy in loads[4:]:
+        copy.start()
     flat = lambda ref: ref[...].reshape(4 * SP, D)
 
     def branch(t, _):
@@ -660,34 +662,29 @@
     for n in range(4, 7):
         loads[n].wait()
 
-    def tile(n, _):
-        at = pl.multiple_of(n * 256, 256)
-        cols = pl.ds(at, 256)
-        low = pl.ds(pl.multiple_of((n % 3) * 256, 256), 256)
-        u = mm(flat(n_s), wu_s[:, cols]) + bu_s[n, 0:1, :]
-        cdf = 0.5 * (1.0 + lax.erf(u * 0.7071067811865476))
-        a = (u * cdf).astype(bf)
-        slope = cdf + u * (jnp.exp(u * u * -0.5) * 0.3989422804014327)
-        da = mm(flat(dy_s), wd_s[cols, :], NT)
-        du = (da * slope).astype(bf)
-        a_s[:, low] = a
-        du_s[:, low] = du
-        gd_s[cols, :] = mm(jnp.transpose(a), flat(dy_s)).astype(bf)
-        gu_s[:, cols] = mm(nt_s[...], du).astype(bf)
-        gbu_s[n, 0:1, :] = jnp.sum(du.astype(f32), axis=0, keepdims=True)
-
-        @pl.when(n % 3 == 2)
-        def _():
-            start = pl.multiple_of((n // 3) * D, D)
-
-            def add(t, _):
-                out = pl.ds(pl.multiple_of(t * 256, 256), 256)
-                mlp_s[:, out] += mm(a_s[...], wd_s[pl.ds(start, D), out])
-                dn_s[:, out] += mm(du_s[...], wu_s[out, pl.ds(start, D)], NT)
-                return 0
-            lax.fori_loop(0, 3, add, 0)
+    def group(g, _):
+        start = pl.multiple_of(g * D, D)
+        for k in range(3):
+            n, low = 3 * g + k, slice(256 * k, 256 * k + 256)
+            cols = pl.ds(pl.multiple_of(g * D + k * 256, 256), 256)
+            u = mm(flat(n_s), wu_s[:, cols]) + bu_s[n, 0:1, :]
+            cdf = 0.5 * (1.0 + lax.erf(u * 0.7071067811865476))
+            a = (u * cdf).astype(bf)
+            slope = cdf + u * (jnp.exp(u * u * -0.5) * 0.3989422804014327)
+            da = mm(flat(dy_s), wd_s[cols, :], NT)
+            du = (da * slope).astype(bf)
+            a_s[:, low] = a
+            du_s[:, low] = du
+            gd_s[cols, :] = mm(jnp.transpose(a), flat(dy_s)).astype(bf)
+            gu_s[:, cols] = mm(nt_s[...], du).astype(bf)
+            gbu_s[n, 0:1, :] = jnp.sum(du.astype(f32), axis=0, keepdims=True)
+        for t in range(3):
+            out = slice(256 * t, 256 * t + 256)
+            mlp_s[:, out] += mm(a_s[...], wd_s[pl.ds(start, D), out])
+            dn_s[:, out] += mm(du_s[...], wu_s[out, pl.ds(start, D)], NT)
         return 0
-    lax.fori_loop(0, 12, tile, 0)
+
+    lax.fori_loop(0, 4, group, 0)
     for n, z, r, at in spots:
         vp_s[z, r : r + 1, at : at + 256] = gbu_s[n, 0:1, :]
     puts = []
@@ -772,7 +769,8 @@
 class Sums:
     AX, AY, AC0, ADA, ADB, AC1, AC2, AC3 = range(31, 39)
 
-    def __init__(self, n_items, grads, outs, bufs, sems):
+    def __init__(self, n_items, grads, outs, bufs, sems, gathers=True):
+        self.gathers = gathers
         self.grads, self.outs = grads, outs
         self.sums, self.crecv, self.r1, self.r2, self.r3, self.fin, self.ext = bufs
         self.g_send, self.g_recv, self.e_send, self.e_recv, self.half_sem, self.put_sem = sems
@@ -792,10 +790,10 @@
             self.extra.append(bit)
             bit *= 2
 
-    def greet(self):
+    def greet(self, *more):
         barrier = pltpu.get_barrier_semaphore()
         partners = [self.c_dev, self.x_dev, self.y_dev] + [(self.i, z) for z in self.zs]
-        partners += [(self.flip(self.i, b), self.f) for b in self.extra]
+        partners += [(self.flip(self.i, b), self.f) for b in self.extra] + list(more)
         for dev in partners:
             pl.semaphore_signal(barrier, inc=1, device_id=dev, device_id_type=MESH)
         return lambda: pl.semaphore_wait(barrier, len(partners))
@@ -874,7 +872,7 @@
 
     @staticmethod
     def plus(ref, where, other_ref, other_where):
-        ref[where] = (ref[where].astype(jnp.float32) + other_ref[other_where].astype(jnp.float32)).astype(jnp.bfloat16)
+        ref[where] = ref[where] + other_ref[other_where]
 
     def step(self, w, stage):
         f32 = jnp.float32
@@ -914,12 +912,22 @@
                 copy.start()
                 copy.wait()
                 fin[...] = (fin[...].astype(f32) + self.ext[w][n].astype(f32)).astype(jnp.bfloat16)
-            pltpu.make_async_copy(fin, self.region(w, xy, self.core, 0), self.put_sem.at[w]).start()
-            for kind in (self.AX, self.AY, self.AC0):
-                self.a_copy(w, kind).start()
+            if self.gathers:
+                self.gather_begin(w)
+            else:
+                self.fin_put(w).start()
         if stage < 3:
             for copy in self.copies(w, stage + 1):
                 copy.start()
+
+    def fin_put(self, w):
+        dst = self.region(w, self.xy, self.core, 0) if self.gathers else self.outs[w]
+        return pltpu.make_async_copy(self.fin[w], dst, self.put_sem.at[w])
+
+    def gather_begin(self, w):
+        self.fin_put(w).start()
+        for kind in (self.AX, self.AY, self.AC0):
+            self.a_copy(w, kind).start()
 
     def gather_one(self, w):
         self.a_arrival(w, self.AX).wait_recv()
@@ -937,14 +945,18 @@
     def gather_three(self, w):
         for kind in (self.AC0, self.AC1, self.AC2, self.AC3):
             self.a_arrival(w, kind).wait_recv()
-        pltpu.make_async_copy(self.fin[w], self.region(w, self.xy, self.core, 0), self.put_sem.at[w]).wait()
-
-    def finish(self, w):
-        for stage in range(4):
-            for copy in self.copies(w, stage):
-                copy.wait_send()
-        for kind in range(self.AX, self.AC3 + 1):
-            self.a_copy(w, kind).wait_send()
+        self.fin_put(w).wait()
+
+    def finish(self, w, sums=True):
+        if sums:
+            for stage in range(4):
+                for copy in self.copies(w, stage):
+                    copy.wait_send()
+        if self.gathers:
+            for kind in range(self.AX, self.AC3 + 1):
+                self.a_copy(w, kind).wait_send()
+        else:
+            self.fin_put(w).wait()
 
 
 def sums_scratch(n_items, shapes):
@@ -966,31 +978,45 @@
 
 
 def back_kernel(
-    n_items, tab_ref, q_in, k_in, v_in, o_in, do_in, lse_in, nt_in, wq_in, gd, gu, go,
-    dq_out, part_out, gq_out, bias_out, gd_out, gu_out, go_out,
-    q_s, k_s, v_s, o_s, do_s, lse_s, nt_s, wq_s, pk_s, pv_s, gq_s, bias_s, load_sem, out_sem, *rest,
+    n_items, tab_ref, q_in, k_in, v_in, o_in, do_in, lse_in, nt_in, wq_in, y_in, gd, gu, go,
+    y_out, dq_out, part_out, gq_out, bias_out, gd_out, gu_out, go_out,
+    q_s, k_s, v_s, o_s, do_s, lse_s, nt_s, wq_s, pk_s, pv_s, gq_s, bias_s, load_sem, out_sem, y_send, y_recv, *rest,
 ):
     bf, f32 = jnp.bfloat16, jnp.float32
-    net = Sums(n_items, (gd, gu, go), (gd_out, gu_out, go_out), split_refs(rest[:21], 3), rest[21:])
-    ready = net.greet()
+    net = Sums(n_items, (gd, gu, go), (gd_out, gu_out, go_out), split_refs(rest[:21], 3), rest[21:], False)
+    i, f, core, stay, mine, other, far, flip = place()
+    m_dev = (flip(i, 1), 3 - f)
+    ready = net.greet(m_dev)
     loads = [pltpu.make_async_copy(a, b, load_sem.at[n]) for n, (a, b) in enumerate(
         [(q_in, q_s), (k_in, k_s), (v_in, v_s), (o_in, o_s), (do_in, do_s), (lse_in, lse_s), (nt_in, nt_s), (wq_in, wq_s)])]
-    for copy in loads:
+    for copy in loads[:6]:
         copy.start()
     ready()
     for w in range(3):
         net.begin(w)
+    y_stay = pltpu.make_async_copy(y_in, y_out, y_send.at[0])
+
+    def y_copy(j):
+        return net.remote(y_in.at[j], y_out.at[j], y_send.at[j], y_recv.at[j], m_dev)
+
+    @pl.when(stay)
+    def _():
+        y_stay.start()
+
+    @pl.when(jnp.logical_not(stay))
+    def _():
+        for j in range(4):
+            y_copy(j).start()
+
     for n in range(6):
         loads[n].wait()
+    for copy in loads[6:]:
+        copy.start()
     lane = lax.broadcasted_iota(jnp.int32, (SP, 128), 1)
     row = lax.broadcasted_iota(jnp.int32, (SP, D), 0)
-    plan = ((2, 0, 0), (4, 1, 0), (6, 2, 0), (9, 0, 1), (14, 1, 1), (16, 2, 1), (18, 0, 2), (22, 1, 2))
-
-    def one(step, _):
-        for at, w, stage in plan:
-            @pl.when(step == at)
-            def _():
-                net.step(w, stage)
+    plan = ((1, 0, 0), (2, 1, 0), (3, 2, 0), (5, 0, 1), (7, 1, 1), (8, 2, 1), (9, 0, 2), (11, 1, 2))
+
+    def attend_back(step):
         j, b = step // 6, step % 6
         cols = pl.ds(pl.multiple_of(b * 128, 128), 128)
         parts = [k_s[tab_ref[0, j * NK + t], :, cols] for t in range(NK)]
@@ -1024,9 +1050,17 @@
         for t in range(NK):
             pk_s[j * NK + t, :, cols] = dk[t * SP : (t + 1) * SP].astype(bf)
             pv_s[j * NK + t, :, cols] = dv[t * SP : (t + 1) * SP].astype(bf)
+
+    def one(step, _):
+        for at, w, stage in plan:
+            @pl.when(step == at)
+            def _():
+                net.step(w, stage)
+        for half in range(2):
+            attend_back(2 * step + half)
         return 0
 
-    lax.fori_loop(0, 24, one, 0)
+    lax.fori_loop(0, 12, one, 0)
     puts = []
 
     def put(src, dst):
@@ -1069,8 +1103,6 @@
     net.step(2, 3)
     lax.fori_loop(2, 4, partial_rows, 0)
     put(pk_s.at[pl.ds(0, 16)], part_out)
-    net.gather_one(0)
-    mine = place()[4]
 
     def grad_q(t, _):
         cols = pl.ds(pl.multiple_of(t * 256, 256), 256)
@@ -1090,11 +1122,8 @@
                 gq_s[:, :, :, pl.ds(pl.multiple_of(D + t * 256, 256), 256)] = g.astype(bf).reshape(4, 4, D // 16, 256)
         return 0
     lax.fori_loop(0, 3, grad_kv, 0)
-    net.gather_one(1)
-    net.gather_two(0)
     lax.fori_loop(3, 6, grad_kv, 0)
     put(gq_s, gq_out)
-    net.gather_one(2)
 
     def bias_sums(slot, carry):
         bias_q, bias_v = carry
@@ -1108,17 +1137,23 @@
     bias_s[1:2, :] = bias_v
     bias_s[2:8, :] = jnp.zeros((6, D), f32)
     put(bias_s, bias_out)
-    net.gather_two(1)
-    net.gather_two(2)
-    for w in range(3):
-        net.gather_three(w)
     for w in range(3):
         net.finish(w)
+
+    @pl.when(stay)
+    def _():
+        y_stay.wait()
+
+    @pl.when(jnp.logical_not(stay))
+    def _():
+        for j in range(4):
+            y_copy(j).wait()
+
     for copy in puts:
         copy.wait()
 
 
-def back(n_items, tab, q, k, v_, o, do, lse, nt, wq, gd, gu, go):
+def back(n_items, tab, q, k, v_, o, do, lse, nt, wq, y, gd, gu, go):
     bf, f32 = jnp.bfloat16, jnp.float32
     S = jax.ShapeDtypeStruct
     hb = pl.BlockSpec(memory_space=pltpu.HBM)
@@ -1128,31 +1163,35 @@
     bufs, sems = sums_scratch(n_items, [(g.shape[2], g.shape[3] // 2) for g in (gd, gu, go)])
     return pl.pallas_call(
         functools.partial(back_kernel, n_items),
-        out_shape=(S(rows, bf), S((16, SP, D), bf), S((4, 4, D // 16, 3 * D), bf), S((8, D), f32))
-        + tuple(S((4 * g.shape[2], g.shape[3]), bf) for g in (gd, gu, go)),
-        in_specs=[SM] + [hb] * 11,
-        out_specs=(hb,) * 7,
+        out_shape=(S(rows, bf), S(rows, bf), S((16, SP, D), bf), S((4, 4, D // 16, 3 * D), bf), S((8, D), f32))
+        + tuple(S((g.shape[2], g.shape[3] // 2), bf) for g in (gd, gu, go)),
+        in_specs=[SM] + [hb] * 12,
+        out_specs=(hb,) * 8,
         scratch_shapes=[
             v(rows), v((16, SP, D)), v((16, SP, D)), v(rows), v(rows), v((4, 6, 8, SP), f32), v((4, D, 4 * SP)),
-            v((D, 3 * D)), v((24, SP, D)), v((24, SP, D)), v((4, 4, D // 16, 3 * D)), v((8, D), f32), dma((8,)), dma((4,)),
+            v((D, 3 * D)), v((24, SP, D)), v((24, SP, D)), v((4, 4, D // 16, 3 * D)), v((8, D), f32), dma((8,)), dma((4,)), dma((4,)), dma((4,)),
         ] + bufs + sems,
         compiler_params=pltpu.CompilerParams(
             collective_id=3, has_side_effects=True, vmem_limit_bytes=63 * 2**20),
         cost_estimate=pl.CostEstimate(
             flops=2 * 5 * 24 * 12 * SP * SP * 256, bytes_accessed=60 * 2**20, transcendentals=24 * 12 * SP * SP),
         name="back",
-    )(tab, q, k, v_, o, do, lse, nt, wq, gd, gu, go)
+    )(tab, q, k, v_, o, do, lse, nt, wq, y, gd, gu, go)
 
 
 def tail_kernel(
-    n_items, gq, part, dq, x_in, dh, wq, vec, vp, bias,
-    tg_out, vec_out, gq_out,
-    dq_s, x_s, dh_s, wq_s, vec_s, vp_s, bias_s, mine_s, far_mine_s, far_s, near_s, far_e, vb_s,
-    load_sem, out_sem, p_send, p_recv, vb_send, vb_recv, *rest,
+    n_items, gq, part, dq, x_in, dh, wq, vec, vp, bias, fd, fu, fo,
+    tg_out, tb_out, vec_out, gq_out, gd_out, gu_out, go_out,
+    dq_s, x_s, dh_s, wq_s, vec_s, vp_s, bias_s, mine_s, far_mine_s, far_s, near_s, far_e, cut_s, vb_s,
+    load_sem, out_sem, low_sem, late_send, late_recv, late_put, p_send, p_recv, vb_send, vb_recv, *rest,
 ):
     bf, f32 = jnp.bfloat16, jnp.float32
     net = Sums(n_items, (gq,), (gq_out,), split_refs(rest[:7], 1), rest[7:])
     i, f, core, stay, mine, other, far, flip = place()
+    shapes = [jax.ShapeDtypeStruct((4, 4) + r.shape, bf) for r in (fd, fu, fo)]
+    late = Sums(n_items, (None,) * 3, (gd_out, gu_out, go_out), (shapes,) + (None,) * 4 + ((fd, fu, fo), None),
+                (late_send, late_recv, None, None, None, late_put))
+    late.AX, late.AY, late.AC0, late.ADA, late.ADB, late.AC1, late.AC2, late.AC3 = range(8)
     ready = net.greet()
     loads = [pltpu.make_async_copy(a, b, load_sem.at[n]) for n, (a, b) in enumerate(
         [(part.at[far], far_mine_s), (dq, dq_s), (wq.at[:, pl.ds(0, D)], wq_s), (part.at[mine], mine_s), (vec, vec_s),
@@ -1173,6 +1212,8 @@
     for j in range(4):
         far_copy(j).start()
     net.begin(0)
+    for w in range(3):
+        late.gather_begin(w)
     for j in range(4):
         near_copy(j).start()
     loads[0].wait()
@@ -1181,6 +1222,7 @@
         net.plus(far_mine_s, (j,), far_s, (j,))
         chip_copy(j).start()
     net.step(0, 0)
+    late.gather_one(2)
     for n in range(1, 9):
         loads[n].wait()
     zero = jnp.zeros((1, D), f32)
@@ -1197,18 +1239,26 @@
         dn = dn + far_e[j].astype(f32)
         gains = gains + jnp.sum(dn * unit, axis=0, keepdims=True)
         shifts = shifts + jnp.sum(dn, axis=0, keepdims=True)
-        x_s[j] = dh_s[j] + norm_grad(dn * gain, unit, scale)
+        grad = dh_s[j] + norm_grad(dn * gain, unit, scale)
+        cut_s[j] = grad[:FRAME_TOK]
+        dq_s[j] = grad.astype(bf)
         return gains, shifts
 
     def slot_out(j):
-        return pltpu.make_async_copy(x_s.at[j], tg_out.at[j], out_sem.at[j])
+        return pltpu.make_async_copy(cut_s.at[j], tg_out.at[j], out_sem.at[j])
+
+    def low_out(j):
+        return pltpu.make_async_copy(dq_s.at[j], tb_out.at[j], low_sem.at[j])
 
     carry = (zero, zero)
     for j in range(4):
         if j == 2:
             net.step(0, 1)
+            late.gather_one(0)
+            late.gather_one(1)
         carry = norm_back(j, carry)
         slot_out(j).start()
+        low_out(j).start()
     vp_s[0, 0:1, :] = carry[0]
     vp_s[0, 1:2, :] = carry[1]
     ring = [net.c_dev, net.x_dev, net.y_dev, (i, net.zs[0]), (i, net.zs[1])] + [(flip(i, b), f) for b in net.extra]
@@ -1224,6 +1274,8 @@
 
     v_copy(0).start()
     net.step(0, 2)
+    for w in range(3):
+        late.gather_two(w)
     v_step(0)
     v_step(1)
     net.step(0, 3)
@@ -1237,15 +1289,19 @@
     vec_put.start()
     net.gather_three(0)
     net.finish(0)
+    for w in range(3):
+        late.gather_three(w)
+        late.finish(w, False)
     for j in range(4):
         far_copy(j).wait_send()
         near_copy(j).wait_send()
         chip_copy(j).wait_send()
         slot_out(j).wait()
+        low_out(j).wait()
     vec_put.wait()
 
 
-def tail(n_items, gq, part, dq, x_in, dh, wq, vec, vp, bias):
+def tail(n_items, gq, part, dq, x_in, dh, wq, vec, vp, bias, fd, fu, fo):
     bf, f32 = jnp.bfloat16, jnp.float32
     S = jax.ShapeDtypeStruct
     hb = pl.BlockSpec(memory_space=pltpu.HBM)
@@ -1258,19 +1314,20 @@
         steps += 1
     return pl.pallas_call(
         functools.partial(tail_kernel, n_items),
-        out_shape=(S(rows, f32), S((8, D), f32), S((D // 4, 3 * D), bf)),
-        in_specs=[hb] * 9,
-        out_specs=(hb,) * 3,
+        out_shape=(S((4, FRAME_TOK, D), f32), S(rows, bf), S((8, D), f32), S((D // 4, 3 * D), bf))
+        + tuple(S((4 * r.shape[0], 2 * r.shape[1]), bf) for r in (fd, fu, fo)),
+        in_specs=[hb] * 12,
+        out_specs=(hb,) * 7,
         scratch_shapes=[
             v(rows), v(rows, f32), v(rows, f32), v((D, D)), v((4, VEC_ROWS, D)), v((4, 8, D), f32), v((8, D), f32),
-            v(rows), v(rows), v(rows), v(rows), v(rows), v((steps, 4, 8, D), f32),
-            dma((9,)), dma((5,)), dma((3, 4)), dma((3, 4)), dma((steps,)), dma((steps,)),
+            v(rows), v(rows), v(rows), v(rows), v(rows), v((4, FRAME_TOK, D), f32), v((steps, 4, 8, D), f32),
+            dma((9,)), dma((5,)), dma((4,)), dma((3, 8)), dma((3, 8)), dma((3,)), dma((3, 4)), dma((3, 4)), dma((steps,)), dma((steps,)),
         ] + bufs + sems,
         compiler_params=pltpu.CompilerParams(
             collective_id=2, has_side_effects=True, vmem_limit_bytes=60 * 2**20),
         cost_estimate=pl.CostEstimate(flops=2 * 14 * 784 * 768 * 768, bytes_accessed=60 * 2**20, transcendentals=0),
         name="tail",
-    )(gq, part, dq, x_in, dh, wq, vec, vp, bias)
+    )(gq, part, dq, x_in, dh, wq, vec, vp, bias, fd, fu, fo)
 
 
 def on_device(
@@ -1306,9 +1363,6 @@
             if k % 2 != z // 2:
                 swap.append((k * 4 + z, (k ^ 1) * 4 + 3 - z))
 
-    def to_worker(array):
-        return jnp.where(stay, array, lax.ppermute(array, ("items", "frames"), swap))
-
     pad = lambda a: jnp.pad(a[0], ((0, 0), (0, SP - FRAME_TOK), (0, 0)))
     item_index, is_valid = slot_items(item_dates[0], slot_frame[0], frame_mask[0])
     own_items = lax.dynamic_slice_in_dim(item_index, f * 4, 4)
@@ -1321,21 +1375,20 @@
         qkv_weight, out_weight, up_weight, down_weight)
     block_out, hidden_grad, do3, down_grad, up_grad, out_grad, vector_part = mid(
         o3, x3, dy, vec_all, wo, wu, wd)
-    block_out = to_worker(block_out)
     blocks = lambda g: g.reshape(4, 4, g.shape[0] // 16, g.shape[1])
-    dq3, part, gq, bias_part, down_sum, up_sum, out_sum = back(
-        n_items, tab_own, q3, k3, v3, o3, do3, lse, nt, wq, blocks(down_grad), blocks(up_grad), blocks(out_grad))
-    token_grad, vector_sum, qkv_sum = tail(
-        n_items, gq, part.reshape(4, 4, SP, D), dq3, x3, hidden_grad, wq, vec_all, vector_part, bias_part)
-    token_grad = jnp.where(
-        stay, token_grad, lax.ppermute(token_grad.astype(bf), ("items", "frames"), swap).astype(f32))
+    block_out, dq3, part, gq, bias_part, *regions = back(
+        n_items, tab_own, q3, k3, v3, o3, do3, lse, nt, wq, block_out, blocks(down_grad), blocks(up_grad), blocks(out_grad))
+    token_grad, token_low, vector_sum, qkv_sum, down_sum, up_sum, out_sum = tail(
+        n_items, gq, part.reshape(4, 4, SP, D), dq3, x3, hidden_grad, wq, vec_all, vector_part, bias_part, *regions)
+    home = lax.ppermute(token_low, ("items", "frames"), swap)
+    token_grad = jnp.where(stay, token_grad, home[:, :FRAME_TOK].astype(f32))
     qkv_new = adamw(qkv_weight, qkv_first, qkv_second, qkv_sum.astype(f32), 0.05, 0.05)
     out_new = adamw(out_weight, out_first, out_second, out_sum.astype(f32), 0.5, 0.05)
     up_new = adamw(up_weight, up_first, up_second, up_sum.astype(f32), 0.05, 0.05)
     down_new = adamw(down_weight, down_first, down_second, down_sum.astype(f32), 0.03, 0.05)
     vector_new = adamw(vectors, vector_first, vector_second, vector_sum[:3].reshape(3 * D), 0.3, 0.0)
     cut = lambda a: a.reshape(1, 4, SP, D)[:, :, :FRAME_TOK]
-    return (cut(block_out), cut(token_grad)) + qkv_new + out_new + up_new + down_new + vector_new
+    return (cut(block_out), token_grad[None]) + qkv_new + out_new + up_new + down_new + vector_new
 
 
 def solution(mesh):

time: 388 us -> 374 us (0.964)
  Pallas kernels: 324 us -> 318 us
  starting transfers between devices: 6.84 us -> 1.92 us
    pallas_call x1, Pallas kernels: 48 us -> 42.8 us  [mid(): pl.pallas_call(mid_kernel, out_shape=(S(rows, bf), S(rows, f32), S(rows,...]
    ppermute x2 -> x1, starting transfers between devices: 6.84 us -> 1.92 us  [on_device(): home = lax.ppermute(token_low, ('items', 'frames'), swap)]
    ppermute x2 -> x1, waiting for transfers between devices: 7.65 us -> 8.98 us  [on_device(): home = lax.ppermute(token_low, ('items', 'frames'), swap)]
  transfers between devices with their start and end apart: 2 -> 1, of which waited for: 1 -> 1; matrix products, arithmetic and copies ran while one was open for 6% -> 5% of each run, Pallas kernels for 43% -> 0%
where the time goes in v5:
time: 374 us; the launch traced here: 367 us
  Pallas kernels  318 us (85%)
  other arithmetic  24.4 us (7%)
  local copies, waits for them, and re-layouts  12.5 us (3%)
  waiting for transfers between devices  8.98 us (2%)
    pallas_call x1, Pallas kernels, front(): pl.pallas_call(front_kernel, out_shape=(S(rows, bf), S(every, bf), S(ever...  113 us
    pallas_call x1, Pallas kernels, back(): pl.pallas_call(functools.partial(back_kernel, n_items), out_shape=(S(rows...  107 us
    pallas_call x1, Pallas kernels, tail(): pl.pallas_call(functools.partial(tail_kernel, n_items), out_shape=(S((4,...  56 us
    pallas_call x1, Pallas kernels, mid(): pl.pallas_call(mid_kernel, out_shape=(S(rows, bf), S(rows, f32), S(rows,...  42.8 us
    sub x5, other arithmetic, adamw(): weight - step_rate * (first_hat / (jnp.sqrt(second_hat) + 1e-08) + decay...  17.6 us
    ppermute x1, waiting for transfers between devices, on_device(): home = lax.ppermute(token_low, ('items', 'frames'), swap)  8.98 us
  transfers between devices with their start and end apart: 1, of which 1 were waited for; matrix products, arithmetic and copies ran while one was open for 5% of the time, Pallas kernels for 0%

profile of v5, /device:TPU:13, one launch (start us, length us, event | category | flops | bytes accessed | tf_op | source)
XLA Modules:
  0.0 367.4 jit_solution(2654359946871026116)
XLA Ops:
  0.7 0.8 reduce-window.4
  1.5 0.7 fusion.13
  2.2 0.7 convert_reduce_fusion
  2.9 0.7 compare_reduce_fusion
  3.6 0.1 dynamic_slice.3
  3.7 0.7 fusion.12
  4.4 0.2 convert_reduce_fusion.1
  4.6 0.1 fusion.11
  4.6 0.1 reshape.199
  4.7 0.2 reduce_window_sum.18
  4.9 0.2 select_reduce_fusion
  5.1 0.1 copy.46
  5.2 0.1 reshape.191
  5.3 0.1 select_reduce_fusion.1
  5.5 0.1 concatenate.7
  5.5 0.6 pad.27.tab
  6.1 0.7 convert_element_type.86
  6.9 1.5 copy.52
  8.4 0.6 pad.28.vec
  9.0 1.1 pad.23.tok
  10.1 0.1 copy.51
  10.3 1.1 pad.24.cot
  11.4 0.1 multiply_sine_fusion.1
  11.5 0.1 select_maximum_fusion
  11.6 0.6 pad.26.tmp
  12.2 113.1 %front.1 = (bf16[4,208,768]{2,1,0:T(8,128)(2,1)}, bf16[16,208,768]{2,1,0:T(8,128)(2,1)}, bf16[16,208,768]{2,1,0:T(8,128)(2,1)}, bf16[4,208,768]{2,1,0:T(8,128)(2...) custom-call(bf16[4,208,768]{2,1,0:T(8,128)(2,1)} %pad.23.tok, ...), custom_call_target="tpu_custom_call" | custom-call | flops 8323596288 | bytes 41943040 | tf_op jit(solution)/shard_map/front/pallas_call | solution.py:589
  125.3 42.8 %mid.1 = (bf16[4,208,768]{2,1,0:T(8,128)(2,1)}, f32[4,208,768]{2,1,0:T(8,128)}, bf16[4,208,768]{2,1,0:T(8,128)(2,1)}, bf16[3072,768]{1,0:T(8,128)(2,1)}, bf16[76...) custom-call(bf16[4,208,768]{2,1,0:T(8,128)(2,1)} %get-tuple-element.57.o_in, ...), custom_call_target="tpu_custom_call" | custom-call | flops 26499612672 | bytes 41943040 | tf_op jit(solution)/shard_map/mid/pallas_call | solution.py:751
  168.2 106.6 %back.1 = (bf16[4,208,768]{2,1,0:T(8,128)(2,1)}, bf16[4,208,768]{2,1,0:T(8,128)(2,1)}, bf16[16,208,768]{2,1,0:T(8,128)(2,1)}, bf16[4,4,48,2304]{3,2,1,0:T(8,128)...) custom-call(s32[8,128]{1,0:T(8,128)} %get-tuple-element.53.tab_ref, ...), custom_call_target="tpu_custom_call" | custom-call | flops 31897681920 | bytes 62914560 | tf_op jit(solution)/shard_map/back/pallas_call | solution.py:1164
  274.7 56.0 %tail.1 = (f32[4,196,768]{2,1,0:T(8,128)}, bf16[4,208,768]{2,1,0:T(8,128)(2,1)}, f32[8,768]{1,0:T(8,128)}, bf16[192,2304]{1,0:T(8,128)(2,1)}, bf16[768,768]{1,0:...) custom-call(bf16[4,4,48,2304]{3,2,1,0:T(8,128)(2,1)} %get-tuple-element.73.gq, ...), custom_call_target="tpu_custom_call" | custom-call | flops 12947816448 | bytes 62914560 | tf_op jit(solution)/shard_map/tail/pallas_call | solution.py:1315
  330.7 1.9 collective-permute-start
  332.7 0.1 slice.12
  332.8 1.5 copy.47
  334.3 0.6 reshape.198
  334.9 3.3 multiply_subtract_fusion.3
  338.2 0.0 copy-start.2
  338.2 0.0 copy-start.3
  338.2 5.1 %multiply_subtract_fusion.2 = (f32[192,2304]{1,0:T(8,128)}, f32[192,2304]{1,0:T(8,128)}, f32[192,2304]{1,0:T(8,128)}) fusion(f32[192,2304]{1,0:T(8,128)S(1)} %copy-done.7, bf16[192,2304]{1,0:T(8,128)(2,1)} %get-tuple-element.84, f32[192,2304]{1,0:T(8,128)S(1)} %copy-done.8, f32[192,2304]{1,0:T(8,128)} %param.31), kind=kLoop, calls=%fused_computation.15 | loop fusion | flops 7077888 | bytes 11501568 | tf_op jit(solution)/shard_map/sub | solution.py:135
  343.4 0.8 copy-done.12
  344.2 0.0 copy-start.4
  344.2 0.0 copy-start.5
  344.2 4.4 %multiply_subtract_fusion = (f32[768,768]{1,0:T(8,128)}, f32[768,768]{1,0:T(8,128)}, f32[768,768]{1,0:T(8,128)}) fusion(f32[768,768]{1,0:T(8,128)S(1)} %copy-done.1, bf16[768,768]{1,0:T(8,128)(2,1)S(1)} %copy-done.12, f32[768,768]{1,0:T(8,128)S(1)} %copy-done.2, f32[768,768]{1,0:T(8,128)S(1)} %copy-done.3), kind=kLoop, calls=%fused_computation.10 | loop fusion | flops 9437184 | bytes 15335424 | tf_op jit(solution)/shard_map/sub | solution.py:135
  348.6 0.6 multiply_subtract_fusion.4
  349.2 0.6 copy-done.6
  349.9 0.3 copy-done.11
  350.2 4.2 %multiply_subtract_fusion.1 = (f32[192,3072]{1,0:T(8,128)}, f32[192,3072]{1,0:T(8,128)}, f32[192,3072]{1,0:T(8,128)}) fusion(f32[192,3072]{1,0:T(8,128)S(1)} %copy-done.4, bf16[192,3072]{1,0:T(8,128)(2,1)S(1)} %copy-done.11, f32[192,3072]{1,0:T(8,128)S(1)} %copy-done.5, f32[192,3072]{1,0:T(8,128)S(1)} %copy-done.6), kind=kLoop, calls=%fused_computation.11 | loop fusion | flops 9437184 | bytes 15335424 | tf_op jit(solution)/shard_map/sub | solution.py:135
  354.3 9.0 %collective-permute-done = bf16[4,208,768]{2,1,0:T(8,128)(2,1)} collective-permute-done((bf16[4,208,768]{2,1,0:T(8,128)(2,1)}, bf16[4,208,768]{2,1,0:T(8,128)(2,1)}, u32[]{:S(2)}, u32[]{:S(2)}) %collective-permute-start) | collective-permute-done | bytes 1277984 | tf_op jit(solution)/shard_map/ppermute | solution.py:1383
  363.3 1.5 select_bitcast_fusion
  364.8 2.4 copy.48
  (42 shorter events, 0.1 us)
Async XLA Ops:
  6.9 3.3 copy-start.9
  10.1 1.3 copy-start.18
  10.1 1.3 copy-start.19
  274.7 57.9 %copy-start.10 = (bf16[4,208,768]{2,1,0:T(8,128)(2,1)S(1)}, bf16[4,208,768]{2,1,0:T(8,128)(2,1)}, u32[]{:S(2)}) copy-start(bf16[4,208,768]{2,1,0:T(8,128)(2,1)} %get-tuple-element.72) | copy-start | bytes 3833860
  330.7 32.6 %collective-permute-start = (bf16[4,208,768]{2,1,0:T(8,128)(2,1)}, bf16[4,208,768]{2,1,0:T(8,128)(2,1)}, u32[]{:S(2)}, u32[]{:S(2)}) collective-permute-start(bf16[4,208,768]{2,1,0:T(8,128)(2,1)} %get-tuple-element.83), channel_id=1, source_target_pairs={{2,5},{3,4},{4,3},{5,2},{10,13},{11,12},{12,11},{13,10},{18,21},{1... | collective-permute-start | bytes 3833864 | tf_op jit(solution)/shard_map/ppermute | solution.py:1383
  332.7 1.6 copy-start.17
  334.3 3.9 %copy-start.7 = (f32[192,2304]{1,0:T(8,128)S(1)}, f32[192,2304]{1,0:T(8,128)}, u32[]{:S(2)}) copy-start(f32[192,2304]{1,0:T(8,128)} %wq.1) | copy-start | bytes 5308420
  334.3 3.9 %copy-start.8 = (f32[192,2304]{1,0:T(8,128)S(1)}, f32[192,2304]{1,0:T(8,128)}, u32[]{:S(2)}) copy-start(f32[192,2304]{1,0:T(8,128)} %param.32) | copy-start | bytes 5308420
  338.2 5.2 %copy-start.1 = (f32[768,768]{1,0:T(8,128)S(1)}, f32[768,768]{1,0:T(8,128)}, u32[]{:S(2)}) copy-start(f32[768,768]{1,0:T(8,128)} %wd.1) | copy-start | bytes 7077892
  338.2 5.2 %copy-start.2 = (f32[768,768]{1,0:T(8,128)S(1)}, f32[768,768]{1,0:T(8,128)}, u32[]{:S(2)}) copy-start(f32[768,768]{1,0:T(8,128)} %param.41) | copy-start | bytes 7077892
  338.2 5.2 %copy-start.3 = (f32[768,768]{1,0:T(8,128)S(1)}, f32[768,768]{1,0:T(8,128)}, u32[]{:S(2)}) copy-start(f32[768,768]{1,0:T(8,128)} %param.40) | copy-start | bytes 7077892
  338.2 5.9 %copy-start.12 = (bf16[768,768]{1,0:T(8,128)(2,1)S(1)}, bf16[768,768]{1,0:T(8,128)(2,1)}, u32[]{:S(2)}) copy-start(bf16[768,768]{1,0:T(8,128)(2,1)} %get-tuple-element.87) | copy-start | bytes 3538948
  344.2 4.4 %copy-start.13 = (f32[2304]{0:T(1024)S(1)}, f32[2304]{0:T(1024)}, u32[]{:S(2)}) copy-start(f32[2304]{0:T(1024)} %param.42) | copy-start | bytes 27652
  344.2 4.4 %copy-start.14 = (f32[2304]{0:T(1024)S(1)}, f32[2304]{0:T(1024)}, u32[]{:S(2)}) copy-start(f32[2304]{0:T(1024)} %reshape.198) | copy-start | bytes 27652
  344.2 4.4 %copy-start.15 = (f32[2304]{0:T(1024)S(1)}, f32[2304]{0:T(1024)}, u32[]{:S(2)}) copy-start(f32[2304]{0:T(1024)} %param.44) | copy-start | bytes 27652
  344.2 4.4 %copy-start.16 = (f32[2304]{0:T(1024)S(1)}, f32[2304]{0:T(1024)}, u32[]{:S(2)}) copy-start(f32[2304]{0:T(1024)} %param.43) | copy-start | bytes 27652
  344.2 5.1 %copy-start.4 = (f32[192,3072]{1,0:T(8,128)S(1)}, f32[192,3072]{1,0:T(8,128)}, u32[]{:S(2)}) copy-start(f32[192,3072]{1,0:T(8,128)} %wu.1) | copy-start | bytes 7077892
  344.2 5.1 %copy-start.5 = (f32[192,3072]{1,0:T(8,128)S(1)}, f32[192,3072]{1,0:T(8,128)}, u32[]{:S(2)}) copy-start(f32[192,3072]{1,0:T(8,128)} %param.38) | copy-start | bytes 7077892
  344.2 5.7 %copy-start.6 = (f32[192,3072]{1,0:T(8,128)S(1)}, f32[192,3072]{1,0:T(8,128)}, u32[]{:S(2)}) copy-start(f32[192,3072]{1,0:T(8,128)} %param.37) | copy-start | bytes 7077892
  344.2 5.9 %copy-start.11 = (bf16[192,3072]{1,0:T(8,128)(2,1)S(1)}, bf16[192,3072]{1,0:T(8,128)(2,1)}, u32[]{:S(2)}) copy-start(bf16[192,3072]{1,0:T(8,128)(2,1)} %get-tuple-element.86) | copy-start | bytes 3538948
  350.2 13.2 %copy-start = (f32[4,196,768]{2,1,0:T(8,128)S(1)}, f32[4,196,768]{2,1,0:T(8,128)}, u32[]{:S(2)}) copy-start(f32[4,196,768]{2,1,0:T(8,128)} %get-tuple-element.82) | copy-start | bytes 7225348

commit v6 on v5

--- a/solution.py
+++ b/solution.py
@@ -1013,7 +1013,6 @@
     for copy in loads[6:]:
         copy.start()
     lane = lax.broadcasted_iota(jnp.int32, (SP, 128), 1)
-    row = lax.broadcasted_iota(jnp.int32, (SP, D), 0)
     plan = ((1, 0, 0), (2, 1, 0), (3, 2, 0), (5, 0, 1), (7, 1, 1), (8, 2, 1), (9, 0, 2), (11, 1, 2))
 
     def attend_back(step):
@@ -1027,9 +1026,7 @@
         q, do, o = q_s[j, :, cols], do_s[j, :, cols], o_s[j, :, cols]
         prod_t = jnp.transpose(do.astype(f32) * o.astype(f32))
         logs = lse_s[j, b]
-        dk = jnp.zeros((NK * SP, 128), f32)
-        dv = jnp.zeros((NK * SP, 128), f32)
-        dq_t = []
+        dk_h, dv_h, dq_t = [], [], []
         for h in range(2):
             mine = (lane < 64) if h == 0 else (lane >= 64)
             spare = 64 if h == 0 else 0
@@ -1042,10 +1039,11 @@
             da_t = mm(vg, dom, NT)
             p = jnp.exp(s_t - logs[h : h + 1])
             ds = (p * (da_t - centre)).astype(bf)
-            dv = dv + mm(p.astype(bf), dom)
-            dk = dk + mm(ds, qm)
+            dv_h.append(mm(p.astype(bf), dom))
+            dk_h.append(mm(ds, qm))
             dq_t.append(mm(kg_t, ds))
         dq = jnp.transpose(jnp.concatenate([dq_t[0][:64], dq_t[1][64:]], axis=0))
+        dk, dv = dk_h[0] + dk_h[1], dv_h[0] + dv_h[1]
         q_s[j, :, cols] = (dq * 0.125).astype(bf)
         for t in range(NK):
             pk_s[j * NK + t, :, cols] = dk[t * SP : (t + 1) * SP].astype(bf)
@@ -1073,11 +1071,10 @@
 
     def combine(slot, _):
         first, second = tab_ref[0, 8 * NK + slot], tab_ref[0, 8 * NK + 16 + slot]
-        keep_a = jnp.logical_and(row < FRAME_TOK, tab_ref[0, 8 * NK + 32 + slot] > 0)
-        keep_b = jnp.logical_and(row < FRAME_TOK, tab_ref[0, 8 * NK + 48 + slot] > 0)
+        keep_a, keep_b = tab_ref[0, 8 * NK + 32 + slot] > 0, tab_ref[0, 8 * NK + 48 + slot] > 0
+        none = jnp.zeros((SP, D), bf)
         for out, part in ((k_s, pk_s), (v_s, pv_s)):
-            total = jnp.where(keep_a, part[first].astype(f32), 0.0) + jnp.where(keep_b, part[second].astype(f32), 0.0)
-            out[slot] = total.astype(bf)
+            out[slot] = jnp.where(keep_a, part[first], none) + jnp.where(keep_b, part[second], none)
         return 0
 
     lax.fori_loop(0, 16, combine, 0)
@@ -1252,10 +1249,14 @@
 
     carry = (zero, zero)
     for j in range(4):
-        if j == 2:
+        if j == 1:
             net.step(0, 1)
             late.gather_one(0)
             late.gather_one(1)
+        if j == 3:
+            net.step(0, 2)
+            for w in range(3):
+                late.gather_two(w)
         carry = norm_back(j, carry)
         slot_out(j).start()
         low_out(j).start()
@@ -1273,9 +1274,6 @@
             v_copy(n + 1).start()
 
     v_copy(0).start()
-    net.step(0, 2)
-    for w in range(3):
-        late.gather_two(w)
     v_step(0)
     v_step(1)
     net.step(0, 3)

time: 374 us -> 371 us (level)
  Pallas kernels: 318 us -> 314 us
where the time goes in v6:
time: 371 us; the launch traced here: 364 us
  Pallas kernels  314 us (85%)
  other arithmetic  24.4 us (7%)
  local copies, waits for them, and re-layouts  12.5 us (3%)
  waiting for transfers between devices  7.26 us (2%)
  starting transfers between devices  4.41 us (1%)
    pallas_call x1, Pallas kernels, front(): pl.pallas_call(front_kernel, out_shape=(S(rows, bf), S(every, bf), S(ever...  113 us
    pallas_call x1, Pallas kernels, back(): pl.pallas_call(functools.partial(back_kernel, n_items), out_shape=(S(rows...  106 us
    pallas_call x1, Pallas kernels, tail(): pl.pallas_call(functools.partial(tail_kernel, n_items), out_shape=(S((4,...  52.6 us
    pallas_call x1, Pallas kernels, mid(): pl.pallas_call(mid_kernel, out_shape=(S(rows, bf), S(rows, f32), S(rows,...  42.8 us
    sub x5, other arithmetic, adamw(): weight - step_rate * (first_hat / (jnp.sqrt(second_hat) + 1e-08) + decay...  17.6 us
  transfers between devices with their start and end apart: 1, of which 1 were waited for; matrix products, arithmetic and copies ran while one was open for 5% of the time, Pallas kernels for 0%

profile of v6, /device:TPU:13, one launch (start us, length us, event | category | flops | bytes accessed | tf_op | source)
XLA Modules:
  0.0 364.0 jit_solution(2069403172133434838)
XLA Ops:
  0.7 0.8 reduce-window.4
  1.5 0.7 fusion.13
  2.2 0.7 convert_reduce_fusion
  2.9 0.7 compare_reduce_fusion
  3.6 0.1 dynamic_slice.3
  3.7 0.7 fusion.12
  4.4 0.2 convert_reduce_fusion.1
  4.6 0.1 fusion.11
  4.6 0.1 reshape.199
  4.7 0.2 reduce_window_sum.18
  4.9 0.2 select_reduce_fusion
  5.1 0.1 copy.46
  5.2 0.1 reshape.191
  5.3 0.1 select_reduce_fusion.1
  5.5 0.1 concatenate.7
  5.5 0.6 pad.27.tab
  6.1 0.7 convert_element_type.86
  6.9 1.5 copy.52
  8.4 0.6 pad.28.vec
  9.0 1.1 pad.23.tok
  10.1 0.1 copy.51
  10.3 1.1 pad.24.cot
  11.4 0.1 multiply_sine_fusion.1
  11.5 0.1 select_maximum_fusion
  11.6 0.6 pad.26.tmp
  12.2 113.1 %front.1 = (bf16[4,208,768]{2,1,0:T(8,128)(2,1)}, bf16[16,208,768]{2,1,0:T(8,128)(2,1)}, bf16[16,208,768]{2,1,0:T(8,128)(2,1)}, bf16[4,208,768]{2,1,0:T(8,128)(2...) custom-call(bf16[4,208,768]{2,1,0:T(8,128)(2,1)} %pad.23.tok, ...), custom_call_target="tpu_custom_call" | custom-call | flops 8323596288 | bytes 41943040 | tf_op jit(solution)/shard_map/front/pallas_call | solution.py:589
  125.3 42.8 %mid.1 = (bf16[4,208,768]{2,1,0:T(8,128)(2,1)}, f32[4,208,768]{2,1,0:T(8,128)}, bf16[4,208,768]{2,1,0:T(8,128)(2,1)}, bf16[3072,768]{1,0:T(8,128)(2,1)}, bf16[76...) custom-call(bf16[4,208,768]{2,1,0:T(8,128)(2,1)} %get-tuple-element.57.o_in, ...), custom_call_target="tpu_custom_call" | custom-call | flops 26499612672 | bytes 41943040 | tf_op jit(solution)/shard_map/mid/pallas_call | solution.py:751
  168.1 105.7 %back.1 = (bf16[4,208,768]{2,1,0:T(8,128)(2,1)}, bf16[4,208,768]{2,1,0:T(8,128)(2,1)}, bf16[16,208,768]{2,1,0:T(8,128)(2,1)}, bf16[4,4,48,2304]{3,2,1,0:T(8,128)...) custom-call(s32[8,128]{1,0:T(8,128)} %get-tuple-element.53.tab_ref, ...), custom_call_target="tpu_custom_call" | custom-call | flops 31897681920 | bytes 62914560 | tf_op jit(solution)/shard_map/back/pallas_call | solution.py:1161
  273.9 52.6 %tail.1 = (f32[4,196,768]{2,1,0:T(8,128)}, bf16[4,208,768]{2,1,0:T(8,128)(2,1)}, f32[8,768]{1,0:T(8,128)}, bf16[192,2304]{1,0:T(8,128)(2,1)}, bf16[768,768]{1,0:...) custom-call(bf16[4,4,48,2304]{3,2,1,0:T(8,128)(2,1)} %get-tuple-element.73.gq, ...), custom_call_target="tpu_custom_call" | custom-call | flops 12947816448 | bytes 62914560 | tf_op jit(solution)/shard_map/tail/pallas_call | solution.py:1313
  326.5 4.4 %collective-permute-start = (bf16[4,208,768]{2,1,0:T(8,128)(2,1)}, bf16[4,208,768]{2,1,0:T(8,128)(2,1)}, u32[]{:S(2)}, u32[]{:S(2)}) collective-permute-start(bf16[4,208,768]{2,1,0:T(8,128)(2,1)} %get-tuple-element.83), channel_id=1, source_target_pairs={{2,5},{3,4},{4,3},{5,2},{10,13},{11,12},{12,11},{13,10},{18,21},{1... | collective-permute-start | bytes 3833864 | tf_op jit(solution)/shard_map/ppermute | solution.py:1381
  331.0 0.1 slice.12
  331.1 1.5 copy.47
  332.6 0.6 reshape.198
  333.2 3.3 multiply_subtract_fusion.3
  336.5 0.0 copy-start.2
  336.5 0.0 copy-start.3
  336.5 5.1 %multiply_subtract_fusion.2 = (f32[192,2304]{1,0:T(8,128)}, f32[192,2304]{1,0:T(8,128)}, f32[192,2304]{1,0:T(8,128)}) fusion(f32[192,2304]{1,0:T(8,128)S(1)} %copy-done.7, bf16[192,2304]{1,0:T(8,128)(2,1)} %get-tuple-element.84, f32[192,2304]{1,0:T(8,128)S(1)} %copy-done.8, f32[192,2304]{1,0:T(8,128)} %param.31), kind=kLoop, calls=%fused_computation.15 | loop fusion | flops 7077888 | bytes 11501568 | tf_op jit(solution)/shard_map/sub | solution.py:135
  341.7 0.8 copy-done.12
  342.5 0.0 copy-start.4
  342.5 0.0 copy-start.6
  342.5 4.4 %multiply_subtract_fusion = (f32[768,768]{1,0:T(8,128)}, f32[768,768]{1,0:T(8,128)}, f32[768,768]{1,0:T(8,128)}) fusion(f32[768,768]{1,0:T(8,128)S(1)} %copy-done.1, bf16[768,768]{1,0:T(8,128)(2,1)S(1)} %copy-done.12, f32[768,768]{1,0:T(8,128)S(1)} %copy-done.2, f32[768,768]{1,0:T(8,128)S(1)} %copy-done.3), kind=kLoop, calls=%fused_computation.10 | loop fusion | flops 9437184 | bytes 15335424 | tf_op jit(solution)/shard_map/sub | solution.py:135
  346.9 0.6 multiply_subtract_fusion.4
  347.5 0.6 copy-done.6
  348.2 0.3 copy-done.11
  348.5 4.2 %multiply_subtract_fusion.1 = (f32[192,3072]{1,0:T(8,128)}, f32[192,3072]{1,0:T(8,128)}, f32[192,3072]{1,0:T(8,128)}) fusion(f32[192,3072]{1,0:T(8,128)S(1)} %copy-done.4, bf16[192,3072]{1,0:T(8,128)(2,1)S(1)} %copy-done.11, f32[192,3072]{1,0:T(8,128)S(1)} %copy-done.5, f32[192,3072]{1,0:T(8,128)S(1)} %copy-done.6), kind=kLoop, calls=%fused_computation.11 | loop fusion | flops 9437184 | bytes 15335424 | tf_op jit(solution)/shard_map/sub | solution.py:135
  352.6 7.3 %collective-permute-done = bf16[4,208,768]{2,1,0:T(8,128)(2,1)} collective-permute-done((bf16[4,208,768]{2,1,0:T(8,128)(2,1)}, bf16[4,208,768]{2,1,0:T(8,128)(2,1)}, u32[]{:S(2)}, u32[]{:S(2)}) %collective-permute-start) | collective-permute-done | bytes 1277984 | tf_op jit(solution)/shard_map/ppermute | solution.py:1381
  359.9 1.5 select_bitcast_fusion
  361.4 2.4 copy.48
  (42 shorter events, 0.1 us)
Async XLA Ops:
  6.9 3.3 copy-start.9
  10.1 1.3 copy-start.18
  10.1 1.3 copy-start.19
  273.9 57.1 %copy-start.10 = (bf16[4,208,768]{2,1,0:T(8,128)(2,1)S(1)}, bf16[4,208,768]{2,1,0:T(8,128)(2,1)}, u32[]{:S(2)}) copy-start(bf16[4,208,768]{2,1,0:T(8,128)(2,1)} %get-tuple-element.72) | copy-start | bytes 3833860
  326.5 33.4 %collective-permute-start = (bf16[4,208,768]{2,1,0:T(8,128)(2,1)}, bf16[4,208,768]{2,1,0:T(8,128)(2,1)}, u32[]{:S(2)}, u32[]{:S(2)}) collective-permute-start(bf16[4,208,768]{2,1,0:T(8,128)(2,1)} %get-tuple-element.83), channel_id=1, source_target_pairs={{2,5},{3,4},{4,3},{5,2},{10,13},{11,12},{12,11},{13,10},{18,21},{1... | collective-permute-start | bytes 3833864 | tf_op jit(solution)/shard_map/ppermute | solution.py:1381
  331.0 1.6 copy-start.17
  332.6 3.9 %copy-start.7 = (f32[192,2304]{1,0:T(8,128)S(1)}, f32[192,2304]{1,0:T(8,128)}, u32[]{:S(2)}) copy-start(f32[192,2304]{1,0:T(8,128)} %wq.1) | copy-start | bytes 5308420
  332.6 3.9 %copy-start.8 = (f32[192,2304]{1,0:T(8,128)S(1)}, f32[192,2304]{1,0:T(8,128)}, u32[]{:S(2)}) copy-start(f32[192,2304]{1,0:T(8,128)} %param.32) | copy-start | bytes 5308420
  336.5 5.2 %copy-start.1 = (f32[768,768]{1,0:T(8,128)S(1)}, f32[768,768]{1,0:T(8,128)}, u32[]{:S(2)}) copy-start(f32[768,768]{1,0:T(8,128)} %wd.1) | copy-start | bytes 7077892
  336.5 5.2 %copy-start.2 = (f32[768,768]{1,0:T(8,128)S(1)}, f32[768,768]{1,0:T(8,128)}, u32[]{:S(2)}) copy-start(f32[768,768]{1,0:T(8,128)} %param.41) | copy-start | bytes 7077892
  336.5 5.2 %copy-start.3 = (f32[768,768]{1,0:T(8,128)S(1)}, f32[768,768]{1,0:T(8,128)}, u32[]{:S(2)}) copy-start(f32[768,768]{1,0:T(8,128)} %param.40) | copy-start | bytes 7077892
  336.5 5.9 %copy-start.12 = (bf16[768,768]{1,0:T(8,128)(2,1)S(1)}, bf16[768,768]{1,0:T(8,128)(2,1)}, u32[]{:S(2)}) copy-start(bf16[768,768]{1,0:T(8,128)(2,1)} %get-tuple-element.87) | copy-start | bytes 3538948
  342.5 4.4 %copy-start.13 = (f32[2304]{0:T(1024)S(1)}, f32[2304]{0:T(1024)}, u32[]{:S(2)}) copy-start(f32[2304]{0:T(1024)} %param.42) | copy-start | bytes 27652
  342.5 4.4 %copy-start.14 = (f32[2304]{0:T(1024)S(1)}, f32[2304]{0:T(1024)}, u32[]{:S(2)}) copy-start(f32[2304]{0:T(1024)} %reshape.198) | copy-start | bytes 27652
  342.5 4.4 %copy-start.15 = (f32[2304]{0:T(1024)S(1)}, f32[2304]{0:T(1024)}, u32[]{:S(2)}) copy-start(f32[2304]{0:T(1024)} %param.44) | copy-start | bytes 27652
  342.5 4.4 %copy-start.16 = (f32[2304]{0:T(1024)S(1)}, f32[2304]{0:T(1024)}, u32[]{:S(2)}) copy-start(f32[2304]{0:T(1024)} %param.43) | copy-start | bytes 27652
  342.5 5.1 %copy-start.4 = (f32[192,3072]{1,0:T(8,128)S(1)}, f32[192,3072]{1,0:T(8,128)}, u32[]{:S(2)}) copy-start(f32[192,3072]{1,0:T(8,128)} %wu.1) | copy-start | bytes 7077892
  342.5 5.1 %copy-start.5 = (f32[192,3072]{1,0:T(8,128)S(1)}, f32[192,3072]{1,0:T(8,128)}, u32[]{:S(2)}) copy-start(f32[192,3072]{1,0:T(8,128)} %param.38) | copy-start | bytes 7077892
  342.5 5.7 %copy-start.6 = (f32[192,3072]{1,0:T(8,128)S(1)}, f32[192,3072]{1,0:T(8,128)}, u32[]{:S(2)}) copy-start(f32[192,3072]{1,0:T(8,128)} %param.37) | copy-start | bytes 7077892
  342.5 5.9 %copy-start.11 = (bf16[192,3072]{1,0:T(8,128)(2,1)S(1)}, bf16[192,3072]{1,0:T(8,128)(2,1)}, u32[]{:S(2)}) copy-start(bf16[192,3072]{1,0:T(8,128)(2,1)} %get-tuple-element.86) | copy-start | bytes 3538948
  348.5 11.4 %copy-start = (f32[4,196,768]{2,1,0:T(8,128)S(1)}, f32[4,196,768]{2,1,0:T(8,128)}, u32[]{:S(2)}) copy-start(f32[4,196,768]{2,1,0:T(8,128)} %get-tuple-element.82) | copy-start | bytes 7225348

commit v7 on v6

--- a/solution.py
+++ b/solution.py
@@ -867,6 +867,9 @@
 
     def begin(self, w):
         self.half_load(w).start()
+        self.send_halves(w)
+
+    def send_halves(self, w):
         for copy in self.copies(w, 0):
             copy.start()
 
@@ -993,7 +996,7 @@
         copy.start()
     ready()
     for w in range(3):
-        net.begin(w)
+        net.send_halves(w)
     y_stay = pltpu.make_async_copy(y_in, y_out, y_send.at[0])
 
     def y_copy(j):
@@ -1010,6 +1013,8 @@
 
     for n in range(6):
         loads[n].wait()
+    for w in range(3):
+        net.half_load(w).start()
     for copy in loads[6:]:
         copy.start()
     lane = lax.broadcasted_iota(jnp.int32, (SP, 128), 1)

time: 371 us -> 371 us (level)
  no operation moved by 1% of the time
where the time goes in v7:
time: 371 us; the launch traced here: 364 us
  Pallas kernels  314 us (85%)
  other arithmetic  24.4 us (7%)
  local copies, waits for them, and re-layouts  12.5 us (3%)
  waiting for transfers between devices  7.26 us (2%)
  starting transfers between devices  4.41 us (1%)
    pallas_call x1, Pallas kernels, front(): pl.pallas_call(front_kernel, out_shape=(S(rows, bf), S(every, bf), S(ever...  113 us
    pallas_call x1, Pallas kernels, back(): pl.pallas_call(functools.partial(back_kernel, n_items), out_shape=(S(rows...  106 us
    pallas_call x1, Pallas kernels, tail(): pl.pallas_call(functools.partial(tail_kernel, n_items), out_shape=(S((4,...  52.6 us
    pallas_call x1, Pallas kernels, mid(): pl.pallas_call(mid_kernel, out_shape=(S(rows, bf), S(rows, f32), S(rows,...  42.8 us
    sub x5, other arithmetic, adamw(): weight - step_rate * (first_hat / (jnp.sqrt(second_hat) + 1e-08) + decay...  17.6 us
  transfers between devices with their start and end apart: 1, of which 1 were waited for; matrix products, arithmetic and copies ran while one was open for 5% of the time, Pallas kernels for 0%

profile of v7, /device:TPU:13, one launch (start us, length us, event | category | flops | bytes accessed | tf_op | source)
XLA Modules:
  0.0 363.9 jit_solution(17976813347214331213)
XLA Ops:
  0.7 0.8 reduce-window.4
  1.5 0.7 fusion.13
  2.2 0.7 convert_reduce_fusion
  2.9 0.7 compare_reduce_fusion
  3.6 0.1 dynamic_slice.3
  3.7 0.7 fusion.12
  4.4 0.2 convert_reduce_fusion.1
  4.6 0.1 fusion.11
  4.6 0.1 reshape.199
  4.7 0.2 reduce_window_sum.18
  4.9 0.2 select_reduce_fusion
  5.1 0.1 copy.46
  5.2 0.1 reshape.191
  5.3 0.1 select_reduce_fusion.1
  5.5 0.1 concatenate.7
  5.5 0.6 pad.27.tab
  6.1 0.7 convert_element_type.86
  6.9 1.5 copy.52
  8.4 0.6 pad.28.vec
  9.0 1.1 pad.23.tok
  10.1 0.1 copy.51
  10.3 1.1 pad.24.cot
  11.4 0.1 multiply_sine_fusion.1
  11.5 0.1 select_maximum_fusion
  11.6 0.6 pad.26.tmp
  12.2 113.1 %front.1 = (bf16[4,208,768]{2,1,0:T(8,128)(2,1)}, bf16[16,208,768]{2,1,0:T(8,128)(2,1)}, bf16[16,208,768]{2,1,0:T(8,128)(2,1)}, bf16[4,208,768]{2,1,0:T(8,128)(2...) custom-call(bf16[4,208,768]{2,1,0:T(8,128)(2,1)} %pad.23.tok, ...), custom_call_target="tpu_custom_call" | custom-call | flops 8323596288 | bytes 41943040 | tf_op jit(solution)/shard_map/front/pallas_call | solution.py:589
  125.3 42.8 %mid.1 = (bf16[4,208,768]{2,1,0:T(8,128)(2,1)}, f32[4,208,768]{2,1,0:T(8,128)}, bf16[4,208,768]{2,1,0:T(8,128)(2,1)}, bf16[3072,768]{1,0:T(8,128)(2,1)}, bf16[76...) custom-call(bf16[4,208,768]{2,1,0:T(8,128)(2,1)} %get-tuple-element.57.o_in, ...), custom_call_target="tpu_custom_call" | custom-call | flops 26499612672 | bytes 41943040 | tf_op jit(solution)/shard_map/mid/pallas_call | solution.py:751
  168.1 105.7 %back.1 = (bf16[4,208,768]{2,1,0:T(8,128)(2,1)}, bf16[4,208,768]{2,1,0:T(8,128)(2,1)}, bf16[16,208,768]{2,1,0:T(8,128)(2,1)}, bf16[4,4,48,2304]{3,2,1,0:T(8,128)...) custom-call(s32[8,128]{1,0:T(8,128)} %get-tuple-element.53.tab_ref, ...), custom_call_target="tpu_custom_call" | custom-call | flops 31897681920 | bytes 62914560 | tf_op jit(solution)/shard_map/back/pallas_call | solution.py:1166
  273.9 52.6 %tail.1 = (f32[4,196,768]{2,1,0:T(8,128)}, bf16[4,208,768]{2,1,0:T(8,128)(2,1)}, f32[8,768]{1,0:T(8,128)}, bf16[192,2304]{1,0:T(8,128)(2,1)}, bf16[768,768]{1,0:...) custom-call(bf16[4,4,48,2304]{3,2,1,0:T(8,128)(2,1)} %get-tuple-element.73.gq, ...), custom_call_target="tpu_custom_call" | custom-call | flops 12947816448 | bytes 62914560 | tf_op jit(solution)/shard_map/tail/pallas_call | solution.py:1318
  326.5 4.4 %collective-permute-start = (bf16[4,208,768]{2,1,0:T(8,128)(2,1)}, bf16[4,208,768]{2,1,0:T(8,128)(2,1)}, u32[]{:S(2)}, u32[]{:S(2)}) collective-permute-start(bf16[4,208,768]{2,1,0:T(8,128)(2,1)} %get-tuple-element.83), channel_id=1, source_target_pairs={{2,5},{3,4},{4,3},{5,2},{10,13},{11,12},{12,11},{13,10},{18,21},{1... | collective-permute-start | bytes 3833864 | tf_op jit(solution)/shard_map/ppermute | solution.py:1386
  331.0 0.1 slice.12
  331.1 1.5 copy.47
  332.6 0.6 reshape.198
  333.2 3.3 multiply_subtract_fusion.3
  336.5 0.0 copy-start.2
  336.5 0.0 copy-start.3
  336.5 5.1 %multiply_subtract_fusion.2 = (f32[192,2304]{1,0:T(8,128)}, f32[192,2304]{1,0:T(8,128)}, f32[192,2304]{1,0:T(8,128)}) fusion(f32[192,2304]{1,0:T(8,128)S(1)} %copy-done.7, bf16[192,2304]{1,0:T(8,128)(2,1)} %get-tuple-element.84, f32[192,2304]{1,0:T(8,128)S(1)} %copy-done.8, f32[192,2304]{1,0:T(8,128)} %param.31), kind=kLoop, calls=%fused_computation.15 | loop fusion | flops 7077888 | bytes 11501568 | tf_op jit(solution)/shard_map/sub | solution.py:135
  341.7 0.8 copy-done.12
  342.5 0.0 copy-start.5
  342.5 0.0 copy-start.6
  342.5 4.4 %multiply_subtract_fusion = (f32[768,768]{1,0:T(8,128)}, f32[768,768]{1,0:T(8,128)}, f32[768,768]{1,0:T(8,128)}) fusion(f32[768,768]{1,0:T(8,128)S(1)} %copy-done.1, bf16[768,768]{1,0:T(8,128)(2,1)S(1)} %copy-done.12, f32[768,768]{1,0:T(8,128)S(1)} %copy-done.2, f32[768,768]{1,0:T(8,128)S(1)} %copy-done.3), kind=kLoop, calls=%fused_computation.10 | loop fusion | flops 9437184 | bytes 15335424 | tf_op jit(solution)/shard_map/sub | solution.py:135
  346.9 0.6 multiply_subtract_fusion.4
  347.5 0.6 copy-done.6
  348.2 0.3 copy-done.11
  348.4 4.2 %multiply_subtract_fusion.1 = (f32[192,3072]{1,0:T(8,128)}, f32[192,3072]{1,0:T(8,128)}, f32[192,3072]{1,0:T(8,128)}) fusion(f32[192,3072]{1,0:T(8,128)S(1)} %copy-done.4, bf16[192,3072]{1,0:T(8,128)(2,1)S(1)} %copy-done.11, f32[192,3072]{1,0:T(8,128)S(1)} %copy-done.5, f32[192,3072]{1,0:T(8,128)S(1)} %copy-done.6), kind=kLoop, calls=%fused_computation.11 | loop fusion | flops 9437184 | bytes 15335424 | tf_op jit(solution)/shard_map/sub | solution.py:135
  352.6 7.3 %collective-permute-done = bf16[4,208,768]{2,1,0:T(8,128)(2,1)} collective-permute-done((bf16[4,208,768]{2,1,0:T(8,128)(2,1)}, bf16[4,208,768]{2,1,0:T(8,128)(2,1)}, u32[]{:S(2)}, u32[]{:S(2)}) %collective-permute-start) | collective-permute-done | bytes 1277984 | tf_op jit(solution)/shard_map/ppermute | solution.py:1386
  359.9 1.5 select_bitcast_fusion
  361.4 2.4 copy.48
  (42 shorter events, 0.1 us)
Async XLA Ops:
  6.9 3.3 copy-start.9
  10.1 1.3 copy-start.18
  10.1 1.3 copy-start.19
  273.9 57.1 %copy-start.10 = (bf16[4,208,768]{2,1,0:T(8,128)(2,1)S(1)}, bf16[4,208,768]{2,1,0:T(8,128)(2,1)}, u32[]{:S(2)}) copy-start(bf16[4,208,768]{2,1,0:T(8,128)(2,1)} %get-tuple-element.72) | copy-start | bytes 3833860
  326.5 33.4 %collective-permute-start = (bf16[4,208,768]{2,1,0:T(8,128)(2,1)}, bf16[4,208,768]{2,1,0:T(8,128)(2,1)}, u32[]{:S(2)}, u32[]{:S(2)}) collective-permute-start(bf16[4,208,768]{2,1,0:T(8,128)(2,1)} %get-tuple-element.83), channel_id=1, source_target_pairs={{2,5},{3,4},{4,3},{5,2},{10,13},{11,12},{12,11},{13,10},{18,21},{1... | collective-permute-start | bytes 3833864 | tf_op jit(solution)/shard_map/ppermute | solution.py:1386
  331.0 1.6 copy-start.17
  332.5 3.9 %copy-start.7 = (f32[192,2304]{1,0:T(8,128)S(1)}, f32[192,2304]{1,0:T(8,128)}, u32[]{:S(2)}) copy-start(f32[192,2304]{1,0:T(8,128)} %wq.1) | copy-start | bytes 5308420
  332.5 3.9 %copy-start.8 = (f32[192,2304]{1,0:T(8,128)S(1)}, f32[192,2304]{1,0:T(8,128)}, u32[]{:S(2)}) copy-start(f32[192,2304]{1,0:T(8,128)} %param.32) | copy-start | bytes 5308420
  336.5 5.2 %copy-start.1 = (f32[768,768]{1,0:T(8,128)S(1)}, f32[768,768]{1,0:T(8,128)}, u32[]{:S(2)}) copy-start(f32[768,768]{1,0:T(8,128)} %wd.1) | copy-start | bytes 7077892
  336.5 5.2 %copy-start.2 = (f32[768,768]{1,0:T(8,128)S(1)}, f32[768,768]{1,0:T(8,128)}, u32[]{:S(2)}) copy-start(f32[768,768]{1,0:T(8,128)} %param.41) | copy-start | bytes 7077892
  336.5 5.2 %copy-start.3 = (f32[768,768]{1,0:T(8,128)S(1)}, f32[768,768]{1,0:T(8,128)}, u32[]{:S(2)}) copy-start(f32[768,768]{1,0:T(8,128)} %param.40) | copy-start | bytes 7077892
  336.5 5.9 %copy-start.12 = (bf16[768,768]{1,0:T(8,128)(2,1)S(1)}, bf16[768,768]{1,0:T(8,128)(2,1)}, u32[]{:S(2)}) copy-start(bf16[768,768]{1,0:T(8,128)(2,1)} %get-tuple-element.87) | copy-start | bytes 3538948
  342.4 4.4 %copy-start.13 = (f32[2304]{0:T(1024)S(1)}, f32[2304]{0:T(1024)}, u32[]{:S(2)}) copy-start(f32[2304]{0:T(1024)} %param.42) | copy-start | bytes 27652
  342.4 4.4 %copy-start.14 = (f32[2304]{0:T(1024)S(1)}, f32[2304]{0:T(1024)}, u32[]{:S(2)}) copy-start(f32[2304]{0:T(1024)} %reshape.198) | copy-start | bytes 27652
  342.4 4.4 %copy-start.15 = (f32[2304]{0:T(1024)S(1)}, f32[2304]{0:T(1024)}, u32[]{:S(2)}) copy-start(f32[2304]{0:T(1024)} %param.44) | copy-start | bytes 27652
  342.4 4.4 %copy-start.16 = (f32[2304]{0:T(1024)S(1)}, f32[2304]{0:T(1024)}, u32[]{:S(2)}) copy-start(f32[2304]{0:T(1024)} %param.43) | copy-start | bytes 27652
  342.5 5.1 %copy-start.4 = (f32[192,3072]{1,0:T(8,128)S(1)}, f32[192,3072]{1,0:T(8,128)}, u32[]{:S(2)}) copy-start(f32[192,3072]{1,0:T(8,128)} %wu.1) | copy-start | bytes 7077892
  342.5 5.1 %copy-start.5 = (f32[192,3072]{1,0:T(8,128)S(1)}, f32[192,3072]{1,0:T(8,128)}, u32[]{:S(2)}) copy-start(f32[192,3072]{1,0:T(8,128)} %param.38) | copy-start | bytes 7077892
  342.5 5.7 %copy-start.6 = (f32[192,3072]{1,0:T(8,128)S(1)}, f32[192,3072]{1,0:T(8,128)}, u32[]{:S(2)}) copy-start(f32[192,3072]{1,0:T(8,128)} %param.37) | copy-start | bytes 7077892
  342.5 5.9 %copy-start.11 = (bf16[192,3072]{1,0:T(8,128)(2,1)S(1)}, bf16[192,3072]{1,0:T(8,128)(2,1)}, u32[]{:S(2)}) copy-start(bf16[192,3072]{1,0:T(8,128)(2,1)} %get-tuple-element.86) | copy-start | bytes 3538948
  348.4 11.4 %copy-start = (f32[4,196,768]{2,1,0:T(8,128)S(1)}, f32[4,196,768]{2,1,0:T(8,128)}, u32[]{:S(2)}) copy-start(f32[4,196,768]{2,1,0:T(8,128)} %get-tuple-element.82) | copy-start | bytes 7225348
